TPU v7x, 32 devices: a whole 2x2x4 slice. The times are simulated.
32 devices in a mesh: section: 4 (over y, core), dp: 8 (over z, x).
Axes of the slice: x: 2, y: 2, z: 4, core: 2. Of those that a mesh axis runs over, the one named last changes fastest.
Arguments:
- tokens_in: bfloat16 [16, 1024, 768], P('dp', 'section'), may hold values from -6 to 6
- seg_starts: int32 [16, 6], P('dp'), may hold values from 0 to 1023, as said below
- pad_mask: int32 [16, 1024], P('dp'), may hold values from 0 to 1, as said below
- w_qkv: bfloat16 [4, 768, 2304], P('section'), may hold values from -0.21875 to 0.21875
- b_qv: float32 [4, 1536], P('section'), may hold values from -3 to 3
- w_attn_out: bfloat16 [4, 768, 768], P('section'), may hold values from -0.875 to 0.875
- b_attn_out: float32 [4, 768], P('section'), may hold values from -3 to 3
- ln_gain: float32 [4, 2, 768], P('section'), may hold values from 0.5 to 1.5
- ln_bias: float32 [4, 2, 768], P('section'), may hold values from -2 to 2
- w_up: bfloat16 [4, 768, 3072], P('section'), may hold values from -0.21875 to 0.21875
- b_up: float32 [4, 3072], P('section'), may hold values from -3 to 3
- w_down: bfloat16 [4, 3072, 768], P('section'), may hold values from -0.109375 to 0.109375
- b_down: float32 [4, 768], P('section'), may hold values from -3 to 3
- w_proj: bfloat16 [768, 128], P(None, 'section'), may hold values from -0.21875 to 0.21875
- cotangent: bfloat16 [16, 1024, 128], P('dp', None, 'section'), may hold values from -6 to 6
Outputs:
- embedded: bfloat16 [16, 1024, 128], P('dp', None, 'section')
- grad_in: float32 [16, 1024, 768], P('dp', 'section')
- grad_w_qkv: float32 [4, 768, 2304], P('section', 'dp')
- grad_b_qv: float32 [4, 1536], P('section', 'dp')
- grad_w_attn_out: float32 [4, 768, 768], P('section', 'dp')
- grad_b_attn_out: float32 [4, 768], P('section', 'dp')
- grad_ln_gain: float32 [4, 2, 768], P('section', None, 'dp')
- grad_ln_bias: float32 [4, 2, 768], P('section', None, 'dp')
- grad_w_up: float32 [4, 768, 3072], P('section', 'dp')
- grad_b_up: float32 [4, 3072], P('section', 'dp')
- grad_w_down: float32 [4, 3072, 768], P('section', 'dp')
- grad_b_down: float32 [4, 768], P('section', 'dp')
- grad_w_proj: float32 [768, 128], P('dp', 'section')
Inputs may be any that keep to these rules, and one draw needn't show every extreme that they name: `seg_starts`: in each row the 6 starts rise strictly and the first is 0. `pad_mask`: in each row the zeros form a tail of at most 256 positions.
All inputs are finite; a program needn't handle non-finite values.
Results may differ from a plain program's by a relative error of at most 0.025.
Values may be sent and summed in bfloat16 or wider, within the bound.
No kernel may reach another device: no remote copies, remote signals or barrier semaphores. Data moves between devices by JAX's collectives and lax.ppermute only.
A program may use at most 512 MiB of HBM per device.

v0:
```python
from functools import partial
import math

import jax
import jax.numpy as jnp
from jax import lax
from jax.experimental import pallas as pl
from jax.experimental.pallas import tpu as pltpu
from jax.sharding import PartitionSpec as P

HEAD = 64
PAIR = 2 * HEAD
QB = 128
KB = 512
KEYS = 256
EPS_NORM = 1e-05
EPS_PROJ = 1e-06
NEG_FILL = -1e30
PARAMS = pltpu.CompilerParams(vmem_limit_bytes=60 * 1024 * 1024)


def cost(micros):
    return pl.CostEstimate(flops=int(micros * 1e9), bytes_accessed=1024, transcendentals=0)


BF = jnp.bfloat16
F32 = jnp.float32

NT = (((1,), (1,)), ((), ()))
TN = (((0,), (0,)), ((), ()))


def dot(a, b):
    return jnp.dot(a, b, preferred_element_type=F32)


def dot_nt(a, b):
    return lax.dot_general(a, b, NT, preferred_element_type=F32)


def dot_tn(a, b):
    return lax.dot_general(a, b, TN, preferred_element_type=F32)


def pack_small(b_qv, b_out, gains, shifts, b_up, b_down):
    return jnp.concatenate(
        [b_up, b_qv, b_out, gains[0], gains[1], shifts[0], shifts[1], b_down]
    )


def small_spec(layer, width):
    return pl.BlockSpec((1, 1, width), lambda *_: (layer, 0, 0))


def attention_plan(starts, real_flags):
    length = real_flags.shape[0]
    places = jnp.arange(length, dtype=jnp.int32)
    segment = jnp.sum((starts[None, :] <= places[:, None]).astype(jnp.int32), axis=1)
    key_code = jnp.where(real_flags == 1, segment, -1).astype(F32)
    key_code = jnp.broadcast_to(key_code[:, None], (length, PAIR))
    query_code = segment.astype(F32).reshape(length // QB, QB)
    first = jnp.arange(length // QB, dtype=jnp.int32) * QB
    low = jnp.max(jnp.where(starts[None, :] <= first[:, None], starts[None, :], 0), axis=1)
    high = jnp.min(
        jnp.where(starts[None, :] > first[:, None] + (QB - 1), starts[None, :], length), axis=1
    )
    begin = (low // QB) * QB
    count = (high - begin + KEYS - 1) // KEYS
    begin = jnp.minimum(begin, length - KEYS * count)
    return (begin, count, key_code, query_code)


def pair_mask(rows):
    return lax.broadcasted_iota(jnp.int32, (rows, PAIR), 1) < HEAD


def stacked_heads(block):
    first = pair_mask(block.shape[0])
    zero = jnp.zeros_like(block)
    return jnp.concatenate([jnp.where(first, block, zero), jnp.where(first, zero, block)], axis=0)


def block_bias(key_code, query_code, key_at, query_at):
    shape = key_code.shape
    keys = lax.broadcasted_iota(jnp.int32, shape, 0) + (key_at - query_at)
    same = keys == lax.broadcasted_iota(jnp.int32, shape, 1)
    bias = jnp.where((key_code == query_code) | same, 0.0, NEG_FILL)
    return jnp.concatenate([bias, bias], axis=1)


def over_keys(begin, count, step, state):
    state = lax.fori_loop(
        0,
        lax.shift_right_logical(count, 1),
        lambda j, now: step(pl.multiple_of(begin + j * KB, QB), KB, now),
        state,
    )
    last = pl.multiple_of(begin + (count - 1) * KEYS, QB)
    return lax.fori_loop(
        0, jnp.bitwise_and(count, 1), lambda _, now: step(last, KEYS, now), state
    )


def unstack_heads(flat):
    rows = lax.broadcasted_iota(jnp.int32, (PAIR, QB), 0)
    return jnp.where(rows < HEAD, flat[:PAIR, :QB], flat[:PAIR, QB:]).T


def attend_forward(
    begin_ref, count_ref, qkv_ref, key_code_ref, query_code_ref, out_ref, logsum_ref,
    value_scr, query_scr, total_scr,
):
    length = qkv_ref.shape[1]
    pairs = qkv_ref.shape[2] // PAIR
    every = range(pairs)
    cols = [slice(p * PAIR, (p + 1) * PAIR) for p in every]
    for p in every:
        value_scr[p, :PAIR, :] = qkv_ref[2, :, cols[p]].T
        value_scr[p, PAIR:, :] = jnp.ones((value_scr.shape[1] - PAIR, length), BF)

    def one_query_block(i, _):
        query_at = pl.multiple_of(i * QB, QB)
        begin, count = begin_ref[i], count_ref[i]
        query_code = query_code_ref[pl.ds(i, 1), :]
        for p in every:
            query_scr[p] = stacked_heads(qkv_ref[0, pl.ds(query_at, QB), cols[p]])
        total_scr[...] = jnp.zeros_like(total_scr)

        def one_key_block(key_at, size, tops):
            rows = pl.ds(key_at, size)
            bias = block_bias(key_code_ref[rows, :], query_code, key_at, query_at)
            scores = [dot_nt(qkv_ref[1, rows, cols[p]], query_scr[p]) + bias for p in every]
            fresh = [
                jnp.maximum(tops[p], jnp.max(scores[p], axis=0, keepdims=True)) for p in every
            ]
            probs = [jnp.exp(scores[p] - fresh[p]).astype(BF) for p in every]
            for p in every:
                total_scr[p] = total_scr[p] * jnp.exp(tops[p] - fresh[p]) + dot(
                    value_scr[p, :, rows], probs[p]
                )
            return tuple(fresh)

        tops = tuple(jnp.full((1, 2 * QB), 2 * NEG_FILL, F32) for _ in every)
        tops = over_keys(begin, count, one_key_block, tops)
        for p in every:
            weight = total_scr[p, PAIR : PAIR + 1, :]
            logsum_ref[pl.ds(p * (length // QB) + i, 1), :] = tops[p] + jnp.log(weight)
            out_ref[pl.ds(query_at, QB), cols[p]] = unstack_heads(
                total_scr[p, :PAIR, :] * (1.0 / weight)
            ).astype(BF)
        return 0

    lax.fori_loop(0, length // QB, one_query_block, 0)


def attend_backward(
    begin_ref, count_ref, qkv, key_code_ref, query_code_ref, context, logsum_ref, grad, sums_ref,
    key_scr, query_scr, given_scr, down_scr, grad_key_scr, grad_value_scr,
):
    length = qkv.shape[1]
    pairs = qkv.shape[2] // PAIR
    every = range(pairs)
    blocks = length // QB
    cols = [slice(p * PAIR, (p + 1) * PAIR) for p in every]
    for p in every:
        key_scr[p] = qkv[1, :, cols[p]].T

    def one_query_block(i, _):
        query_at = pl.multiple_of(i * QB, QB)
        queries = pl.ds(query_at, QB)
        begin, count = begin_ref[i], count_ref[i]
        query_code = query_code_ref[pl.ds(i, 1), :]
        inner, logsum = [], []
        for p in every:
            query_scr[p] = stacked_heads(qkv[0, queries, cols[p]])
            given = grad[queries, cols[p]]
            given_scr[p] = stacked_heads(given)
            both = (given.astype(F32) * context[queries, cols[p]].astype(F32)).T
            inner.append(
                jnp.concatenate(
                    [
                        jnp.sum(both[:HEAD], axis=0, keepdims=True),
                        jnp.sum(both[HEAD:], axis=0, keepdims=True),
                    ],
                    axis=1,
                )
            )
            logsum.append(logsum_ref[pl.ds(p * blocks + i, 1), :])
        down_scr[...] = jnp.zeros_like(down_scr)

        def one_key_block(key_at, size, state):
            rows = pl.ds(key_at, size)
            bias = block_bias(key_code_ref[rows, :], query_code, key_at, query_at)
            grads = [
                (dot_nt(qkv[2, rows, cols[p]], given_scr[p]) - inner[p]).astype(BF) for p in every
            ]
            parts = [dot_nt(qkv[1, rows, cols[p]], query_scr[p]) + bias for p in every]
            probs = [jnp.exp(parts[p] - logsum[p]).astype(BF) for p in every]
            scores = [probs[p] * grads[p] for p in every]
            for p in every:
                grad_value_scr[rows, cols[p]] += dot(probs[p], given_scr[p])
            for p in every:
                grad_key_scr[rows, cols[p]] += dot(scores[p], query_scr[p])
            for p in every:
                down_scr[p] += dot(key_scr[p, :, rows], scores[p])
            return state

        over_keys(begin, count, one_key_block, 0)
        for p in every:
            grad_query = (unstack_heads(down_scr[p]) * (HEAD**-0.5)).astype(BF)
            qkv[0, queries, cols[p]] = grad_query
            sums_ref[0:1, cols[p]] += jnp.sum(grad_query.astype(F32), axis=0, keepdims=True)
        return 0

    lax.fori_loop(0, blocks, one_query_block, 0)
    qkv[1] = grad_key_scr[...].astype(BF)
    grad_value = grad_value_scr[...].astype(BF)
    qkv[2] = grad_value
    sums_ref[1:2, :] = jnp.sum(grad_value.astype(F32), axis=0, keepdims=True)


ANY = pl.BlockSpec(memory_space=pl.ANY)
ROWS = 256


class Held:
    def __init__(self, sel_ref, layer, pairs, held, sems, first=None):
        self.own = sel_ref[0] == layer
        self.items = list(zip(pairs, held, range(len(held))))
        self.sems = sems
        self.first = pl.program_id(0) == 0 if first is None else first

    def start(self):
        for pair, held, n in self.items:
            for wanted, source in zip((self.own, jnp.logical_not(self.own)), pair):

                @pl.when(self.first & wanted)
                def _():
                    pltpu.make_async_copy(source, held, self.sems.at[n]).start()

    def wait(self, n):
        pair, held, _ = self.items[n]

        @pl.when(self.first)
        def _():
            pltpu.make_async_copy(pair[0], held, self.sems.at[n]).wait()


def held_shapes(*weights):
    return [pltpu.VMEM(own.shape, own.dtype) for own, _ in weights]


def normalized(values):
    centred = values - jnp.mean(values, axis=-1, keepdims=True)
    inverse = lax.rsqrt(jnp.mean(centred * centred, axis=-1, keepdims=True) + EPS_NORM)
    return (centred * inverse, inverse)


def normalized_pull(grad_hat, hat, inverse):
    return inverse * (
        grad_hat
        - jnp.mean(grad_hat, axis=-1, keepdims=True)
        - hat * jnp.mean(grad_hat * hat, axis=-1, keepdims=True)
    )


ERF = (0.254829592, -0.284496736, 1.421413741, -1.453152027, 1.061405429)
ERF_SLOPE = 0.3275911


def gelu_parts(x):
    t = pl.reciprocal(1.0 + (ERF_SLOPE * math.sqrt(0.5)) * jnp.abs(x), approx=True)
    bell = jnp.exp(-0.5 * (x * x))
    tail = 0.5 * ERF[4]
    for term in ERF[3::-1]:
        tail = tail * t + 0.5 * term
    tail = tail * t * bell
    below = jnp.where(x >= 0, 1.0 - tail, tail)
    return (x * below, below + x * bell * (1.0 / math.sqrt(2.0 * math.pi)))


FB = 1024


def small_slices(width, ff_width):
    names = ("b_q", "b_v", "b_out", "gain1", "gain2", "shift1", "shift2", "b_down")
    at = {"b_up": slice(0, ff_width)}
    for n, name in enumerate(names):
        at[name] = slice(ff_width + n * width, ff_width + (n + 1) * width)
    return at


def refine_back_kernel(
    layer, sel_ref, grad_ref, hidden_ref, out_ref, scale1_ref, scale2_ref, slope_ref,
    out_own_ref, out_other_ref, up_own_ref, up_other_ref, down_own_ref, down_other_ref, small_ref,
    grad_low_ref, grad_raised_ref, grad_attn_ref, grad_context_ref, sums_ref, up_sums_ref,
    w_out, w_up, w_down, sems,
):
    pairs = [(out_own_ref, out_other_ref), (up_own_ref, up_other_ref), (down_own_ref, down_other_ref)]
    weights = Held(sel_ref, layer, pairs, [w_out, w_up, w_down], sems)
    weights.start()
    rows, width = grad_ref.shape
    ff_width = slope_ref.shape[1]
    at = small_slices(width, ff_width)

    @pl.when(pl.program_id(0) == 0)
    def _():
        sums_ref[...] = jnp.zeros_like(sums_ref)
        up_sums_ref[...] = jnp.zeros_like(up_sums_ref)

    def vector(name):
        return small_ref[0, :, at[name]]

    def add(row, values):
        sums_ref[row : row + 1, :] += jnp.sum(values, axis=0, keepdims=True)

    grad = grad_ref[...].astype(F32)
    hat = (out_ref[...].astype(F32) - vector("shift2")) * (1.0 / vector("gain2"))
    joined = normalized_pull(grad * vector("gain2"), hat, scale2_ref[:, :1])
    low = joined.astype(BF)
    grad_low_ref[...] = low
    add(2, grad * hat)
    add(4, grad)
    add(5, low.astype(F32))
    weights.wait(2)
    weights.wait(1)
    total = joined
    parts = [slice(f, f + FB) for f in range(0, ff_width, FB)]
    active = dot_nt(low, w_down[parts[0], :])
    for n, part in enumerate(parts):
        following = dot_nt(low, w_down[parts[n + 1], :]) if n + 1 < len(parts) else None
        raised = active * slope_ref[:, part].astype(F32)
        up_sums_ref[:, part] += jnp.sum(raised, axis=0, keepdims=True)
        raised = raised.astype(BF)
        grad_raised_ref[:, part] = raised
        total += dot_nt(raised, w_up[:, part])
        active = following
    hat = (hidden_ref[...].astype(F32) - vector("shift1")) * (1.0 / vector("gain1"))
    summed = normalized_pull(total * vector("gain1"), hat, scale1_ref[:, :1])
    attn = summed.astype(BF)
    grad_attn_ref[...] = attn
    weights.wait(0)
    grad_context_ref[...] = dot_nt(attn, w_out[...]).astype(BF)
    add(1, total * hat)
    add(3, total)
    add(0, attn.astype(F32))


def refine_back_second_kernel(layer, *refs):
    refine_back_kernel(layer, *refs[:14], *refs[18:])


def refine_back(sel, grad, kept, weights, layer, first=0, begun=()):
    w_out, w_up, w_down, small = weights
    hidden, out, scale1, scale2, slope = kept
    length, width = hidden.shape
    ff_width = w_up[0].shape[1]
    at = first // ROWS
    rows = pl.BlockSpec((ROWS, width), lambda n, _: (n + at, 0))
    lanes = pl.BlockSpec((ROWS, 128), lambda n, _: (n + at, 0))
    part = pl.BlockSpec((ROWS, ff_width), lambda n, _: (n + at, 0))
    row_shape = jax.ShapeDtypeStruct((length, width), BF)
    return pl.pallas_call(
        partial(refine_back_second_kernel if begun else refine_back_kernel, layer),
        name="refine_back",
        grid_spec=pltpu.PrefetchScalarGridSpec(
            num_scalar_prefetch=1,
            grid=(grad.shape[0] // ROWS,),
            in_specs=[
                pl.BlockSpec((ROWS, width), lambda n, _: (n, 0)),
                rows, rows, lanes, lanes, part,
            ]
            + [ANY] * 6
            + [small_spec(layer, small.shape[2])]
            + [ANY] * len(begun),
            out_specs=[
                rows, part, rows, rows,
                pl.BlockSpec((6, width), lambda n, _: (0, 0)),
                pl.BlockSpec((1, ff_width), lambda n, _: (0, 0)),
            ],
            scratch_shapes=[
                *held_shapes(w_out, w_up, w_down),
                pltpu.SemaphoreType.DMA((3,)),
            ],
        ),
        out_shape=[
            row_shape,
            jax.ShapeDtypeStruct((length, ff_width), BF),
            row_shape,
            row_shape,
            jax.ShapeDtypeStruct((6, width), F32),
            jax.ShapeDtypeStruct((1, ff_width), F32),
        ],
        input_output_aliases={14 + n: n for n in range(len(begun))},
        compiler_params=PARAMS,
        cost_estimate=cost(24),
    )(sel, grad, hidden, out, scale1, scale2, slope, *w_out, *w_up, *w_down, small, *begun)


def head_kernel(rows_ref, proj_ref, given_ref, embedded_ref, grad_proj_ref, grad_rows_ref):
    factor = math.sqrt(proj_ref.shape[0])
    columns = dot_nt(proj_ref[...], rows_ref[...])
    given = given_ref[...].astype(F32)
    inverse = lax.rsqrt(jnp.sum(columns * columns, axis=0, keepdims=True) + EPS_PROJ)
    cross = jnp.sum(columns * given, axis=0, keepdims=True)
    embedded_ref[...] = (factor * columns * inverse).astype(BF)
    grad = (factor * (given * inverse - columns * (cross * inverse * inverse * inverse))).astype(BF)
    grad_proj_ref[...] = dot(grad, rows_ref[...]).T.astype(BF)
    grad_rows_ref[...] = dot_tn(grad, proj_ref[...]).astype(BF)


def head(rows, proj, given):
    length, width = rows.shape
    cols = proj.shape[0]
    return pl.pallas_call(
        head_kernel,
        name="head",
        out_shape=[
            jax.ShapeDtypeStruct((cols, length), BF),
            jax.ShapeDtypeStruct((width, cols), BF),
            jax.ShapeDtypeStruct((length, width), BF),
        ],
        compiler_params=PARAMS,
        cost_estimate=cost(6),
    )(rows, proj, given)


HALF = 384
SHARDS = 8


def feed_grads_kernel(
    sel_ref, hidden_ref, raised_late_ref, raised_ref, active_ref, low_late_ref, low_ref, out_ref
):
    step = pl.program_id(0)
    shards, rows, _ = out_ref.shape
    blocks = raised_ref.shape[1] // HALF
    share = rows // blocks
    late = sel_ref[1] == 1

    def up(raised):
        part = dot_tn(hidden_ref[...], raised).astype(BF)
        for m in range(shards):
            for n in range(blocks):
                out_ref[m, n * share : (n + 1) * share, :] = part[
                    m * share : (m + 1) * share, n * HALF : (n + 1) * HALF
                ]

    def down(low):
        for m in range(shards):
            out_ref[m] = dot_tn(active_ref[:, m * rows : (m + 1) * rows], low).astype(BF)

    for wanted, raised_now, low_now in (
        (late, raised_late_ref, low_late_ref),
        (jnp.logical_not(late), raised_ref, low_ref),
    ):

        @pl.when(wanted & (step < 2))
        def _():
            up(raised_now[...])

        @pl.when(wanted & (step >= 2))
        def _():
            down(low_now[...])


def feed_grads(sel, hidden, raised_late, raised, active, low_late, low):
    length, width = hidden.shape
    ff_width = active.shape[1]
    half_ff = ff_width // 2

    def late_spec(shape, wanted):
        return pl.BlockSpec(shape, lambda n, sel: (0, jnp.where(sel[1] == wanted, sel[2], 0)))

    return pl.pallas_call(
        feed_grads_kernel,
        name="feed_grads",
        grid_spec=pltpu.PrefetchScalarGridSpec(
            num_scalar_prefetch=1,
            grid=(4,),
            in_specs=[
                pl.BlockSpec((length, width // 2), lambda n, _: (0, jnp.minimum(n, 1))),
                late_spec((length, half_ff), 1),
                late_spec((length, half_ff), 0),
                pl.BlockSpec((length, ff_width // 2), lambda n, _: (0, jnp.maximum(n - 2, 0))),
                late_spec((length, width // 2), 1),
                late_spec((length, width // 2), 0),
            ],
            out_specs=pl.BlockSpec(
                (SHARDS // 2, ff_width // SHARDS, HALF), lambda n, _: (lax.rem(n, 2), n // 2, 0)
            ),
        ),
        out_shape=jax.ShapeDtypeStruct((SHARDS, 2 * (ff_width // SHARDS), HALF), BF),
        compiler_params=PARAMS,
        cost_estimate=cost(12),
    )(sel, hidden, raised_late, raised, active, low_late, low)


def attend_grads_kernel(
    sel_ref, context_ref, x_ref, attn_late_ref, attn_ref, mixed_late_ref, mixed_ref, out_ref
):
    step = pl.program_id(0)
    late = sel_ref[1] == 1

    for wanted, attn_now, mixed_now in (
        (late, attn_late_ref, mixed_late_ref),
        (jnp.logical_not(late), attn_ref, mixed_ref),
    ):

        @pl.when(wanted & (step == 0))
        def _():
            part = dot_tn(context_ref[...], attn_now[...]).astype(BF)
            out_ref[...] = part.reshape(out_ref.shape)

        @pl.when(wanted & (step > 0))
        def _():
            part = dot_tn(x_ref[...], mixed_now[0]).astype(BF)
            out_ref[...] = part.reshape(out_ref.shape)


def attend_grads(sel, context, x, attn_late, attn, mixed_late, mixed):
    length, width = x.shape

    def late_spec(wanted):
        return pl.BlockSpec(
            (length, HALF), lambda n, sel: (0, jnp.where(sel[1] == wanted, sel[2], 0))
        )

    def mixed_spec(wanted):
        def at(n, sel):
            return (
                jnp.where(sel[1] == wanted, jnp.maximum(n - 1, 0), 0),
                0,
                jnp.where(sel[1] == wanted, sel[2], 0),
            )

        return pl.BlockSpec((1, length, HALF), at)

    whole = pl.BlockSpec((length, width), lambda n, _: (0, 0))
    share = width // SHARDS
    return pl.pallas_call(
        attend_grads_kernel,
        name="attend_grads",
        grid_spec=pltpu.PrefetchScalarGridSpec(
            num_scalar_prefetch=1,
            grid=(4,),
            in_specs=[whole, whole, late_spec(1), late_spec(0), mixed_spec(1), mixed_spec(0)],
            out_specs=pl.BlockSpec((SHARDS, share, HALF), lambda n, _: (0, n, 0)),
        ),
        out_shape=jax.ShapeDtypeStruct((SHARDS, 4 * share, HALF), BF),
        compiler_params=PARAMS,
        cost_estimate=cost(8),
    )(sel, context, x, attn_late, attn, mixed_late, mixed)


EXTRA_ROWS = 48


def pack_extras_kernel(
    sel_ref, proj_ref,
    late_sums_0, late_up_0, late_mix_0, late_sums_1, late_up_1, late_mix_1,
    sums_0, up_0, mix_0, sums_1, up_1, mix_1, out_ref,
):
    shards = out_ref.shape[0]
    width = sums_0.shape[1]
    share = width // shards
    third = share // 3
    cols = proj_ref.shape[1]
    out_ref[...] = jnp.zeros_like(out_ref)

    def layer(first, sums, up, mix):
        up_share = up.shape[1] // shards
        both = jnp.concatenate([mix[0:1, :], mix[1:2, :]], axis=1)
        for m in range(shards):
            rows = [up[0:1, m * up_share : (m + 1) * up_share]]
            rows += [both[:, 2 * m * share : 2 * (m + 1) * share]]
            rows += [sums[n : n + 1, m * share : (m + 1) * share] for n in range(6)]
            for n, row in enumerate(rows):
                out_ref[m, first + n : first + n + 1, : row.shape[1]] = row

    late = sel_ref[1] == 1
    for wanted, even, odd in (
        (late, (late_sums_0, late_up_0, late_mix_0), (late_sums_1, late_up_1, late_mix_1)),
        (jnp.logical_not(late), (sums_0, up_0, mix_0), (sums_1, up_1, mix_1)),
    ):

        @pl.when(wanted)
        def _():
            layer(0, *even)
            layer(8, *odd)

    for m in range(shards):
        for n in range(3):
            at = m * share + n * third
            out_ref[m, 16:, n * cols : (n + 1) * cols] = proj_ref[at : at + third, :].astype(F32)


def pack_extras(sel, proj, late_even, late_odd, even, odd):
    vmem = pl.BlockSpec(memory_space=pltpu.VMEM)
    return pl.pallas_call(
        pack_extras_kernel,
        name="pack_extras",
        in_specs=[pl.BlockSpec(memory_space=pltpu.SMEM)] + [vmem] * 13,
        out_specs=vmem,
        out_shape=jax.ShapeDtypeStruct((SHARDS, EXTRA_ROWS, HALF), F32),
        compiler_params=PARAMS,
        cost_estimate=cost(3),
    )(sel, proj, *late_even, *late_odd, *even, *odd)


def forward_kernel(
    layer, begin_ref, count_ref, sel_ref, x_hbm, key_code_ref, query_code_ref,
    mix_own_ref, mix_other_ref, out_own_ref, out_other_ref,
    up_own_ref, up_other_ref, down_own_ref, down_other_ref, small_ref,
    qkv_hbm, context_hbm, logsum_ref, out_hbm, hidden_hbm, scale1_ref, scale2_ref,
    active_hbm, slope_hbm,
    w_mix, w_out, w_up, w_down, x, qkv, context, hidden_rows, out_rows, active_rows, slope_rows,
    value_scr, query_scr, total_scr, weight_sems, in_sems, qkv_sems, row_sems, context_sem,
):
    pairs = [
        (mix_own_ref, mix_other_ref), (out_own_ref, out_other_ref),
        (up_own_ref, up_other_ref), (down_own_ref, down_other_ref),
    ]
    length, width = x.shape
    ff_width = w_up.shape[1]
    blocks = length // ROWS
    at = small_slices(width, ff_width)

    def vector(name):
        return small_ref[0, :, at[name]]

    def rows_of(n):
        return pl.ds(pl.multiple_of(n * ROWS, ROWS), ROWS)

    def x_copy(n):
        return pltpu.make_async_copy(x_hbm.at[rows_of(n)], x.at[rows_of(n)], in_sems.at[n])

    def qkv_copy(n):
        return pltpu.make_async_copy(
            qkv.at[:, rows_of(n)], qkv_hbm.at[:, rows_of(n)], qkv_sems.at[n]
        )

    saved = [
        (hidden_rows, hidden_hbm), (out_rows, out_hbm),
        (active_rows, active_hbm), (slope_rows, slope_hbm),
    ]

    def row_copies(n):
        return [
            pltpu.make_async_copy(rows.at[rows_of(n)], whole.at[rows_of(n)], row_sems.at[k, n])
            for k, (rows, whole) in enumerate(saved)
        ]

    weights = Held(sel_ref, layer, pairs, [w_mix, w_out, w_up, w_down], weight_sems, True)
    for n in range(blocks):
        x_copy(n).start()
    weights.start()
    weights.wait(0)

    def mix_rows(n, _):
        x_copy(n).wait()
        rows = rows_of(n)
        part = dot(x[rows, :], w_mix[...])
        qkv[0, rows, :] = ((part[:, :width] + vector("b_q")) * HEAD**-0.5).astype(BF)
        qkv[1, rows, :] = part[:, width : 2 * width].astype(BF)
        qkv[2, rows, :] = (part[:, 2 * width :] + vector("b_v")).astype(BF)
        qkv_copy(n).start()
        return 0

    lax.fori_loop(0, blocks, mix_rows, 0)
    attend_forward(
        begin_ref, count_ref, qkv, key_code_ref, query_code_ref, context, logsum_ref,
        value_scr, query_scr, total_scr,
    )
    context_copy = pltpu.make_async_copy(context, context_hbm, context_sem)
    context_copy.start()
    for n in (1, 2, 3):
        weights.wait(n)

    def refine_rows(n, _):
        rows = rows_of(n)
        summed = x[rows, :].astype(F32) + dot(context[rows, :], w_out[...]) + vector("b_out")
        hat, inverse = normalized(summed)
        hidden = hat * vector("gain1") + vector("shift1")
        scale1_ref[rows, :] = jnp.broadcast_to(inverse, (ROWS, 128))
        hidden_low = hidden.astype(BF)
        hidden_rows[rows, :] = hidden_low
        total = hidden + vector("b_down")
        parts = [slice(f, f + FB) for f in range(0, ff_width, FB)]
        raised = dot(hidden_low, w_up[:, parts[0]])
        for m, part in enumerate(parts):
            following = dot(hidden_low, w_up[:, parts[m + 1]]) if m + 1 < len(parts) else None
            active, slope = gelu_parts(raised + small_ref[0, :, part])
            active = active.astype(BF)
            active_rows[rows, part] = active
            slope_rows[rows, part] = slope.astype(BF)
            total += dot(active, w_down[part, :])
            raised = following
        hat, inverse = normalized(total)
        scale2_ref[rows, :] = jnp.broadcast_to(inverse, (ROWS, 128))
        out_rows[rows, :] = (hat * vector("gain2") + vector("shift2")).astype(BF)
        for copy in row_copies(n):
            copy.start()
        return 0

    lax.fori_loop(0, blocks, refine_rows, 0)
    context_copy.wait()
    for n in range(blocks):
        qkv_copy(n).wait()
        for copy in row_copies(n):
            copy.wait()


def layer_forward(sel, x, weights, layer, plan):
    w_qkv, w_out, w_up, w_down, small = weights
    begin, count, key_code, query_code = plan
    length, width = x.shape
    ff_width = w_up[0].shape[1]
    pairs = width // PAIR
    blocks = length // ROWS

    def whole(shape):
        return pl.BlockSpec(shape, lambda *_: (0,) * len(shape))

    row = jax.ShapeDtypeStruct((length, width), BF)
    lanes = jax.ShapeDtypeStruct((length, 128), F32)
    wide = jax.ShapeDtypeStruct((length, ff_width), BF)
    logsum_shape = (pairs * (length // QB), 2 * QB)
    qkv, context, logsum, out, hidden, scale1, scale2, active, slope = pl.pallas_call(
        partial(forward_kernel, layer),
        name="layer_forward",
        grid_spec=pltpu.PrefetchScalarGridSpec(
            num_scalar_prefetch=3,
            grid=(1,),
            in_specs=[ANY, whole(key_code.shape), whole(query_code.shape)]
            + [ANY] * 8
            + [small_spec(layer, small.shape[2])],
            out_specs=[
                ANY, ANY, whole(logsum_shape), ANY, ANY,
                whole((length, 128)), whole((length, 128)), ANY, ANY,
            ],
            scratch_shapes=[
                *held_shapes(w_qkv, w_out, w_up, w_down),
                pltpu.VMEM((length, width), BF),
                pltpu.VMEM((3, length, width), BF),
                pltpu.VMEM((length, width), BF),
                pltpu.VMEM((length, width), BF),
                pltpu.VMEM((length, width), BF),
                pltpu.VMEM((length, ff_width), BF),
                pltpu.VMEM((length, ff_width), BF),
                pltpu.VMEM((pairs, PAIR + 16, length), BF),
                pltpu.VMEM((pairs, 2 * QB, PAIR), BF),
                pltpu.VMEM((pairs, PAIR + 16, 2 * QB), F32),
                pltpu.SemaphoreType.DMA((4,)),
                pltpu.SemaphoreType.DMA((blocks,)),
                pltpu.SemaphoreType.DMA((blocks,)),
                pltpu.SemaphoreType.DMA((4, blocks)),
                pltpu.SemaphoreType.DMA,
            ],
        ),
        out_shape=[
            jax.ShapeDtypeStruct((3, length, width), BF), row,
            jax.ShapeDtypeStruct(logsum_shape, F32), row, row, lanes, lanes, wide, wide,
        ],
        compiler_params=PARAMS,
        cost_estimate=cost(48),
    )(begin, count, sel, x, key_code, query_code, *w_qkv, *w_out, *w_up, *w_down, small)
    return (out, (x, qkv, context, logsum, hidden, out, scale1, scale2, slope, active))


def feed_backward(sel, grads, kept, weights, layer):
    first, begun, totals = 0, (), []
    for grad in grads:
        *begun, sums, up_sums = refine_back(
            sel, grad, kept[4:9], weights[1:], layer, first, tuple(begun)
        )
        first += grad.shape[0]
        totals.append((sums, up_sums))
    grad_low, grad_raised, grad_attn, grad_context = begun
    sums = tuple(sum(parts) for parts in zip(*totals))
    return (grad_context, (grad_low, grad_raised, grad_attn), sums)


def mixed_backward_kernel(
    layer, begin_ref, count_ref, sel_ref, qkv_hbm, key_code_ref, query_code_ref, context_hbm,
    logsum_ref, grad_hbm, skip_hbm, mix_own_ref, mix_other_ref,
    mixed_hbm, grad_x_hbm, sums_ref,
    w_mix, qkv, context, grad, skip, key_scr, query_scr, given_scr, down_scr,
    grad_key_scr, grad_value_scr, weight_sems, in_sems, mixed_sems, row_sems,
):
    length, width = skip.shape
    blocks = length // ROWS
    weights = Held(sel_ref, layer, [(mix_own_ref, mix_other_ref)], [w_mix], weight_sems, True)
    arrays = [(qkv_hbm, qkv), (context_hbm, context), (grad_hbm, grad), (skip_hbm, skip)]
    loads = [
        pltpu.make_async_copy(whole, held, in_sems.at[n]) for n, (whole, held) in enumerate(arrays)
    ]
    for load in loads:
        load.start()
    weights.start()
    grad_key_scr[...] = jnp.zeros_like(grad_key_scr)
    grad_value_scr[...] = jnp.zeros_like(grad_value_scr)
    sums_ref[...] = jnp.zeros_like(sums_ref)
    for load in loads:
        load.wait()
    attend_backward(
        begin_ref, count_ref, qkv, key_code_ref, query_code_ref, context, logsum_ref, grad,
        sums_ref, key_scr, query_scr, given_scr, down_scr, grad_key_scr, grad_value_scr,
    )
    store = pltpu.make_async_copy(qkv, mixed_hbm, mixed_sems.at[0])
    store.start()
    weights.wait(0)

    def rows_of(n):
        return pl.ds(pl.multiple_of(n * ROWS, ROWS), ROWS)

    def row_copy(n):
        return pltpu.make_async_copy(skip.at[rows_of(n)], grad_x_hbm.at[rows_of(n)], row_sems.at[n])

    def unmix_rows(n, _):
        rows = rows_of(n)
        total = skip[rows, :].astype(F32)
        for c in range(3):
            total += dot_nt(qkv[c, rows, :], w_mix[:, c * width : (c + 1) * width])
        skip[rows, :] = total.astype(BF)
        row_copy(n).start()
        return 0

    lax.fori_loop(0, blocks, unmix_rows, 0)
    store.wait()
    for n in range(blocks):
        row_copy(n).wait()


def mixed_backward(sel, grad_context, skip, kept, weights, layer, plan):
    _, qkv, context, logsum = kept[:4]
    begin, count, key_code, query_code = plan
    _, length, width = qkv.shape
    pairs = width // PAIR
    blocks = length // ROWS
    w_qkv = weights[0]

    def whole(shape):
        return pl.BlockSpec(shape, lambda *_: (0,) * len(shape))

    row = pltpu.VMEM((length, width), BF)
    return pl.pallas_call(
        partial(mixed_backward_kernel, layer),
        name="mixed_backward",
        grid_spec=pltpu.PrefetchScalarGridSpec(
            num_scalar_prefetch=3,
            grid=(1,),
            in_specs=[ANY, whole(key_code.shape), whole(query_code.shape), ANY, whole(logsum.shape)]
            + [ANY] * 4,
            out_specs=[ANY, ANY, whole((2, width))],
            scratch_shapes=[
                *held_shapes(w_qkv),
                pltpu.VMEM((3, length, width), BF),
                row, row, row,
                pltpu.VMEM((pairs, PAIR, length), BF),
                pltpu.VMEM((pairs, 2 * QB, PAIR), BF),
                pltpu.VMEM((pairs, 2 * QB, PAIR), BF),
                pltpu.VMEM((pairs, PAIR, 2 * QB), F32),
                pltpu.VMEM((length, width), F32),
                pltpu.VMEM((length, width), F32),
                pltpu.SemaphoreType.DMA((1,)),
                pltpu.SemaphoreType.DMA((4,)),
                pltpu.SemaphoreType.DMA((1,)),
                pltpu.SemaphoreType.DMA((blocks,)),
            ],
        ),
        out_shape=[
            jax.ShapeDtypeStruct((3, length, width), BF),
            jax.ShapeDtypeStruct((length, width), BF),
            jax.ShapeDtypeStruct((2, width), F32),
        ],
        compiler_params=PARAMS,
        cost_estimate=cost(38),
    )(begin, count, sel, qkv, key_code, query_code, context, logsum, grad_context, skip, *w_qkv)


def layer_backward(sel, grad, kept, weights, layer, plan):
    grad_context, grads, sums = feed_backward(sel, (grad,), kept, weights, layer)
    grad_mixed, grad_x, mix_sums = mixed_backward(
        sel, grad_context, grads[2], kept, weights, layer, plan
    )
    return (grad_x, grads + (grad_mixed,), sums + (mix_sums,))


def swap_cores(value):
    return send(value, ((0, 1), (1, 0), (2, 3), (3, 2)))


def send(value, routes):
    return lax.ppermute(value, "section", routes)


def pick_row(value, at, axis=0):
    return lax.dynamic_index_in_dim(value, at, axis, keepdims=False)


def plus(*values):
    return sum(value.astype(F32) for value in values).astype(BF)


class RowSum:
    def __init__(self, mine, arrived, blocks):
        self.value, self.blocks, self.travelling = (mine, arrived), blocks, None
        self.plain = lax.axis_size("dp") != SHARDS
        if not self.plain:
            at = lax.axis_index("dp")
            self.z, self.x, self.line_at = at // 2, at % 2, 0

    def state(self):
        return (self.value, self.travelling)

    def set(self, state):
        self.value, self.travelling = state

    def cross(self):
        if self.plain:
            return
        values = [part.reshape(4, 2, *part.shape[1:]) for part in self.value]
        other = plus(*[pick_row(part, 1 - self.x, 1) for part in values])
        arrived = lax.ppermute(other, "dp", [(n, n ^ 1) for n in range(8)])
        self.value = plus(*[pick_row(part, self.x, 1) for part in values], arrived)

    def line(self):
        if self.plain:
            return
        self.line_at += 1
        far = 4 - self.line_at
        right = pick_row(self.value, jnp.minimum(self.z + far, 3))
        left = pick_row(self.value, jnp.maximum(self.z - far, 0))
        if self.travelling is not None:
            right, left = plus(right, self.travelling[0]), plus(left, self.travelling[1])
        self.travelling = (
            lax.ppermute(right, "dp", [(n, n + 2) for n in range(6)]),
            lax.ppermute(left, "dp", [(n + 2, n) for n in range(6)]),
        )

    def direct(self):
        if self.plain:
            return
        arrived = []
        for far in (3, 2, 1):
            for way in (far, -far):
                part = pick_row(self.value, jnp.clip(self.z + way, 0, 3))
                routes = [(n, n + 2 * way) for n in range(8) if 0 <= n + 2 * way < 8]
                arrived.append(lax.ppermute(part, "dp", routes))
        self.travelling = tuple(arrived)

    def result(self):
        if not self.plain:
            return plus(pick_row(self.value, self.z), *self.travelling)
        shards = lax.axis_size("dp")
        parts, at, value = [], 0, plus(*self.value)
        for rows in self.blocks:
            part = value[:, at : at + rows].reshape(shards, -1, value.shape[2])
            parts, at = parts + [part], at + rows
        whole = jnp.concatenate(parts, axis=1)
        return lax.psum_scatter(whole, "dp", scatter_dimension=0, tiled=True)[0]


def body(
    tokens_in, seg_starts, pad_mask, w_qkv, b_qv, w_attn_out, b_attn_out, ln_gain, ln_bias,
    w_up, b_up, w_down, b_down, w_proj, cotangent,
):
    section_at = lax.axis_index("section")
    core = section_at % 2
    is_late = section_at >= 2
    flip = core == 1
    quarter = tokens_in.shape[1]
    length, width = 4 * quarter, tokens_in.shape[2]
    ff_width = w_up.shape[2]
    proj_cols = w_proj.shape[1]
    shards = lax.axis_size("dp")
    share = width // shards

    def sel_for(half):
        return jnp.stack([core, section_at // 2, half]).astype(jnp.int32)

    sel_mine, sel_theirs = sel_for(core), sel_for(1 - core)

    own = pick_row(tokens_in, core)
    other = pick_row(tokens_in, 1 - core)
    straight = send(own, [(2, 0), (3, 1)])
    crossed = send(other, [(2, 1), (3, 0)])
    near = swap_cores(other)
    small = pack_small(b_qv[0], b_attn_out[0], ln_gain[0], ln_bias[0], b_up[0], b_down[0])[None]
    small_other = swap_cores(small)
    small = jnp.stack([jnp.where(flip, small_other, small), jnp.where(flip, small, small_other)])
    weights = tuple((w[0], swap_cores(w[0])) for w in (w_qkv, w_attn_out, w_up, w_down)) + (small,)
    x = jnp.concatenate(
        [
            jnp.where(flip, near, own),
            jnp.where(flip, own, near),
            jnp.where(flip, crossed, straight),
            jnp.where(flip, straight, crossed),
        ],
        axis=0,
    )

    head_own = jnp.concatenate([w_proj.T, pick_row(cotangent, core).T], axis=1)
    head_other = jnp.concatenate([w_proj.T, pick_row(cotangent, 1 - core).T], axis=1)
    head_late = send(head_other, [(2, 3), (3, 2)])
    head_straight = send(head_own, [(0, 2), (1, 3)])
    head_crossed = send(head_other, [(0, 3), (1, 2)])
    head_cols = jnp.concatenate(
        [
            jnp.where(flip, head_crossed, head_straight),
            jnp.where(flip, head_straight, head_crossed),
            jnp.where(flip, head_late, head_own),
            jnp.where(flip, head_own, head_late),
        ],
        axis=0,
    )
    proj_rows, given_rows = head_cols[:, :width], head_cols[:, width:]
    plan = attention_plan(pick_row(seg_starts, core), pick_row(pad_mask, core))

    def both_forward(rows):
        middle, kept_even = layer_forward(sel_mine, rows, weights, 0, plan)
        last, kept_odd = layer_forward(sel_mine, middle, weights, 1, plan)
        return (last, kept_even, kept_odd)

    early, kept_even, kept_odd = both_forward(x)
    hopped = send(early, [(0, 2), (1, 3)])
    hopped, proj_rows, given_rows = lax.optimization_barrier((hopped, proj_rows, given_rows))

    def late_turn(rows, *_):
        last, kept_even, kept_odd = both_forward(rows)
        embedded, grad_proj, grad = head(last, proj_rows, given_rows)
        grad, grads_odd, sums_odd = layer_backward(sel_mine, grad, kept_odd, weights, 1, plan)
        grad, grads_even, sums_even = layer_backward(sel_mine, grad, kept_even, weights, 0, plan)
        return (
            kept_even, kept_odd, embedded, grad_proj, grad,
            grads_odd, sums_odd, grads_even, sums_even,
        )

    def early_turn(rows, kept_even, kept_odd):
        row, ff = jnp.zeros((length, width), BF), jnp.zeros((length, ff_width), BF)
        grads = (row, ff, row, jnp.zeros((3, length, width), BF))
        sums = (
            jnp.zeros((6, width), F32),
            jnp.zeros((1, ff_width), F32),
            jnp.zeros((2, width), F32),
        )
        return (
            kept_even, kept_odd, jnp.zeros((4 * proj_cols, length), BF),
            jnp.zeros((width, 4 * proj_cols), BF), row, grads, sums, grads, sums,
        )

    (
        kept_even, kept_odd, embedded, grad_proj, grad_mid,
        late_odd, late_sums_odd, late_even, late_sums_even,
    ) = lax.cond(is_late, late_turn, early_turn, hopped, kept_even, kept_odd)

    halfway = length // 2
    arriving = [
        send(grad_mid[at : at + halfway], [(2, 0), (3, 1)]) for at in (0, halfway)
    ]
    embedded_cols = embedded.reshape(4, proj_cols, length)

    rows_of_one = width // SHARDS
    attend_blocks = (rows_of_one,) * 4
    feed_blocks = (rows_of_one,) * (ff_width // (2 * HALF)) + (ff_width // SHARDS,)

    def tie(*values):
        return lax.optimization_barrier(values)

    def feed_args(kept, late, now):
        return (kept[4], late[1], now[1], kept[9], late[0], now[0])

    def attend_args(kept, late, now, mixed):
        return (kept[2], kept[0], late[2], now[2], late[3], mixed)

    def tie_sums(values, *sums):
        values, states = tie(values, [part.state() for part in sums])
        for part, state in zip(sums, states):
            part.set(state)
        return values

    grad_context, grads_odd, sums_odd = feed_backward(sel_mine, arriving, kept_odd, weights, 1)
    args = feed_args(kept_odd, late_odd, grads_odd)
    arrived = swap_cores(feed_grads(sel_theirs, *args))
    feed_odd = RowSum(feed_grads(sel_mine, *args), arrived, feed_blocks)
    grad_context = tie_sums(grad_context, feed_odd)
    feed_odd.cross()
    straight_cols = send(pick_row(embedded_cols, core), [(2, 0), (3, 1)])
    crossed_cols = send(pick_row(embedded_cols, 1 - core), [(2, 1), (3, 0)])
    near_cols = swap_cores(pick_row(embedded_cols, 3 - core))
    mixed_odd, grad, mix_sums = mixed_backward(
        sel_mine, grad_context, grads_odd[2], kept_odd, weights, 1, plan
    )
    sums_odd = sums_odd + (mix_sums,)
    args = attend_args(kept_odd, late_odd, grads_odd, mixed_odd)
    args, straight_cols, crossed_cols, near_cols = tie_sums(
        (args, straight_cols, crossed_cols, near_cols), feed_odd
    )
    feed_odd.line()
    theirs = attend_grads(sel_theirs, *args)
    args, theirs = tie_sums((args, theirs), feed_odd)
    arrived = swap_cores(theirs)
    attend_odd = RowSum(attend_grads(sel_mine, *args), arrived, attend_blocks)
    grad = tie_sums(grad, feed_odd, attend_odd)
    feed_odd.line()
    attend_odd.cross()

    grad_context, grads_even, sums_even = feed_backward(sel_mine, (grad,), kept_even, weights, 0)
    args = tie_sums(feed_args(kept_even, late_even, grads_even), feed_odd, attend_odd)
    feed_odd.line()
    theirs = feed_grads(sel_theirs, *args)
    args, theirs = tie_sums((args, theirs), feed_odd)
    arrived = swap_cores(theirs)
    feed_even = RowSum(feed_grads(sel_mine, *args), arrived, feed_blocks)
    grad_context = tie_sums(grad_context, feed_even, attend_odd)
    feed_even.cross()
    attend_odd.direct()
    mixed_even, grad, mix_sums = mixed_backward(
        sel_mine, grad_context, grads_even[2], kept_even, weights, 0, plan
    )
    sums_even = sums_even + (mix_sums,)
    args = attend_args(kept_even, late_even, grads_even, mixed_even)
    args = tie_sums(args, feed_even, attend_odd)
    feed_even.line()
    routes_odd, routes_even = ((0, 1), (2, 3)), ((1, 0), (3, 2))
    feed_odd, attend_odd = feed_odd.result(), attend_odd.result()
    theirs = attend_grads(sel_theirs, *args)
    extras = pack_extras(sel_mine, grad_proj, late_sums_even, late_sums_odd, sums_even, sums_odd)
    theirs = jnp.concatenate([theirs, extras.astype(BF)], axis=1)
    args, theirs, extras = tie_sums((args, theirs, extras), feed_even)
    arrived = swap_cores(theirs)
    feed_even.line()
    quarters = grad.reshape(4, quarter, width)
    near_grad = swap_cores(pick_row(quarters, 1 - core))
    sent_odd = [send(part, routes_odd) for part in (feed_odd, attend_odd)]
    mine = jnp.concatenate([attend_grads(sel_mine, *args), extras.astype(BF)], axis=1)
    mine, quarters, near_grad, sent_odd = tie_sums(
        (mine, quarters, near_grad, sent_odd), feed_even
    )
    attend_even = RowSum(mine, arrived, attend_blocks)
    attend_even.cross()
    feed_even.line()
    straight_grad = send(pick_row(quarters, 2 + core), [(0, 2), (1, 3)])
    crossed_grad = send(pick_row(quarters, 3 - core), [(0, 3), (1, 2)])
    straight_grad, crossed_grad = tie_sums((straight_grad, crossed_grad), feed_even, attend_even)
    attend_even.direct()
    feed_even = feed_even.result()
    if shards == SHARDS:
        tail = attend_even.result()
        attend_even, extras = tail[: 4 * share], tail[4 * share :].astype(F32)
    else:
        attend_even = attend_even.result()
        extras = plus(mine[:, -EXTRA_ROWS:], arrived[:, -EXTRA_ROWS:])
        extras = lax.psum(extras.astype(F32), "dp")

    def halves(even, odd, sent):
        arrived = jnp.where(flip, sent, send(even, routes_even))
        mine = jnp.where(flip, odd, even)
        return (jnp.where(flip, arrived, mine), jnp.where(flip, mine, arrived))

    blocks = ff_width // (2 * HALF)
    feed_halves = halves(feed_even, feed_odd, sent_odd[0])
    attend_halves = halves(attend_even, attend_odd, sent_odd[1])

    def columns(pair, first, count):
        parts = [part[n * share : (n + 1) * share] for part in pair for n in range(first, first + count)]
        return jnp.concatenate(parts, axis=1).astype(F32)

    grad_w_up = columns(feed_halves, 0, blocks)[None]
    grad_w_down = jnp.concatenate([part[blocks * share :] for part in feed_halves], axis=1)
    grad_w_down = grad_w_down.astype(F32)[None]
    grad_w_out = columns(attend_halves, 0, 1)[None]
    grad_w_qkv = jnp.concatenate([columns(attend_halves, 1 + c, 1) for c in range(3)], axis=1)[None]

    if shards == SHARDS:
        at, pick = 0, lambda values: values
    else:
        at = lax.axis_index("dp") % (shards // SHARDS)
        extras = pick_row(extras, lax.axis_index("dp") // (shards // SHARDS))

        def pick(values):
            size = values.shape[-1] * SHARDS // shards
            return lax.dynamic_slice_in_dim(values, at * size, size, values.ndim - 1)

    one = width // SHARDS
    small_mine = jnp.where(flip, extras[8:16], extras[:8])
    grad_b_up = pick(small_mine[0:1, : ff_width // SHARDS])
    grad_b_qv = pick(small_mine[1:2, : 2 * one])
    rows = pick(small_mine[2:8, :one])
    grad_proj = extras[16:].reshape(-1, 3, 4 * proj_cols).transpose(1, 0, 2)
    grad_proj = grad_proj.reshape(one, 4 * proj_cols)
    grad_proj = lax.dynamic_slice_in_dim(grad_proj, at * share, share, 0).astype(BF)
    grad_proj = jnp.where(is_late, grad_proj, send(grad_proj, [(2, 0), (3, 1)])).astype(F32)
    grad_w_proj = lax.dynamic_slice_in_dim(grad_proj, section_at * proj_cols, proj_cols, 1)

    own_cols = jnp.where(is_late, pick_row(embedded_cols, section_at), straight_cols)
    other_cols = jnp.where(is_late, near_cols, crossed_cols)
    embedded_out = jnp.stack(
        [jnp.where(flip, other_cols, own_cols).T, jnp.where(flip, own_cols, other_cols).T]
    )

    mine = jnp.where(is_late, straight_grad, pick_row(quarters, core))
    others = jnp.where(is_late, crossed_grad, near_grad)
    grad_in = jnp.stack(
        [jnp.where(flip, others, mine), jnp.where(flip, mine, others)]
    ).astype(F32)

    return (
        embedded_out,
        grad_in,
        grad_w_qkv,
        grad_b_qv,
        grad_w_out,
        rows[0][None],
        rows[1:3][None],
        rows[3:5][None],
        grad_w_up,
        grad_b_up,
        grad_w_down,
        rows[5][None],
        grad_w_proj,
    )


def solution(mesh):
    in_specs = (
        P("dp", "section", None),
        P("dp", None),
        P("dp", None),
        P("section", None, None),
        P("section", None),
        P("section", None, None),
        P("section", None),
        P("section", None, None),
        P("section", None, None),
        P("section", None, None),
        P("section", None),
        P("section", None, None),
        P("section", None),
        P(None, "section"),
        P("dp", None, "section"),
    )
    out_specs = (
        P("dp", None, "section"),
        P("dp", "section", None),
        P("section", "dp", None),
        P("section", "dp"),
        P("section", "dp", None),
        P("section", "dp"),
        P("section", None, "dp"),
        P("section", None, "dp"),
        P("section", "dp", None),
        P("section", "dp"),
        P("section", "dp", None),
        P("section", "dp"),
        P("dp", "section"),
    )
    return jax.shard_map(body, mesh=mesh, in_specs=in_specs, out_specs=out_specs, check_vma=False)
```

profile of v0, /device:TPU:13, one launch (start us, length us, event | category | flops | bytes accessed | tf_op | source)
XLA Modules:
  0.0 864.2 jit_solution(17161843715125628909)
XLA Ops:
  17.4 8.3 collective-permute-done.2
  33.4 45.8 %layer_forward.8 = (bf16[3,1024,768]{2,1,0:T(8,128)(2,1)}, bf16[1024,768]{1,0:T(8,128)(2,1)}, f32[48,256]{1,0:T(8,128)}, bf16[1024,768]{1,0:T(8,128)(2,1)}, bf16...) custom-call(s32[8]{0:T(128)S(1)} %get-tuple-element.630.begin_ref, ...), custom_call_target="tpu_custom_call" | custom-call | flops 48000000000 | bytes 1024 | tf_op jit(solution)/shard_map/layer_forward/pallas_call | solution.py:729
  79.2 45.8 %layer_forward.9 = (bf16[3,1024,768]{2,1,0:T(8,128)(2,1)}, bf16[1024,768]{1,0:T(8,128)(2,1)}, f32[48,256]{1,0:T(8,128)}, bf16[1024,768]{1,0:T(8,128)(2,1)}, bf16...) custom-call(s32[8]{0:T(128)S(1)} %get-tuple-element.630.begin_ref, ...), custom_call_target="tpu_custom_call" | custom-call | flops 48000000000 | bytes 1024 | tf_op jit(solution)/shard_map/layer_forward/pallas_call | solution.py:729
  132.1 34.9 %collective-permute-done.9 = bf16[32,1792]{1,0:T(8,128)(2,1)S(1)} collective-permute-done((bf16[32,1792]{1,0:T(8,128)(2,1)S(1)}, bf16[32,1792]{1,0:T(8,128)(2,1)S(1)}, u32[]{:S(2)}, u32[]{:S(2)}) %collective-permute-start.9) | collective-permute-done | bytes 114720 | tf_op jit(solution)/shard_map/ppermute | solution.py:895
  167.1 208.6 %conditional.1 = (bf16[1024,768]{1,0:T(8,128)(2,1)}, bf16[3,1024,768]{2,1,0:T(8,128)(2,1)}, bf16[1024,768]{1,0:T(8,128)(2,1)}, f32[48,256]{1,0:T(8,128)}, bf16[1...) conditional(s32[]{:T(128)} %convert_element_type.370, ...), branch_computations={%region_3.4_spmd, %region_4.5_spmd} | conditional | flops 226000011264 | bytes 43916856 | solution.py:1056
  167.1 46.2 %layer_forward.6 = (bf16[3,1024,768]{2,1,0:T(8,128)(2,1)}, bf16[1024,768]{1,0:T(8,128)(2,1)}, f32[48,256]{1,0:T(8,128)}, bf16[1024,768]{1,0:T(8,128)(2,1)}, bf16...) custom-call(s32[8]{0:T(128)S(1)} %get-tuple-element.184.begin_ref, ...), custom_call_target="tpu_custom_call" | custom-call | flops 48000000000 | bytes 1024 | tf_op jit(solution)/shard_map/cond/branch_1_fun/layer_forward/pallas_call | solution.py:729
  213.3 46.4 %layer_forward.7 = (bf16[3,1024,768]{2,1,0:T(8,128)(2,1)}, bf16[1024,768]{1,0:T(8,128)(2,1)}, f32[48,256]{1,0:T(8,128)S(1)}, bf16[1024,768]{1,0:T(8,128)(2,1)S(1...) custom-call(s32[8]{0:T(128)S(1)} %get-tuple-element.184.begin_ref, ...), custom_call_target="tpu_custom_call" | custom-call | flops 48000000000 | bytes 1024 | tf_op jit(solution)/shard_map/cond/branch_1_fun/layer_forward/pallas_call | solution.py:729
  262.5 24.1 %refine_back.7 = (bf16[1024,768]{1,0:T(8,128)(2,1)}, bf16[1024,3072]{1,0:T(8,128)(2,1)}, bf16[1024,768]{1,0:T(8,128)(2,1)S(1)}, bf16[1024,768]{1,0:T(8,128)(2,1)}, f32[6,768]{1,0:T(8,128)}, /*index=5*/f32[1,3072]{1,0:T(1,128)}) custom-call(s32[3]{0:T(128)S(1)} %get-tuple-element.186.sel_ref, bf16[1024,768]{1,0:T(8,128)(2,1)} %get-tuple-element.219.grad_ref, ...), custom_call_target="tpu_custom_call" | custom-call | flops 24000000000 | bytes 1024 | tf_op jit(solution)/shard_map/cond/branch_1_fun/refine_back/pallas_call | solution.py:363
  286.6 31.7 %mixed_backward.6 = (bf16[3,1024,768]{2,1,0:T(8,128)(2,1)}, bf16[1024,768]{1,0:T(8,128)(2,1)}, f32[2,768]{1,0:T(2,128)}) custom-call(s32[8]{0:T(128)S(1)} %get-tuple-element.184.begin_ref, s32[8]{0:T(128)S(1)} %get-tuple-element.185.count_ref, s32[3]{0:T(128)S(1)} %get-tuple-element.186.sel_ref, bf16[3,1024,768]{2,1,0:T(8,128)(2,1)} %get-tuple-element.742.qkv_hbm, ...), custom_call_target="tpu_custom_call" | custom-call | flops 38000001024 | bytes 1024 | tf_op jit(solution)/shard_map/cond/branch_1_fun/mixed_backward/pallas_call | solution.py:847
  318.4 24.4 %refine_back.8 = (bf16[1024,768]{1,0:T(8,128)(2,1)}, bf16[1024,3072]{1,0:T(8,128)(2,1)}, bf16[1024,768]{1,0:T(8,128)(2,1)}, bf16[1024,768]{1,0:T(8,128)(2,1)}, f32[6,768]{1,0:T(8,128)}, /*index=5*/f32[1,3072]{1,0:T(1,128)}) custom-call(s32[3]{0:T(128)S(1)} %get-tuple-element.186.sel_ref, bf16[1024,768]{1,0:T(8,128)(2,1)} %get-tuple-element.222.grad_ref, ...), custom_call_target="tpu_custom_call" | custom-call | flops 24000000000 | bytes 1024 | tf_op jit(solution)/shard_map/cond/branch_1_fun/refine_back/pallas_call | solution.py:363
  342.8 31.3 %mixed_backward.7 = (bf16[3,1024,768]{2,1,0:T(8,128)(2,1)}, bf16[1024,768]{1,0:T(8,128)(2,1)}, f32[2,768]{1,0:T(2,128)}) custom-call(s32[8]{0:T(128)S(1)} %get-tuple-element.184.begin_ref, s32[8]{0:T(128)S(1)} %get-tuple-element.185.count_ref, s32[3]{0:T(128)S(1)} %get-tuple-element.186.sel_ref, bf16[3,1024,768]{2,1,0:T(8,128)(2,1)} %get-tuple-element.733.qkv_hbm, ...), custom_call_target="tpu_custom_call" | custom-call | flops 38000001024 | bytes 1024 | tf_op jit(solution)/shard_map/cond/branch_1_fun/mixed_backward/pallas_call | solution.py:847
  381.5 8.1 collective-permute-done.13.grad_ref
  390.5 15.4 %refine_back.9 = (bf16[1024,768]{1,0:T(8,128)(2,1)}, bf16[1024,3072]{1,0:T(8,128)(2,1)}, bf16[1024,768]{1,0:T(8,128)(2,1)}, bf16[1024,768]{1,0:T(8,128)(2,1)}, f32[6,768]{1,0:T(8,128)}, /*index=5*/f32[1,3072]{1,0:T(1,128)}) custom-call(s32[3]{0:T(128)S(1)} %pad_add_fusion.sel_ref.refs_0_, bf16[512,768]{1,0:T(8,128)(2,1)} %copy-done.52, ...), custom_call_target="tpu_custom_call" | custom-call | flops 24000000000 | bytes 1024 | tf_op jit(solution)/shard_map/refine_back/pallas_call | solution.py:363
  406.4 15.4 %refine_back.10 = (bf16[1024,768]{1,0:T(8,128)(2,1)}, bf16[1024,3072]{1,0:T(8,128)(2,1)}, bf16[1024,768]{1,0:T(8,128)(2,1)}, bf16[1024,768]{1,0:T(8,128)(2,1)}, f32[6,768]{1,0:T(8,128)}, /*index=5*/f32[1,3072]{1,0:T(1,128)}) custom-call(s32[3]{0:T(128)S(1)} %pad_add_fusion.sel_ref.refs_0_, ...), custom_call_target="tpu_custom_call", output_to_operand_aliasing={{0}: (14, {}), {1}: (15, {}), {2}: (16, {}), {3}: (17, {})} | custom-call | flops 24000000000 | bytes 1024 | tf_op jit(solution)/shard_map/refine_back/pallas_call | solution.py:363
  421.8 13.6 %feed_grads.5 = bf16[8,768,384]{2,1,0:T(8,128)(2,1)} custom-call(s32[3]{0:T(128)} %pad_add_fusion.2.sel_ref, bf16[1024,768]{1,0:T(8,128)(2,1)} %get-tuple-element.450.hidden_ref.refs_2_, bf16[1024,3072]{1,0:T(8,128)(2,1)} %get-tuple-element.464.raised_late_ref, bf16[1024,3072]{1,0:T(8,128)(2,1)} %get-tuple-element.465.raised_ref, ...), custom_call_target="tpu_custom_call" | custom-call | flops 12000000000 | bytes 1024 | tf_op jit(solution)/shard_map/feed_grads/pallas_call | solution.py:475
  435.4 12.8 %collective-permute-start.14 = (bf16[8,768,384]{2,1,0:T(8,128)(2,1)}, bf16[8,768,384]{2,1,0:T(8,128)(2,1)}, u32[]{:S(2)}, u32[]{:S(2)}) collective-permute-start(bf16[8,768,384]{2,1,0:T(8,128)(2,1)} %feed_grads.5), channel_id=1, source_target_pairs={{0,8},{8,0},{16,24},{24,16},{1,9},{9,1},{17,25},{25,17},{2,10},{10... | collective-permute-start | bytes 14155784 | tf_op jit(solution)/shard_map/ppermute | solution.py:895
  455.5 12.9 %feed_grads.4 = bf16[8,768,384]{2,1,0:T(8,128)(2,1)} custom-call(s32[3]{0:T(128)S(1)} %pad_add_fusion.sel_ref.refs_0_, bf16[1024,768]{1,0:T(8,128)(2,1)S(1)} %copy-done.53, bf16[1024,3072]{1,0:T(8,128)(2,1)} %get-tuple-element.464.raised_late_ref, bf16[1024,3072]{1,0:T(8,128)(2,1)} %get-tuple-element.465.raised_ref, ...), custom_call_target="tpu_custom_call" | custom-call | flops 12000000000 | bytes 1024 | tf_op jit(solution)/shard_map/feed_grads/pallas_call | solution.py:475
  471.4 14.6 %collective-permute-start.18 = (bf16[4,768,384]{2,1,0:T(8,128)(2,1)S(1)}, bf16[4,768,384]{2,1,0:T(8,128)(2,1)}, u32[]{:S(2)}, u32[]{:S(2)}) collective-permute-start(bf16[4,768,384]{2,1,0:T(8,128)(2,1)S(1)} %fusion.3), channel_id=1, source_target_pairs={{0,1},{1,0},{2,3},{3,2},{4,5},{5,4},{6,7},{7,6},{8,9},{9,8},{10,11... | collective-permute-start | bytes 7077896 | tf_op jit(solution)/shard_map/ppermute | solution.py:925
  486.0 31.7 %mixed_backward.8 = (bf16[3,1024,768]{2,1,0:T(8,128)(2,1)}, bf16[1024,768]{1,0:T(8,128)(2,1)}, f32[2,768]{1,0:T(2,128)}) custom-call(s32[8]{0:T(128)S(1)} %get-tuple-element.630.begin_ref, s32[8]{0:T(128)S(1)} %get-tuple-element.631.count_ref, s32[3]{0:T(128)S(1)} %pad_add_fusion.sel_ref.refs_0_, bf16[3,1024,768]{2,1,0:T(8,128)(2,1)} %get-tuple-element.461.qkv_hbm, ...), custom_call_target="tpu_custom_call" | custom-call | flops 38000001024 | bytes 1024 | tf_op jit(solution)/shard_map/mixed_backward/pallas_call | solution.py:847
  517.7 19.8 %collective-permute-done.18 = bf16[4,768,384]{2,1,0:T(8,128)(2,1)} collective-permute-done((bf16[4,768,384]{2,1,0:T(8,128)(2,1)S(1)}, bf16[4,768,384]{2,1,0:T(8,128)(2,1)}, u32[]{:S(2)}, u32[]{:S(2)}) %collective-permute-start.18) | collective-permute-done | bytes 2359328 | tf_op jit(solution)/shard_map/ppermute | solution.py:925
  542.8 7.9 collective-permute-start.19
  552.6 8.9 %attend_grads.4 = bf16[8,384,384]{2,1,0:T(8,128)(2,1)} custom-call(s32[3]{0:T(128)} %pad_add_fusion.2.sel_ref, bf16[1024,768]{1,0:T(8,128)(2,1)} %get-tuple-element.491.context_hbm.context_ref, bf16[1024,768]{1,0:T(8,128)(2,1)} %get-tuple-element.492.x_ref.out_ref, bf16[1024,768]{1,0:T(8,128)(2,1)} %get-tuple-element.493.attn_late_ref, ...), custom_call_target="tpu_custom_call" | custom-call | flops 8000000000 | bytes 1024 | tf_op jit(solution)/shard_map/attend_grads/pallas_call | solution.py:541
  568.6 8.7 %attend_grads.5 = bf16[8,384,384]{2,1,0:T(8,128)(2,1)} custom-call(s32[3]{0:T(128)S(1)} %pad_add_fusion.sel_ref.refs_0_, bf16[1024,768]{1,0:T(8,128)(2,1)} %get-tuple-element.491.context_hbm.context_ref, bf16[1024,768]{1,0:T(8,128)(2,1)} %get-tuple-element.492.x_ref.out_ref, bf16[1024,768]{1,0:T(8,128)(2,1)} %get-tuple-element.493.attn_late_ref, ...), custom_call_target="tpu_custom_call" | custom-call | flops 8000000000 | bytes 1024 | tf_op jit(solution)/shard_map/attend_grads/pallas_call | solution.py:541
  587.3 24.4 %refine_back.11 = (bf16[1024,768]{1,0:T(8,128)(2,1)}, bf16[1024,3072]{1,0:T(8,128)(2,1)}, bf16[1024,768]{1,0:T(8,128)(2,1)}, bf16[1024,768]{1,0:T(8,128)(2,1)}, f32[6,768]{1,0:T(8,128)}, /*index=5*/f32[1,3072]{1,0:T(1,128)}) custom-call(s32[3]{0:T(128)S(1)} %pad_add_fusion.sel_ref.refs_0_, bf16[1024,768]{1,0:T(8,128)(2,1)} %get-tuple-element.498.grad_ref, ...), custom_call_target="tpu_custom_call" | custom-call | flops 24000000000 | bytes 1024 | tf_op jit(solution)/shard_map/refine_back/pallas_call | solution.py:363
  623.0 13.4 %feed_grads.6 = bf16[8,768,384]{2,1,0:T(8,128)(2,1)} custom-call(s32[3]{0:T(128)} %pad_add_fusion.2.sel_ref, bf16[1024,768]{1,0:T(8,128)(2,1)} %get-tuple-element.527.hidden_ref, bf16[1024,3072]{1,0:T(8,128)(2,1)} %get-tuple-element.528.raised_late_ref, bf16[1024,3072]{1,0:T(8,128)(2,1)} %get-tuple-element.529.raised_ref, ...), custom_call_target="tpu_custom_call" | custom-call | flops 12000000000 | bytes 1024 | tf_op jit(solution)/shard_map/feed_grads/pallas_call | solution.py:475
  640.6 13.2 %feed_grads.7 = bf16[8,768,384]{2,1,0:T(8,128)(2,1)} custom-call(s32[3]{0:T(128)S(1)} %copy-done.59, bf16[1024,768]{1,0:T(8,128)(2,1)} %get-tuple-element.527.hidden_ref, bf16[1024,3072]{1,0:T(8,128)(2,1)} %get-tuple-element.528.raised_late_ref, bf16[1024,3072]{1,0:T(8,128)(2,1)} %get-tuple-element.529.raised_ref, ...), custom_call_target="tpu_custom_call" | custom-call | flops 12000000000 | bytes 1024 | tf_op jit(solution)/shard_map/feed_grads/pallas_call | solution.py:475
  663.4 7.7 collective-permute-start.31
  672.5 32.8 %mixed_backward.9 = (bf16[3,1024,768]{2,1,0:T(8,128)(2,1)}, bf16[1024,768]{1,0:T(8,128)(2,1)}, f32[2,768]{1,0:T(2,128)}) custom-call(s32[8]{0:T(128)S(1)} %copy-done.43, s32[8]{0:T(128)S(1)} %copy-done.45, s32[3]{0:T(128)S(1)} %copy-done.60, bf16[3,1024,768]{2,1,0:T(8,128)(2,1)} %get-tuple-element.505.qkv_hbm, f32[1024,128]{1,0:T(8,128)S(1)} %copy-done.23, ...), custom_call_target="tpu_custom_call" | custom-call | flops 38000001024 | bytes 1024 | tf_op jit(solution)/shard_map/mixed_backward/pallas_call | solution.py:847
  732.4 8.9 %attend_grads.6 = bf16[8,384,384]{2,1,0:T(8,128)(2,1)} custom-call(s32[3]{0:T(128)} %pad_add_fusion.2.sel_ref, bf16[1024,768]{1,0:T(8,128)(2,1)} %get-tuple-element.562.context_hbm.context_ref, bf16[1024,768]{1,0:T(8,128)(2,1)} %get-tuple-element.563.x_ref, bf16[1024,768]{1,0:T(8,128)(2,1)} %get-tuple-element.564.attn_late_ref, ...), custom_call_target="tpu_custom_call" | custom-call | flops 8000000000 | bytes 1024 | tf_op jit(solution)/shard_map/attend_grads/pallas_call | solution.py:541
  766.1 8.6 attend_grads.7
  791.6 18.0 %collective-permute-done.47 = bf16[4,432,384]{2,1,0:T(8,128)(2,1)} collective-permute-done((bf16[4,432,384]{2,1,0:T(8,128)(2,1)}, bf16[4,432,384]{2,1,0:T(8,128)(2,1)}, u32[]{:S(2)}, u32[]{:S(2)}) %collective-permute-start.47) | collective-permute-done | bytes 1327136 | tf_op jit(solution)/shard_map/ppermute | solution.py:925
  814.1 7.7 collective-permute-start.50
  (333 shorter events, 217.6 us)
Async XLA Ops:
  9.6 21.6 %collective-permute-start.5 = (bf16[768,3072]{1,0:T(8,128)(2,1)}, bf16[768,3072]{1,0:T(8,128)(2,1)}, u32[]{:S(2)}, u32[]{:S(2)}) collective-permute-start(bf16[768,3072]{1,0:T(8,128)(2,1)} %bitcast.269), channel_id=1, source_target_pairs={{0,8},{8,0},{16,24},{24,16},{1,9},{9,1},{17,25},{25,17},{2,10},{10... | collective-permute-start | bytes 14155784 | tf_op jit(solution)/shard_map/ppermute | solution.py:895
  9.7 21.7 %collective-permute-start.6 = (bf16[3072,768]{1,0:T(8,128)(2,1)}, bf16[3072,768]{1,0:T(8,128)(2,1)}, u32[]{:S(2)}, u32[]{:S(2)}) collective-permute-start(bf16[3072,768]{1,0:T(8,128)(2,1)} %bitcast.276), channel_id=1, source_target_pairs={{0,8},{8,0},{16,24},{24,16},{1,9},{9,1},{17,25},{25,17},{2,10},{10... | collective-permute-start | bytes 14155784 | tf_op jit(solution)/shard_map/ppermute | solution.py:895
  125.0 42.0 %collective-permute-start.8 = (bf16[1024,768]{1,0:T(8,128)(2,1)}, bf16[1024,768]{1,0:T(8,128)(2,1)S(1)}, u32[]{:S(2)}, u32[]{:S(2)}) collective-permute-start(bf16[1024,768]{1,0:T(8,128)(2,1)} %get-tuple-element.438), channel_id=1, source_target_pairs={{0,16},{8,24},{1,17},{9,25},{2,18},{10,26},{3,19},{11,27},{4,20},{... | collective-permute-start | bytes 4718600 | tf_op jit(solution)/shard_map/ppermute | solution.py:895
  129.4 37.5 %collective-permute-start.9 = (bf16[32,1792]{1,0:T(8,128)(2,1)S(1)}, bf16[32,1792]{1,0:T(8,128)(2,1)S(1)}, u32[]{:S(2)}, u32[]{:S(2)}) collective-permute-start(bf16[32,1792]{1,0:T(8,128)(2,1)S(1)} %pad_maximum_fusion.8), channel_id=1, source_target_pairs={{0,24},{8,16},{1,25},{9,17},{2,26},{10,18},{3,27},{11,19},{4,28},{... | collective-permute-start | bytes 344072 | tf_op jit(solution)/shard_map/ppermute | solution.py:895
  130.8 36.2 %collective-permute-start.10 = (bf16[32,1792]{1,0:T(8,128)(2,1)S(1)}, bf16[32,1792]{1,0:T(8,128)(2,1)S(1)}, u32[]{:S(2)}, u32[]{:S(2)}) collective-permute-start(bf16[32,1792]{1,0:T(8,128)(2,1)S(1)} %get-tuple-element.685), channel_id=1, source_target_pairs={{0,16},{8,24},{1,17},{9,25},{2,18},{10,26},{3,19},{11,27},{4,20},{... | collective-permute-start | bytes 344072 | tf_op jit(solution)/shard_map/ppermute | solution.py:895
  379.3 27.2 %collective-permute-start.12 = (bf16[512,768]{1,0:T(8,128)(2,1)S(1)}, bf16[512,768]{1,0:T(8,128)(2,1)}, u32[]{:S(2)}, u32[]{:S(2)}) collective-permute-start(bf16[512,768]{1,0:T(8,128)(2,1)S(1)} %get-tuple-element.653), channel_id=1, source_target_pairs={{16,0},{24,8},{17,1},{25,9},{18,2},{26,10},{19,3},{27,11},{20,4},{... | collective-permute-start | bytes 2359304 | tf_op jit(solution)/shard_map/ppermute | solution.py:895
  435.4 33.0 %collective-permute-start.14 = (bf16[8,768,384]{2,1,0:T(8,128)(2,1)}, bf16[8,768,384]{2,1,0:T(8,128)(2,1)}, u32[]{:S(2)}, u32[]{:S(2)}) collective-permute-start(bf16[8,768,384]{2,1,0:T(8,128)(2,1)} %feed_grads.5), channel_id=1, source_target_pairs={{0,8},{8,0},{16,24},{24,16},{1,9},{9,1},{17,25},{25,17},{2,10},{10... | collective-permute-start | bytes 14155784 | tf_op jit(solution)/shard_map/ppermute | solution.py:895
  449.2 92.4 %collective-permute-start.15 = (bf16[32,1024]{1,0:T(8,128)(2,1)S(1)}, bf16[32,1024]{1,0:T(8,128)(2,1)S(1)}, u32[]{:S(2)}, u32[]{:S(2)}) collective-permute-start(bf16[32,1024]{1,0:T(8,128)(2,1)S(1)} %get-tuple-element.678), channel_id=1, source_target_pairs={{16,0},{24,8},{17,1},{25,9},{18,2},{26,10},{19,3},{27,11},{20,4},{... | collective-permute-start | bytes 196616 | tf_op jit(solution)/shard_map/ppermute | solution.py:895
  453.7 87.9 %collective-permute-start.16 = (bf16[32,1024]{1,0:T(8,128)(2,1)S(1)}, bf16[32,1024]{1,0:T(8,128)(2,1)S(1)}, u32[]{:S(2)}, u32[]{:S(2)}) collective-permute-start(bf16[32,1024]{1,0:T(8,128)(2,1)S(1)} %get-tuple-element.677), channel_id=1, source_target_pairs={{16,8},{24,0},{17,9},{25,1},{18,10},{26,2},{19,11},{27,3},{20,12},... | collective-permute-start | bytes 196616 | tf_op jit(solution)/shard_map/ppermute | solution.py:895
  455.0 86.6 %collective-permute-start.17 = (bf16[32,1024]{1,0:T(8,128)(2,1)S(1)}, bf16[32,1024]{1,0:T(8,128)(2,1)S(1)}, u32[]{:S(2)}, u32[]{:S(2)}) collective-permute-start(bf16[32,1024]{1,0:T(8,128)(2,1)S(1)} %get-tuple-element.676), channel_id=1, source_target_pairs={{0,8},{8,0},{16,24},{24,16},{1,9},{9,1},{17,25},{25,17},{2,10},{10... | collective-permute-start | bytes 196616 | tf_op jit(solution)/shard_map/ppermute | solution.py:895
  471.4 66.2 %collective-permute-start.18 = (bf16[4,768,384]{2,1,0:T(8,128)(2,1)S(1)}, bf16[4,768,384]{2,1,0:T(8,128)(2,1)}, u32[]{:S(2)}, u32[]{:S(2)}) collective-permute-start(bf16[4,768,384]{2,1,0:T(8,128)(2,1)S(1)} %fusion.3), channel_id=1, source_target_pairs={{0,1},{1,0},{2,3},{3,2},{4,5},{5,4},{6,7},{7,6},{8,9},{9,8},{10,11... | collective-permute-start | bytes 7077896 | tf_op jit(solution)/shard_map/ppermute | solution.py:925
  542.8 19.7 %collective-permute-start.19 = (bf16[768,384]{1,0:T(8,128)(2,1)}, bf16[768,384]{1,0:T(8,128)(2,1)S(1)}, u32[]{:S(2)}, u32[]{:S(2)}) collective-permute-start(bf16[768,384]{1,0:T(8,128)(2,1)} %get-tuple-element.649), channel_id=1, source_target_pairs={{0,2},{1,3},{2,4},{3,5},{4,6},{5,7},{8,10},{9,11},{10,12},{11,13},... | collective-permute-start | bytes 1769480 | tf_op jit(solution)/shard_map/ppermute | solution.py:938
  579.4 32.3 %collective-permute-start.24 = (bf16[4,384,384]{2,1,0:T(8,128)(2,1)S(1)}, bf16[4,384,384]{2,1,0:T(8,128)(2,1)}, u32[]{:S(2)}, u32[]{:S(2)}) collective-permute-start(bf16[4,384,384]{2,1,0:T(8,128)(2,1)S(1)} %fusion.7), channel_id=1, source_target_pairs={{0,1},{1,0},{2,3},{3,2},{4,5},{5,4},{6,7},{7,6},{8,9},{9,8},{10,11... | collective-permute-start | bytes 3538952 | tf_op jit(solution)/shard_map/ppermute | solution.py:925
  581.1 33.0 %collective-permute-start.22 = (bf16[768,384]{1,0:T(8,128)(2,1)}, bf16[768,384]{1,0:T(8,128)(2,1)}, u32[]{:S(2)}, u32[]{:S(2)}) collective-permute-start(bf16[768,384]{1,0:T(8,128)(2,1)} %get-tuple-element.647), channel_id=1, source_target_pairs={{0,2},{1,3},{2,4},{3,5},{4,6},{5,7},{8,10},{9,11},{10,12},{11,13},... | collective-permute-start | bytes 1769480 | tf_op jit(solution)/shard_map/ppermute | solution.py:938
  583.1 31.1 %collective-permute-start.23 = (bf16[768,384]{1,0:T(8,128)(2,1)}, bf16[768,384]{1,0:T(8,128)(2,1)}, u32[]{:S(2)}, u32[]{:S(2)}) collective-permute-start(bf16[768,384]{1,0:T(8,128)(2,1)} %get-tuple-element.646), channel_id=1, source_target_pairs={{2,0},{3,1},{4,2},{5,3},{6,4},{7,5},{10,8},{11,9},{12,10},{13,11},... | collective-permute-start | bytes 1769480 | tf_op jit(solution)/shard_map/ppermute | solution.py:939
  658.2 54.1 %collective-permute-start.28 = (bf16[4,768,384]{2,1,0:T(8,128)(2,1)}, bf16[4,768,384]{2,1,0:T(8,128)(2,1)}, u32[]{:S(2)}, u32[]{:S(2)}) collective-permute-start(bf16[4,768,384]{2,1,0:T(8,128)(2,1)} %fusion.4), channel_id=1, source_target_pairs={{0,1},{1,0},{2,3},{3,2},{4,5},{5,4},{6,7},{7,6},{8,9},{9,8},{10,11... | collective-permute-start | bytes 7077896 | tf_op jit(solution)/shard_map/ppermute | solution.py:925
  660.7 47.8 %collective-permute-start.29 = (bf16[384,384]{1,0:T(8,128)(2,1)}, bf16[384,384]{1,0:T(8,128)(2,1)}, u32[]{:S(2)}, u32[]{:S(2)}) collective-permute-start(bf16[384,384]{1,0:T(8,128)(2,1)} %get-tuple-element.667), channel_id=1, source_target_pairs={{0,6},{1,7},{8,14},{9,15},{16,22},{17,23},{24,30},{25,31}} | collective-permute-start | bytes 884744 | tf_op jit(solution)/shard_map/ppermute | solution.py:950
  662.0 56.6 %collective-permute-start.30 = (bf16[384,384]{1,0:T(8,128)(2,1)}, bf16[384,384]{1,0:T(8,128)(2,1)}, u32[]{:S(2)}, u32[]{:S(2)}) collective-permute-start(bf16[384,384]{1,0:T(8,128)(2,1)} %get-tuple-element.666), channel_id=1, source_target_pairs={{6,0},{7,1},{14,8},{15,9},{22,16},{23,17},{30,24},{31,25}} | collective-permute-start | bytes 884744 | tf_op jit(solution)/shard_map/ppermute | solution.py:950
  663.4 55.2 %collective-permute-start.31 = (bf16[384,384]{1,0:T(8,128)(2,1)}, bf16[384,384]{1,0:T(8,128)(2,1)}, u32[]{:S(2)}, u32[]{:S(2)}) collective-permute-start(bf16[384,384]{1,0:T(8,128)(2,1)} %get-tuple-element.665), channel_id=1, source_target_pairs={{0,4},{1,5},{2,6},{3,7},{8,12},{9,13},{10,14},{11,15},{16,20},{17,... | collective-permute-start | bytes 884744 | tf_op jit(solution)/shard_map/ppermute | solution.py:950
  671.1 47.5 %collective-permute-start.32 = (bf16[384,384]{1,0:T(8,128)(2,1)}, bf16[384,384]{1,0:T(8,128)(2,1)}, u32[]{:S(2)}, u32[]{:S(2)}) collective-permute-start(bf16[384,384]{1,0:T(8,128)(2,1)} %get-tuple-element.664), channel_id=1, source_target_pairs={{4,0},{5,1},{6,2},{7,3},{12,8},{13,9},{14,10},{15,11},{20,16},{21,... | collective-permute-start | bytes 884744 | tf_op jit(solution)/shard_map/ppermute | solution.py:950
  746.4 31.1 %collective-permute-start.46 = (bf16[8,432,384]{2,1,0:T(8,128)(2,1)}, bf16[8,432,384]{2,1,0:T(8,128)(2,1)}, u32[]{:S(2)}, u32[]{:S(2)}) collective-permute-start(bf16[8,432,384]{2,1,0:T(8,128)(2,1)} %pad_maximum_fusion), channel_id=1, source_target_pairs={{0,8},{8,0},{16,24},{24,16},{1,9},{9,1},{17,25},{25,17},{2,10},{10... | collective-permute-start | bytes 7962632 | tf_op jit(solution)/shard_map/ppermute | solution.py:895
  753.2 23.5 %collective-permute-start.37 = (bf16[256,768]{1,0:T(8,128)(2,1)}, bf16[256,768]{1,0:T(8,128)(2,1)}, u32[]{:S(2)}, u32[]{:S(2)}) collective-permute-start(bf16[256,768]{1,0:T(8,128)(2,1)} %dynamic-slice_bitcast_fusion.6), channel_id=1, source_target_pairs={{0,8},{8,0},{16,24},{24,16},{1,9},{9,1},{17,25},{25,17},{2,10},{10... | collective-permute-start | bytes 1179656 | tf_op jit(solution)/shard_map/ppermute | solution.py:895
  756.6 20.1 %collective-permute-start.39 = (bf16[384,384]{1,0:T(8,128)(2,1)}, bf16[384,384]{1,0:T(8,128)(2,1)}, u32[]{:S(2)}, u32[]{:S(2)}) collective-permute-start(bf16[384,384]{1,0:T(8,128)(2,1)} %fusion.31), channel_id=1, source_target_pairs={{0,8},{16,24},{1,9},{17,25},{2,10},{18,26},{3,11},{19,27},{4,12},{... | collective-permute-start | bytes 884744 | tf_op jit(solution)/shard_map/ppermute | solution.py:895
  781.1 28.5 %collective-permute-start.47 = (bf16[4,432,384]{2,1,0:T(8,128)(2,1)}, bf16[4,432,384]{2,1,0:T(8,128)(2,1)}, u32[]{:S(2)}, u32[]{:S(2)}) collective-permute-start(bf16[4,432,384]{2,1,0:T(8,128)(2,1)} %fusion.6), channel_id=1, source_target_pairs={{0,1},{1,0},{2,3},{3,2},{4,5},{5,4},{6,7},{7,6},{8,9},{9,8},{10,11... | collective-permute-start | bytes 3981320 | tf_op jit(solution)/shard_map/ppermute | solution.py:925
  781.4 30.4 %collective-permute-start.44 = (bf16[768,384]{1,0:T(8,128)(2,1)S(1)}, bf16[768,384]{1,0:T(8,128)(2,1)S(1)}, u32[]{:S(2)}, u32[]{:S(2)}) collective-permute-start(bf16[768,384]{1,0:T(8,128)(2,1)S(1)} %get-tuple-element.639), channel_id=1, source_target_pairs={{0,2},{1,3},{2,4},{3,5},{4,6},{5,7},{8,10},{9,11},{10,12},{11,13},... | collective-permute-start | bytes 1769480 | tf_op jit(solution)/shard_map/ppermute | solution.py:938
  783.5 28.4 %collective-permute-start.45 = (bf16[768,384]{1,0:T(8,128)(2,1)S(1)}, bf16[768,384]{1,0:T(8,128)(2,1)S(1)}, u32[]{:S(2)}, u32[]{:S(2)}) collective-permute-start(bf16[768,384]{1,0:T(8,128)(2,1)S(1)} %get-tuple-element.638), channel_id=1, source_target_pairs={{2,0},{3,1},{4,2},{5,3},{6,4},{7,5},{10,8},{11,9},{12,10},{13,11},... | collective-permute-start | bytes 1769480 | tf_op jit(solution)/shard_map/ppermute | solution.py:939
  788.1 23.7 %collective-permute-start.42 = (bf16[256,768]{1,0:T(8,128)(2,1)S(1)}, bf16[256,768]{1,0:T(8,128)(2,1)S(1)}, u32[]{:S(2)}, u32[]{:S(2)}) collective-permute-start(bf16[256,768]{1,0:T(8,128)(2,1)S(1)} %get-tuple-element.651), channel_id=1, source_target_pairs={{0,16},{8,24},{1,17},{9,25},{2,18},{10,26},{3,19},{11,27},{4,20},{... | collective-permute-start | bytes 1179656 | tf_op jit(solution)/shard_map/ppermute | solution.py:895
  789.4 22.5 %collective-permute-start.43 = (bf16[256,768]{1,0:T(8,128)(2,1)S(1)}, bf16[256,768]{1,0:T(8,128)(2,1)S(1)}, u32[]{:S(2)}, u32[]{:S(2)}) collective-permute-start(bf16[256,768]{1,0:T(8,128)(2,1)S(1)} %get-tuple-element.650), channel_id=1, source_target_pairs={{0,24},{8,16},{1,25},{9,17},{2,26},{10,18},{3,27},{11,19},{4,28},{... | collective-permute-start | bytes 1179656 | tf_op jit(solution)/shard_map/ppermute | solution.py:895
  814.1 24.3 %collective-permute-start.50 = (bf16[432,384]{1,0:T(8,128)(2,1)S(1)}, bf16[432,384]{1,0:T(8,128)(2,1)S(1)}, u32[]{:S(2)}, u32[]{:S(2)}) collective-permute-start(bf16[432,384]{1,0:T(8,128)(2,1)S(1)} %get-tuple-element.658), channel_id=1, source_target_pairs={{0,4},{1,5},{2,6},{3,7},{8,12},{9,13},{10,14},{11,15},{16,20},{17,... | collective-permute-start | bytes 995336 | tf_op jit(solution)/shard_map/ppermute | solution.py:950
  823.1 20.7 %collective-permute-start.52 = (bf16[432,384]{1,0:T(8,128)(2,1)S(1)}, bf16[432,384]{1,0:T(8,128)(2,1)S(1)}, u32[]{:S(2)}, u32[]{:S(2)}) collective-permute-start(bf16[432,384]{1,0:T(8,128)(2,1)S(1)} %get-tuple-element.656), channel_id=1, source_target_pairs={{0,2},{1,3},{2,4},{3,5},{4,6},{5,7},{8,10},{9,11},{10,12},{11,13},... | collective-permute-start | bytes 995336 | tf_op jit(solution)/shard_map/ppermute | solution.py:950
  826.2 23.2 %collective-permute-start.53 = (bf16[432,384]{1,0:T(8,128)(2,1)S(1)}, bf16[432,384]{1,0:T(8,128)(2,1)S(1)}, u32[]{:S(2)}, u32[]{:S(2)}) collective-permute-start(bf16[432,384]{1,0:T(8,128)(2,1)S(1)} %get-tuple-element.655), channel_id=1, source_target_pairs={{2,0},{3,1},{4,2},{5,3},{6,4},{7,5},{10,8},{11,9},{12,10},{13,11},... | collective-permute-start | bytes 995336 | tf_op jit(solution)/shard_map/ppermute | solution.py:950
  831.1 26.9 %collective-permute-start.55 = (bf16[768,384]{1,0:T(8,128)(2,1)S(1)}, bf16[768,384]{1,0:T(8,128)(2,1)}, u32[]{:S(2)}, u32[]{:S(2)}) collective-permute-start(bf16[768,384]{1,0:T(8,128)(2,1)S(1)} %fusion.9), channel_id=1, source_target_pairs={{8,0},{24,16},{9,1},{25,17},{10,2},{26,18},{11,3},{27,19},{12,4},{... | collective-permute-start | bytes 1769480 | tf_op jit(solution)/shard_map/ppermute | solution.py:895
  (86 other events, 3713.7 us)
where the time goes:
time: 874 us; the launch traced here: 864 us
  Pallas kernels  508 us (58%)
  starting transfers between devices  151 us (17%)
  waiting for transfers between devices  119 us (14%)
  other arithmetic  60.1 us (7%)
  local copies, waits for them, and re-layouts  22.5 us (3%)
    pallas_call x4, Pallas kernels, layer_forward(): pl.pallas_call(partial(forward_kernel, layer), name='layer_forward', grid...  184 us
    pallas_call x4, Pallas kernels, mixed_backward(): pl.pallas_call(partial(mixed_backward_kernel, layer), name='mixed_backwar...  128 us
    pallas_call x5, Pallas kernels, refine_back(): pl.pallas_call(partial(refine_back_second_kernel if begun else refine_bac...  104 us
    ppermute x29, starting transfers between devices, send(): return lax.ppermute(value, 'section', routes)  61.4 us
    ppermute x29, waiting for transfers between devices, send(): return lax.ppermute(value, 'section', routes)  57.3 us
    pallas_call x4, Pallas kernels, feed_grads(): pl.pallas_call(feed_grads_kernel, name='feed_grads', grid_spec=pltpu.Pref...  53.1 us
    ppermute x4, waiting for transfers between devices, cross(): arrived = lax.ppermute(other, 'dp', [(n, n ^ 1) for n in range(8)])  37.9 us
    convert_element_type x16, other arithmetic, plus(): return sum((value.astype(F32) for value in values)).astype(BF)  36.3 us
  transfers between devices with their start and end apart: 57, of which 15 were waited for; matrix products, arithmetic and copies ran while one was open for 7% of the time, Pallas kernels for 21%

commit v1 on v0

--- a/solution.py
+++ b/solution.py
@@ -905,39 +905,48 @@
 
 class RowSum:
     def __init__(self, mine, arrived, blocks):
-        self.value, self.blocks, self.travelling = (mine, arrived), blocks, None
+        self.terms, self.blocks, self.crossed, self.travelling = (mine, arrived), blocks, (), ()
         self.plain = lax.axis_size("dp") != SHARDS
+        self.crossed_rows, self.ring_at = 0, 0
         if not self.plain:
             at = lax.axis_index("dp")
-            self.z, self.x, self.line_at = at // 2, at % 2, 0
+            self.z, self.x = at // 2, at % 2
 
     def state(self):
-        return (self.value, self.travelling)
+        return (self.terms, self.crossed, self.travelling)
 
     def set(self, state):
-        self.value, self.travelling = state
-
-    def cross(self):
+        self.terms, self.crossed, self.travelling = state
+
+    def cross(self, rows=None):
         if self.plain:
             return
-        values = [part.reshape(4, 2, *part.shape[1:]) for part in self.value]
-        other = plus(*[pick_row(part, 1 - self.x, 1) for part in values])
-        arrived = lax.ppermute(other, "dp", [(n, n ^ 1) for n in range(8)])
-        self.value = plus(*[pick_row(part, self.x, 1) for part in values], arrived)
-
-    def line(self):
+        first, last = self.crossed_rows, rows or self.terms[0].shape[1]
+        self.crossed_rows = last
+        others = []
+        for term in self.terms:
+            cut = term.reshape(4, 2, *term.shape[1:])[:, :, first:last]
+            others.append(pick_row(cut, 1 - self.x, 1))
+        pairs = [(n, n ^ 1) for n in range(8)]
+        self.crossed += (lax.ppermute(plus(*others), "dp", pairs),)
+
+    def part(self, z, *more):
+        values = []
+        for term in self.terms:
+            _, rows, cols = term.shape
+            cut = lax.dynamic_slice(
+                term.reshape(4, 2, rows, cols), (z, self.x, 0, 0), (1, 1, rows, cols)
+            )
+            values.append(cut[0, 0])
+        values.append(jnp.concatenate([pick_row(part, z) for part in self.crossed], axis=0))
+        return plus(*values, *more)
+
+    def ring(self):
         if self.plain:
             return
-        self.line_at += 1
-        far = 4 - self.line_at
-        right = pick_row(self.value, jnp.minimum(self.z + far, 3))
-        left = pick_row(self.value, jnp.maximum(self.z - far, 0))
-        if self.travelling is not None:
-            right, left = plus(right, self.travelling[0]), plus(left, self.travelling[1])
-        self.travelling = (
-            lax.ppermute(right, "dp", [(n, n + 2) for n in range(6)]),
-            lax.ppermute(left, "dp", [(n + 2, n) for n in range(6)]),
-        )
+        self.ring_at += 1
+        passing = self.part(lax.rem(self.z + 4 - self.ring_at, 4), *self.travelling)
+        self.travelling = (lax.ppermute(passing, "dp", [(n, (n + 2) % 8) for n in range(8)]),)
 
     def direct(self):
         if self.plain:
@@ -945,16 +954,16 @@
         arrived = []
         for far in (3, 2, 1):
             for way in (far, -far):
-                part = pick_row(self.value, jnp.clip(self.z + way, 0, 3))
+                part = self.part(jnp.clip(self.z + way, 0, 3))
                 routes = [(n, n + 2 * way) for n in range(8) if 0 <= n + 2 * way < 8]
                 arrived.append(lax.ppermute(part, "dp", routes))
         self.travelling = tuple(arrived)
 
     def result(self):
         if not self.plain:
-            return plus(pick_row(self.value, self.z), *self.travelling)
+            return self.part(self.z, *self.travelling)
         shards = lax.axis_size("dp")
-        parts, at, value = [], 0, plus(*self.value)
+        parts, at, value = [], 0, plus(*self.terms)
         for rows in self.blocks:
             part = value[:, at : at + rows].reshape(shards, -1, value.shape[2])
             parts, at = parts + [part], at + rows
@@ -1085,7 +1094,7 @@
     arrived = swap_cores(feed_grads(sel_theirs, *args))
     feed_odd = RowSum(feed_grads(sel_mine, *args), arrived, feed_blocks)
     grad_context = tie_sums(grad_context, feed_odd)
-    feed_odd.cross()
+    feed_odd.cross(rows_of_one * 6)
     straight_cols = send(pick_row(embedded_cols, core), [(2, 0), (3, 1)])
     crossed_cols = send(pick_row(embedded_cols, 1 - core), [(2, 1), (3, 0)])
     near_cols = swap_cores(pick_row(embedded_cols, 3 - core))
@@ -1097,53 +1106,57 @@
     args, straight_cols, crossed_cols, near_cols = tie_sums(
         (args, straight_cols, crossed_cols, near_cols), feed_odd
     )
-    feed_odd.line()
+    feed_odd.cross()
     theirs = attend_grads(sel_theirs, *args)
     args, theirs = tie_sums((args, theirs), feed_odd)
+    feed_odd.ring()
     arrived = swap_cores(theirs)
     attend_odd = RowSum(attend_grads(sel_mine, *args), arrived, attend_blocks)
     grad = tie_sums(grad, feed_odd, attend_odd)
-    feed_odd.line()
+    feed_odd.ring()
     attend_odd.cross()
 
     grad_context, grads_even, sums_even = feed_backward(sel_mine, (grad,), kept_even, weights, 0)
     args = tie_sums(feed_args(kept_even, late_even, grads_even), feed_odd, attend_odd)
-    feed_odd.line()
+    feed_odd.ring()
     theirs = feed_grads(sel_theirs, *args)
     args, theirs = tie_sums((args, theirs), feed_odd)
+    attend_odd.ring()
     arrived = swap_cores(theirs)
     feed_even = RowSum(feed_grads(sel_mine, *args), arrived, feed_blocks)
     grad_context = tie_sums(grad_context, feed_even, attend_odd)
     feed_even.cross()
-    attend_odd.direct()
+    attend_odd.ring()
     mixed_even, grad, mix_sums = mixed_backward(
         sel_mine, grad_context, grads_even[2], kept_even, weights, 0, plan
     )
     sums_even = sums_even + (mix_sums,)
     args = attend_args(kept_even, late_even, grads_even, mixed_even)
     args = tie_sums(args, feed_even, attend_odd)
-    feed_even.line()
+    feed_even.ring()
     routes_odd, routes_even = ((0, 1), (2, 3)), ((1, 0), (3, 2))
-    feed_odd, attend_odd = feed_odd.result(), attend_odd.result()
+    feed_odd = feed_odd.result()
     theirs = attend_grads(sel_theirs, *args)
     extras = pack_extras(sel_mine, grad_proj, late_sums_even, late_sums_odd, sums_even, sums_odd)
     theirs = jnp.concatenate([theirs, extras.astype(BF)], axis=1)
     args, theirs, extras = tie_sums((args, theirs, extras), feed_even)
     arrived = swap_cores(theirs)
-    feed_even.line()
+    feed_even.ring()
+    attend_odd.ring()
     quarters = grad.reshape(4, quarter, width)
     near_grad = swap_cores(pick_row(quarters, 1 - core))
-    sent_odd = [send(part, routes_odd) for part in (feed_odd, attend_odd)]
     mine = jnp.concatenate([attend_grads(sel_mine, *args), extras.astype(BF)], axis=1)
-    mine, quarters, near_grad, sent_odd = tie_sums(
-        (mine, quarters, near_grad, sent_odd), feed_even
-    )
+    mine, quarters, near_grad = tie_sums((mine, quarters, near_grad), feed_even, attend_odd)
     attend_even = RowSum(mine, arrived, attend_blocks)
     attend_even.cross()
-    feed_even.line()
+    feed_even.ring()
+    attend_odd = attend_odd.result()
+    sent_odd = [send(part, routes_odd) for part in (feed_odd, attend_odd)]
     straight_grad = send(pick_row(quarters, 2 + core), [(0, 2), (1, 3)])
     crossed_grad = send(pick_row(quarters, 3 - core), [(0, 3), (1, 2)])
-    straight_grad, crossed_grad = tie_sums((straight_grad, crossed_grad), feed_even, attend_even)
+    straight_grad, crossed_grad, sent_odd = tie_sums(
+        (straight_grad, crossed_grad, sent_odd), feed_even, attend_even
+    )
     attend_even.direct()
     feed_even = feed_even.result()
     if shards == SHARDS:

time: 874 us -> 859 us (0.983)
  starting transfers between devices: 151 us -> 118 us
  local copies, waits for them, and re-layouts: 22.5 us -> 34.3 us
    ppermute x16 -> x14, starting transfers between devices: 56.2 us -> 38.5 us  [the longest x5 24.8 us: cross(): self.crossed += (lax.ppermute(plus(*others), 'dp', pairs),)]
    ppermute x12 -> x6, starting transfers between devices: 33.4 us -> 19.7 us  [direct(): arrived.append(lax.ppermute(part, 'dp', routes))]
    ppermute x29, waiting for transfers between devices: 57.3 us -> 69.8 us  [send(): return lax.ppermute(value, 'section', routes)]
    ppermute x16 -> x14, waiting for transfers between devices: 45.2 us -> 39.7 us  [the longest x5 29 us: cross(): self.crossed += (lax.ppermute(plus(*others), 'dp', pairs),)]
    convert_element_type x16 -> x19, other arithmetic: 36.3 us -> 40.9 us  [plus(): return sum((value.astype(F32) for value in values)).astype(BF)]
  transfers between devices with their start and end apart: 57 -> 49, of which waited for: 15 -> 16; matrix products, arithmetic and copies ran while one was open for 7% -> 8% of each run, Pallas kernels for 21% -> 21%
where the time goes in v1:
time: 859 us; the launch traced here: 842 us
  Pallas kernels  502 us (58%)
  waiting for transfers between devices  122 us (14%)
  starting transfers between devices  118 us (14%)
  other arithmetic  63.5 us (7%)
  local copies, waits for them, and re-layouts  34.3 us (4%)
    pallas_call x4, Pallas kernels, layer_forward(): pl.pallas_call(partial(forward_kernel, layer), name='layer_forward', grid...  183 us
    pallas_call x4, Pallas kernels, mixed_backward(): pl.pallas_call(partial(mixed_backward_kernel, layer), name='mixed_backwar...  122 us
    pallas_call x5, Pallas kernels, refine_back(): pl.pallas_call(partial(refine_back_second_kernel if begun else refine_bac...  104 us
    ppermute x29, waiting for transfers between devices, send(): return lax.ppermute(value, 'section', routes)  69.8 us
    ppermute x29, starting transfers between devices, send(): return lax.ppermute(value, 'section', routes)  59.9 us
    pallas_call x4, Pallas kernels, feed_grads(): pl.pallas_call(feed_grads_kernel, name='feed_grads', grid_spec=pltpu.Pref...  53.1 us
    convert_element_type x19, other arithmetic, plus(): return sum((value.astype(F32) for value in values)).astype(BF)  40.9 us
    pallas_call x4, Pallas kernels, attend_grads(): pl.pallas_call(attend_grads_kernel, name='attend_grads', grid_spec=pltpu....  34.2 us
  transfers between devices with their start and end apart: 49, of which 16 were waited for; matrix products, arithmetic and copies ran while one was open for 8% of the time, Pallas kernels for 21%

profile of v1, /device:TPU:13, one launch (start us, length us, event | category | flops | bytes accessed | tf_op | source)
XLA Modules:
  0.0 842.2 jit_solution(6402971437333015990)
XLA Ops:
  17.5 8.3 collective-permute-done.2
  33.5 45.5 %layer_forward.8 = (bf16[3,1024,768]{2,1,0:T(8,128)(2,1)}, bf16[1024,768]{1,0:T(8,128)(2,1)}, f32[48,256]{1,0:T(8,128)}, bf16[1024,768]{1,0:T(8,128)(2,1)}, bf16...) custom-call(s32[8]{0:T(128)S(1)} %get-tuple-element.674.begin_ref, ...), custom_call_target="tpu_custom_call" | custom-call | flops 48000000000 | bytes 1024 | tf_op jit(solution)/shard_map/layer_forward/pallas_call | solution.py:729
  79.0 45.5 %layer_forward.9 = (bf16[3,1024,768]{2,1,0:T(8,128)(2,1)}, bf16[1024,768]{1,0:T(8,128)(2,1)}, f32[48,256]{1,0:T(8,128)}, bf16[1024,768]{1,0:T(8,128)(2,1)}, bf16...) custom-call(s32[8]{0:T(128)S(1)} %get-tuple-element.674.begin_ref, ...), custom_call_target="tpu_custom_call" | custom-call | flops 48000000000 | bytes 1024 | tf_op jit(solution)/shard_map/layer_forward/pallas_call | solution.py:729
  131.6 34.8 %collective-permute-done.9 = bf16[32,1792]{1,0:T(8,128)(2,1)S(1)} collective-permute-done((bf16[32,1792]{1,0:T(8,128)(2,1)S(1)}, bf16[32,1792]{1,0:T(8,128)(2,1)S(1)}, u32[]{:S(2)}, u32[]{:S(2)}) %collective-permute-start.9) | collective-permute-done | bytes 114720 | tf_op jit(solution)/shard_map/ppermute | solution.py:895
  166.6 206.5 %conditional.1 = (bf16[1024,768]{1,0:T(8,128)(2,1)}, bf16[3,1024,768]{2,1,0:T(8,128)(2,1)}, bf16[1024,768]{1,0:T(8,128)(2,1)}, f32[48,256]{1,0:T(8,128)}, bf16[1...) conditional(s32[]{:T(128)} %convert_element_type.504, ...), branch_computations={%region_3.4_spmd, %region_4.5_spmd} | conditional | flops 226000011264 | bytes 43917008 | solution.py:1065
  166.6 45.9 %layer_forward.6 = (bf16[3,1024,768]{2,1,0:T(8,128)(2,1)}, bf16[1024,768]{1,0:T(8,128)(2,1)}, f32[48,256]{1,0:T(8,128)}, bf16[1024,768]{1,0:T(8,128)(2,1)}, bf16...) custom-call(s32[8]{0:T(128)S(1)} %get-tuple-element.184.begin_ref, ...), custom_call_target="tpu_custom_call" | custom-call | flops 48000000000 | bytes 1024 | tf_op jit(solution)/shard_map/cond/branch_1_fun/layer_forward/pallas_call | solution.py:729
  212.6 46.1 %layer_forward.7 = (bf16[3,1024,768]{2,1,0:T(8,128)(2,1)}, bf16[1024,768]{1,0:T(8,128)(2,1)}, f32[48,256]{1,0:T(8,128)S(1)}, bf16[1024,768]{1,0:T(8,128)(2,1)S(1...) custom-call(s32[8]{0:T(128)S(1)} %get-tuple-element.184.begin_ref, ...), custom_call_target="tpu_custom_call" | custom-call | flops 48000000000 | bytes 1024 | tf_op jit(solution)/shard_map/cond/branch_1_fun/layer_forward/pallas_call | solution.py:729
  261.4 24.1 %refine_back.7 = (bf16[1024,768]{1,0:T(8,128)(2,1)}, bf16[1024,3072]{1,0:T(8,128)(2,1)}, bf16[1024,768]{1,0:T(8,128)(2,1)S(1)}, bf16[1024,768]{1,0:T(8,128)(2,1)}, f32[6,768]{1,0:T(8,128)}, /*index=5*/f32[1,3072]{1,0:T(1,128)}) custom-call(s32[3]{0:T(128)S(1)} %get-tuple-element.186.sel_ref, bf16[1024,768]{1,0:T(8,128)(2,1)} %get-tuple-element.219.grad_ref, ...), custom_call_target="tpu_custom_call" | custom-call | flops 24000000000 | bytes 1024 | tf_op jit(solution)/shard_map/cond/branch_1_fun/refine_back/pallas_call | solution.py:363
  285.6 30.8 %mixed_backward.6 = (bf16[3,1024,768]{2,1,0:T(8,128)(2,1)}, bf16[1024,768]{1,0:T(8,128)(2,1)}, f32[2,768]{1,0:T(2,128)}) custom-call(s32[8]{0:T(128)S(1)} %get-tuple-element.184.begin_ref, s32[8]{0:T(128)S(1)} %get-tuple-element.185.count_ref, s32[3]{0:T(128)S(1)} %get-tuple-element.186.sel_ref, bf16[3,1024,768]{2,1,0:T(8,128)(2,1)} %get-tuple-element.768.qkv_hbm, ...), custom_call_target="tpu_custom_call" | custom-call | flops 38000001024 | bytes 1024 | tf_op jit(solution)/shard_map/cond/branch_1_fun/mixed_backward/pallas_call | solution.py:847
  316.4 24.6 %refine_back.8 = (bf16[1024,768]{1,0:T(8,128)(2,1)}, bf16[1024,3072]{1,0:T(8,128)(2,1)}, bf16[1024,768]{1,0:T(8,128)(2,1)}, bf16[1024,768]{1,0:T(8,128)(2,1)}, f32[6,768]{1,0:T(8,128)}, /*index=5*/f32[1,3072]{1,0:T(1,128)}) custom-call(s32[3]{0:T(128)} %copy-done.47, bf16[1024,768]{1,0:T(8,128)(2,1)} %get-tuple-element.222.grad_ref, ...), custom_call_target="tpu_custom_call" | custom-call | flops 24000000000 | bytes 1024 | tf_op jit(solution)/shard_map/cond/branch_1_fun/refine_back/pallas_call | solution.py:363
  341.1 30.3 %mixed_backward.7 = (bf16[3,1024,768]{2,1,0:T(8,128)(2,1)}, bf16[1024,768]{1,0:T(8,128)(2,1)}, f32[2,768]{1,0:T(2,128)}) custom-call(s32[8]{0:T(128)S(1)} %get-tuple-element.184.begin_ref, s32[8]{0:T(128)S(1)} %get-tuple-element.185.count_ref, s32[3]{0:T(128)S(1)} %copy-done.48, bf16[3,1024,768]{2,1,0:T(8,128)(2,1)} %get-tuple-element.759.qkv_hbm, ...), custom_call_target="tpu_custom_call" | custom-call | flops 38000001024 | bytes 1024 | tf_op jit(solution)/shard_map/cond/branch_1_fun/mixed_backward/pallas_call | solution.py:847
  385.8 15.5 %refine_back.9 = (bf16[1024,768]{1,0:T(8,128)(2,1)}, bf16[1024,3072]{1,0:T(8,128)(2,1)}, bf16[1024,768]{1,0:T(8,128)(2,1)}, bf16[1024,768]{1,0:T(8,128)(2,1)}, f32[6,768]{1,0:T(8,128)}, /*index=5*/f32[1,3072]{1,0:T(1,128)}) custom-call(s32[3]{0:T(128)S(1)} %copy-done.46, bf16[512,768]{1,0:T(8,128)(2,1)} %copy-done.38, ...), custom_call_target="tpu_custom_call" | custom-call | flops 24000000000 | bytes 1024 | tf_op jit(solution)/shard_map/refine_back/pallas_call | solution.py:363
  402.0 15.3 %refine_back.10 = (bf16[1024,768]{1,0:T(8,128)(2,1)}, bf16[1024,3072]{1,0:T(8,128)(2,1)}, bf16[1024,768]{1,0:T(8,128)(2,1)}, bf16[1024,768]{1,0:T(8,128)(2,1)}, f32[6,768]{1,0:T(8,128)}, /*index=5*/f32[1,3072]{1,0:T(1,128)}) custom-call(s32[3]{0:T(128)S(1)} %copy-done.46, ...), custom_call_target="tpu_custom_call", output_to_operand_aliasing={{0}: (14, {}), {1}: (15, {}), {2}: (16, {}), {3}: (17, {})} | custom-call | flops 24000000000 | bytes 1024 | tf_op jit(solution)/shard_map/refine_back/pallas_call | solution.py:363
  417.3 13.7 %feed_grads.5 = bf16[8,768,384]{2,1,0:T(8,128)(2,1)} custom-call(s32[3]{0:T(128)} %pad_add_fusion.2.sel_ref, bf16[1024,768]{1,0:T(8,128)(2,1)} %get-tuple-element.472.hidden_ref.refs_2_, bf16[1024,3072]{1,0:T(8,128)(2,1)} %get-tuple-element.486.raised_late_ref, bf16[1024,3072]{1,0:T(8,128)(2,1)} %get-tuple-element.487.raised_ref, ...), custom_call_target="tpu_custom_call" | custom-call | flops 12000000000 | bytes 1024 | tf_op jit(solution)/shard_map/feed_grads/pallas_call | solution.py:475
  431.0 16.6 %collective-permute-start.14 = (bf16[8,768,384]{2,1,0:T(8,128)(2,1)}, bf16[8,768,384]{2,1,0:T(8,128)(2,1)}, u32[]{:S(2)}, u32[]{:S(2)}) collective-permute-start(bf16[8,768,384]{2,1,0:T(8,128)(2,1)} %feed_grads.5), channel_id=1, source_target_pairs={{0,8},{8,0},{16,24},{24,16},{1,9},{9,1},{17,25},{25,17},{2,10},{10... | collective-permute-start | bytes 14155784 | tf_op jit(solution)/shard_map/ppermute | solution.py:895
  456.2 13.0 %feed_grads.4 = bf16[8,768,384]{2,1,0:T(8,128)(2,1)} custom-call(s32[3]{0:T(128)S(1)} %copy-done.46, bf16[1024,768]{1,0:T(8,128)(2,1)S(1)} %copy-done.39, bf16[1024,3072]{1,0:T(8,128)(2,1)} %get-tuple-element.486.raised_late_ref, bf16[1024,3072]{1,0:T(8,128)(2,1)} %get-tuple-element.487.raised_ref, bf16[1024,3072]{1,0:T(8,128)(2,1)} %get-tuple-element.488.active_ref, ...), custom_call_target="tpu_custom_call" | custom-call | flops 12000000000 | bytes 1024 | tf_op jit(solution)/shard_map/feed_grads/pallas_call | solution.py:475
  474.4 21.0 %collective-permute-start.18 = (bf16[4,576,384]{2,1,0:T(8,128)(2,1)S(1)}, bf16[4,576,384]{2,1,0:T(8,128)(2,1)S(1)}, u32[]{:S(2)}, u32[]{:S(2)}) collective-permute-start(bf16[4,576,384]{2,1,0:T(8,128)(2,1)S(1)} %fusion.1), channel_id=1, source_target_pairs={{0,1},{1,0},{2,3},{3,2},{4,5},{5,4},{6,7},{7,6},{8,9},{9,8},{10,11... | collective-permute-start | bytes 5308424 | tf_op jit(solution)/shard_map/ppermute | solution.py:931
  495.4 30.7 %mixed_backward.8 = (bf16[3,1024,768]{2,1,0:T(8,128)(2,1)}, bf16[1024,768]{1,0:T(8,128)(2,1)}, f32[2,768]{1,0:T(2,128)}) custom-call(s32[8]{0:T(128)S(1)} %get-tuple-element.674.begin_ref, s32[8]{0:T(128)S(1)} %get-tuple-element.675.count_ref, s32[3]{0:T(128)S(1)} %copy-done.46, bf16[3,1024,768]{2,1,0:T(8,128)(2,1)} %get-tuple-element.483.qkv_hbm, ...), custom_call_target="tpu_custom_call" | custom-call | flops 38000001024 | bytes 1024 | tf_op jit(solution)/shard_map/mixed_backward/pallas_call | solution.py:847
  526.1 8.0 collective-permute-done.18
  539.8 8.7 %attend_grads.4 = bf16[8,384,384]{2,1,0:T(8,128)(2,1)} custom-call(s32[3]{0:T(128)} %pad_add_fusion.2.sel_ref, bf16[1024,768]{1,0:T(8,128)(2,1)} %get-tuple-element.516.context_hbm.context_ref, bf16[1024,768]{1,0:T(8,128)(2,1)} %get-tuple-element.517.x_ref.out_ref, bf16[1024,768]{1,0:T(8,128)(2,1)S(1)} %copy-done.11, ...), custom_call_target="tpu_custom_call" | custom-call | flops 8000000000 | bytes 1024 | tf_op jit(solution)/shard_map/attend_grads/pallas_call | solution.py:541
  561.4 8.8 %attend_grads.5 = bf16[8,384,384]{2,1,0:T(8,128)(2,1)} custom-call(s32[3]{0:T(128)S(1)} %copy-done.46, bf16[1024,768]{1,0:T(8,128)(2,1)} %get-tuple-element.516.context_hbm.context_ref, bf16[1024,768]{1,0:T(8,128)(2,1)} %get-tuple-element.517.x_ref.out_ref, bf16[1024,768]{1,0:T(8,128)(2,1)} %get-tuple-element.518.attn_late_ref, ...), custom_call_target="tpu_custom_call" | custom-call | flops 8000000000 | bytes 1024 | tf_op jit(solution)/shard_map/attend_grads/pallas_call | solution.py:541
  584.9 24.3 %refine_back.11 = (bf16[1024,768]{1,0:T(8,128)(2,1)}, bf16[1024,3072]{1,0:T(8,128)(2,1)}, bf16[1024,768]{1,0:T(8,128)(2,1)}, bf16[1024,768]{1,0:T(8,128)(2,1)}, f32[6,768]{1,0:T(8,128)}, /*index=5*/f32[1,3072]{1,0:T(1,128)}) custom-call(s32[3]{0:T(128)S(1)} %copy-done.46, bf16[1024,768]{1,0:T(8,128)(2,1)} %get-tuple-element.523.grad_ref, ...), custom_call_target="tpu_custom_call" | custom-call | flops 24000000000 | bytes 1024 | tf_op jit(solution)/shard_map/refine_back/pallas_call | solution.py:363
  614.7 13.2 %feed_grads.6 = bf16[8,768,384]{2,1,0:T(8,128)(2,1)} custom-call(s32[3]{0:T(128)} %pad_add_fusion.2.sel_ref, bf16[1024,768]{1,0:T(8,128)(2,1)} %get-tuple-element.556.hidden_ref, bf16[1024,3072]{1,0:T(8,128)(2,1)} %get-tuple-element.557.raised_late_ref, bf16[1024,3072]{1,0:T(8,128)(2,1)} %get-tuple-element.558.raised_ref, ...), custom_call_target="tpu_custom_call" | custom-call | flops 12000000000 | bytes 1024 | tf_op jit(solution)/shard_map/feed_grads/pallas_call | solution.py:475
  633.8 13.3 %feed_grads.7 = bf16[8,768,384]{2,1,0:T(8,128)(2,1)} custom-call(s32[3]{0:T(128)S(1)} %copy-done.46, bf16[1024,768]{1,0:T(8,128)(2,1)} %get-tuple-element.556.hidden_ref, bf16[1024,3072]{1,0:T(8,128)(2,1)} %get-tuple-element.557.raised_late_ref, bf16[1024,3072]{1,0:T(8,128)(2,1)} %get-tuple-element.558.raised_ref, ...), custom_call_target="tpu_custom_call" | custom-call | flops 12000000000 | bytes 1024 | tf_op jit(solution)/shard_map/feed_grads/pallas_call | solution.py:475
  653.8 30.7 %mixed_backward.9 = (bf16[3,1024,768]{2,1,0:T(8,128)(2,1)}, bf16[1024,768]{1,0:T(8,128)(2,1)}, f32[2,768]{1,0:T(2,128)}) custom-call(s32[8]{0:T(128)S(1)} %get-tuple-element.674.begin_ref, s32[8]{0:T(128)S(1)} %get-tuple-element.675.count_ref, s32[3]{0:T(128)S(1)} %copy-done.46, bf16[3,1024,768]{2,1,0:T(8,128)(2,1)} %get-tuple-element.530.qkv_hbm, ...), custom_call_target="tpu_custom_call" | custom-call | flops 38000001024 | bytes 1024 | tf_op jit(solution)/shard_map/mixed_backward/pallas_call | solution.py:847
  688.6 16.6 %collective-permute-done.27 = bf16[4,768,384]{2,1,0:T(8,128)(2,1)} collective-permute-done((bf16[4,768,384]{2,1,0:T(8,128)(2,1)S(1)}, bf16[4,768,384]{2,1,0:T(8,128)(2,1)}, u32[]{:S(2)}, u32[]{:S(2)}) %collective-permute-start.27) | collective-permute-done | bytes 2359328 | tf_op jit(solution)/shard_map/ppermute | solution.py:931
  709.5 8.5 %attend_grads.6 = bf16[8,384,384]{2,1,0:T(8,128)(2,1)} custom-call(s32[3]{0:T(128)} %pad_add_fusion.2.sel_ref, bf16[1024,768]{1,0:T(8,128)(2,1)} %get-tuple-element.598.context_hbm.context_ref, bf16[1024,768]{1,0:T(8,128)(2,1)S(1)} %copy-done.7, bf16[1024,768]{1,0:T(8,128)(2,1)} %get-tuple-element.600.attn_late_ref, ...), custom_call_target="tpu_custom_call" | custom-call | flops 8000000000 | bytes 1024 | tf_op jit(solution)/shard_map/attend_grads/pallas_call | solution.py:541
  732.4 8.3 attend_grads.7
  742.7 6.5 collective-permute-done.31
  773.8 10.6 %collective-permute-done.34 = bf16[256,768]{1,0:T(8,128)(2,1)} collective-permute-done((bf16[256,768]{1,0:T(8,128)(2,1)}, bf16[256,768]{1,0:T(8,128)(2,1)}, u32[]{:S(2)}, u32[]{:S(2)}) %collective-permute-start.34) | collective-permute-done | bytes 393248 | tf_op jit(solution)/shard_map/ppermute | solution.py:895
  789.3 11.8 %collective-permute-start.42 = (bf16[432,384]{1,0:T(8,128)(2,1)S(1)}, bf16[432,384]{1,0:T(8,128)(2,1)S(1)}, u32[]{:S(2)}, u32[]{:S(2)}) collective-permute-start(bf16[432,384]{1,0:T(8,128)(2,1)S(1)} %get-tuple-element.682), channel_id=1, source_target_pairs={{0,4},{1,5},{2,6},{3,7},{8,12},{9,13},{10,14},{11,15},{16,20},{17,... | collective-permute-start | bytes 995336 | tf_op jit(solution)/shard_map/ppermute | solution.py:959
  815.4 6.5 collective-permute-done.44
  (304 shorter events, 201.9 us)
Async XLA Ops:
  9.7 21.6 %collective-permute-start.5 = (bf16[768,3072]{1,0:T(8,128)(2,1)}, bf16[768,3072]{1,0:T(8,128)(2,1)}, u32[]{:S(2)}, u32[]{:S(2)}) collective-permute-start(bf16[768,3072]{1,0:T(8,128)(2,1)} %bitcast.324), channel_id=1, source_target_pairs={{0,8},{8,0},{16,24},{24,16},{1,9},{9,1},{17,25},{25,17},{2,10},{10... | collective-permute-start | bytes 14155784 | tf_op jit(solution)/shard_map/ppermute | solution.py:895
  9.7 21.7 %collective-permute-start.6 = (bf16[3072,768]{1,0:T(8,128)(2,1)}, bf16[3072,768]{1,0:T(8,128)(2,1)}, u32[]{:S(2)}, u32[]{:S(2)}) collective-permute-start(bf16[3072,768]{1,0:T(8,128)(2,1)} %bitcast.331), channel_id=1, source_target_pairs={{0,8},{8,0},{16,24},{24,16},{1,9},{9,1},{17,25},{25,17},{2,10},{10... | collective-permute-start | bytes 14155784 | tf_op jit(solution)/shard_map/ppermute | solution.py:895
  12.2 19.0 %collective-permute-start.3 = (bf16[768,2304]{1,0:T(8,128)(2,1)}, bf16[768,2304]{1,0:T(8,128)(2,1)S(1)}, u32[]{:S(2)}, u32[]{:S(2)}) collective-permute-start(bf16[768,2304]{1,0:T(8,128)(2,1)} %bitcast.338), channel_id=1, source_target_pairs={{0,8},{8,0},{16,24},{24,16},{1,9},{9,1},{17,25},{25,17},{2,10},{10... | collective-permute-start | bytes 10616840 | tf_op jit(solution)/shard_map/ppermute | solution.py:895
  12.4 18.8 %collective-permute-start.4 = (bf16[768,768]{1,0:T(8,128)(2,1)}, bf16[768,768]{1,0:T(8,128)(2,1)S(1)}, u32[]{:S(2)}, u32[]{:S(2)}) collective-permute-start(bf16[768,768]{1,0:T(8,128)(2,1)} %bitcast.344), channel_id=1, source_target_pairs={{0,8},{8,0},{16,24},{24,16},{1,9},{9,1},{17,25},{25,17},{2,10},{10... | collective-permute-start | bytes 3538952 | tf_op jit(solution)/shard_map/ppermute | solution.py:895
  124.5 42.0 %collective-permute-start.8 = (bf16[1024,768]{1,0:T(8,128)(2,1)}, bf16[1024,768]{1,0:T(8,128)(2,1)S(1)}, u32[]{:S(2)}, u32[]{:S(2)}) collective-permute-start(bf16[1024,768]{1,0:T(8,128)(2,1)} %get-tuple-element.460), channel_id=1, source_target_pairs={{0,16},{8,24},{1,17},{9,25},{2,18},{10,26},{3,19},{11,27},{4,20},{... | collective-permute-start | bytes 4718600 | tf_op jit(solution)/shard_map/ppermute | solution.py:895
  129.0 37.5 %collective-permute-start.9 = (bf16[32,1792]{1,0:T(8,128)(2,1)S(1)}, bf16[32,1792]{1,0:T(8,128)(2,1)S(1)}, u32[]{:S(2)}, u32[]{:S(2)}) collective-permute-start(bf16[32,1792]{1,0:T(8,128)(2,1)S(1)} %pad_maximum_fusion.8), channel_id=1, source_target_pairs={{0,24},{8,16},{1,25},{9,17},{2,26},{10,18},{3,27},{11,19},{4,28},{... | collective-permute-start | bytes 344072 | tf_op jit(solution)/shard_map/ppermute | solution.py:895
  130.3 36.1 %collective-permute-start.10 = (bf16[32,1792]{1,0:T(8,128)(2,1)S(1)}, bf16[32,1792]{1,0:T(8,128)(2,1)S(1)}, u32[]{:S(2)}, u32[]{:S(2)}) collective-permute-start(bf16[32,1792]{1,0:T(8,128)(2,1)S(1)} %get-tuple-element.711), channel_id=1, source_target_pairs={{0,16},{8,24},{1,17},{9,25},{2,18},{10,26},{3,19},{11,27},{4,20},{... | collective-permute-start | bytes 344072 | tf_op jit(solution)/shard_map/ppermute | solution.py:895
  376.6 25.3 %collective-permute-start.12 = (bf16[512,768]{1,0:T(8,128)(2,1)S(1)}, bf16[512,768]{1,0:T(8,128)(2,1)}, u32[]{:S(2)}, u32[]{:S(2)}) collective-permute-start(bf16[512,768]{1,0:T(8,128)(2,1)S(1)} %get-tuple-element.691), channel_id=1, source_target_pairs={{16,0},{24,8},{17,1},{25,9},{18,2},{26,10},{19,3},{27,11},{20,4},{... | collective-permute-start | bytes 2359304 | tf_op jit(solution)/shard_map/ppermute | solution.py:895
  431.0 38.2 %collective-permute-start.14 = (bf16[8,768,384]{2,1,0:T(8,128)(2,1)}, bf16[8,768,384]{2,1,0:T(8,128)(2,1)}, u32[]{:S(2)}, u32[]{:S(2)}) collective-permute-start(bf16[8,768,384]{2,1,0:T(8,128)(2,1)} %feed_grads.5), channel_id=1, source_target_pairs={{0,8},{8,0},{16,24},{24,16},{1,9},{9,1},{17,25},{25,17},{2,10},{10... | collective-permute-start | bytes 14155784 | tf_op jit(solution)/shard_map/ppermute | solution.py:895
  449.1 77.0 %collective-permute-start.15 = (bf16[32,1024]{1,0:T(8,128)(2,1)}, bf16[32,1024]{1,0:T(8,128)(2,1)}, u32[]{:S(2)}, u32[]{:S(2)}) collective-permute-start(bf16[32,1024]{1,0:T(8,128)(2,1)} %get-tuple-element.704), channel_id=1, source_target_pairs={{16,0},{24,8},{17,1},{25,9},{18,2},{26,10},{19,3},{27,11},{20,4},{... | collective-permute-start | bytes 196616 | tf_op jit(solution)/shard_map/ppermute | solution.py:895
  454.0 72.1 %collective-permute-start.16 = (bf16[32,1024]{1,0:T(8,128)(2,1)}, bf16[32,1024]{1,0:T(8,128)(2,1)}, u32[]{:S(2)}, u32[]{:S(2)}) collective-permute-start(bf16[32,1024]{1,0:T(8,128)(2,1)} %get-tuple-element.703), channel_id=1, source_target_pairs={{16,8},{24,0},{17,9},{25,1},{18,10},{26,2},{19,11},{27,3},{20,12},... | collective-permute-start | bytes 196616 | tf_op jit(solution)/shard_map/ppermute | solution.py:895
  455.9 70.2 %collective-permute-start.17 = (bf16[32,1024]{1,0:T(8,128)(2,1)}, bf16[32,1024]{1,0:T(8,128)(2,1)}, u32[]{:S(2)}, u32[]{:S(2)}) collective-permute-start(bf16[32,1024]{1,0:T(8,128)(2,1)} %get-tuple-element.702), channel_id=1, source_target_pairs={{0,8},{8,0},{16,24},{24,16},{1,9},{9,1},{17,25},{25,17},{2,10},{10... | collective-permute-start | bytes 196616 | tf_op jit(solution)/shard_map/ppermute | solution.py:895
  474.4 59.7 %collective-permute-start.18 = (bf16[4,576,384]{2,1,0:T(8,128)(2,1)S(1)}, bf16[4,576,384]{2,1,0:T(8,128)(2,1)S(1)}, u32[]{:S(2)}, u32[]{:S(2)}) collective-permute-start(bf16[4,576,384]{2,1,0:T(8,128)(2,1)S(1)} %fusion.1), channel_id=1, source_target_pairs={{0,1},{1,0},{2,3},{3,2},{4,5},{5,4},{6,7},{7,6},{8,9},{9,8},{10,11... | collective-permute-start | bytes 5308424 | tf_op jit(solution)/shard_map/ppermute | solution.py:931
  552.9 21.3 %collective-permute-start.21 = (bf16[8,384,384]{2,1,0:T(8,128)(2,1)}, bf16[8,384,384]{2,1,0:T(8,128)(2,1)S(1)}, u32[]{:S(2)}, u32[]{:S(2)}) collective-permute-start(bf16[8,384,384]{2,1,0:T(8,128)(2,1)} %attend_grads.4), channel_id=1, source_target_pairs={{0,8},{8,0},{16,24},{24,16},{1,9},{9,1},{17,25},{25,17},{2,10},{10... | collective-permute-start | bytes 7077896 | tf_op jit(solution)/shard_map/ppermute | solution.py:895
  558.0 16.2 %collective-permute-start.20 = (bf16[768,384]{1,0:T(8,128)(2,1)}, bf16[768,384]{1,0:T(8,128)(2,1)}, u32[]{:S(2)}, u32[]{:S(2)}) collective-permute-start(bf16[768,384]{1,0:T(8,128)(2,1)} %fusion.17), channel_id=1, source_target_pairs={{0,2},{1,3},{2,4},{3,5},{4,6},{5,7},{6,0},{7,1},{8,10},{9,11},{10,... | collective-permute-start | bytes 1769480 | tf_op jit(solution)/shard_map/ppermute | solution.py:949
  577.8 31.5 %collective-permute-start.23 = (bf16[4,384,384]{2,1,0:T(8,128)(2,1)}, bf16[4,384,384]{2,1,0:T(8,128)(2,1)S(1)}, u32[]{:S(2)}, u32[]{:S(2)}) collective-permute-start(bf16[4,384,384]{2,1,0:T(8,128)(2,1)} %fusion.3), channel_id=1, source_target_pairs={{0,1},{1,0},{2,3},{3,2},{4,5},{5,4},{6,7},{7,6},{8,9},{9,8},{10,11... | collective-permute-start | bytes 3538952 | tf_op jit(solution)/shard_map/ppermute | solution.py:931
  582.7 26.6 %collective-permute-start.22 = (bf16[768,384]{1,0:T(8,128)(2,1)}, bf16[768,384]{1,0:T(8,128)(2,1)}, u32[]{:S(2)}, u32[]{:S(2)}) collective-permute-start(bf16[768,384]{1,0:T(8,128)(2,1)} %fusion.16), channel_id=1, source_target_pairs={{0,2},{1,3},{2,4},{3,5},{4,6},{5,7},{6,0},{7,1},{8,10},{9,11},{10,... | collective-permute-start | bytes 1769480 | tf_op jit(solution)/shard_map/ppermute | solution.py:949
  627.9 19.2 %collective-permute-start.25 = (bf16[8,768,384]{2,1,0:T(8,128)(2,1)}, bf16[8,768,384]{2,1,0:T(8,128)(2,1)}, u32[]{:S(2)}, u32[]{:S(2)}) collective-permute-start(bf16[8,768,384]{2,1,0:T(8,128)(2,1)} %feed_grads.6), channel_id=1, source_target_pairs={{0,8},{8,0},{16,24},{24,16},{1,9},{9,1},{17,25},{25,17},{2,10},{10... | collective-permute-start | bytes 14155784 | tf_op jit(solution)/shard_map/ppermute | solution.py:895
  649.0 39.6 %collective-permute-start.28 = (bf16[384,384]{1,0:T(8,128)(2,1)}, bf16[384,384]{1,0:T(8,128)(2,1)}, u32[]{:S(2)}, u32[]{:S(2)}) collective-permute-start(bf16[384,384]{1,0:T(8,128)(2,1)} %fusion.37), channel_id=1, source_target_pairs={{0,2},{1,3},{2,4},{3,5},{4,6},{5,7},{6,0},{7,1},{8,10},{9,11},{10,... | collective-permute-start | bytes 884744 | tf_op jit(solution)/shard_map/ppermute | solution.py:949
  652.6 52.5 %collective-permute-start.27 = (bf16[4,768,384]{2,1,0:T(8,128)(2,1)S(1)}, bf16[4,768,384]{2,1,0:T(8,128)(2,1)}, u32[]{:S(2)}, u32[]{:S(2)}) collective-permute-start(bf16[4,768,384]{2,1,0:T(8,128)(2,1)S(1)} %fusion), channel_id=1, source_target_pairs={{0,1},{1,0},{2,3},{3,2},{4,5},{5,4},{6,7},{7,6},{8,9},{9,8},{10,11... | collective-permute-start | bytes 7077896 | tf_op jit(solution)/shard_map/ppermute | solution.py:931
  721.5 27.7 %collective-permute-start.38 = (bf16[8,432,384]{2,1,0:T(8,128)(2,1)}, bf16[8,432,384]{2,1,0:T(8,128)(2,1)}, u32[]{:S(2)}, u32[]{:S(2)}) collective-permute-start(bf16[8,432,384]{2,1,0:T(8,128)(2,1)} %pad_maximum_fusion), channel_id=1, source_target_pairs={{0,8},{8,0},{16,24},{24,16},{1,9},{9,1},{17,25},{25,17},{2,10},{10... | collective-permute-start | bytes 7962632 | tf_op jit(solution)/shard_map/ppermute | solution.py:895
  724.9 17.8 %collective-permute-start.30 = (bf16[256,768]{1,0:T(8,128)(2,1)}, bf16[256,768]{1,0:T(8,128)(2,1)}, u32[]{:S(2)}, u32[]{:S(2)}) collective-permute-start(bf16[256,768]{1,0:T(8,128)(2,1)} %dynamic-slice_bitcast_fusion.6), channel_id=1, source_target_pairs={{0,8},{8,0},{16,24},{24,16},{1,9},{9,1},{17,25},{25,17},{2,10},{10... | collective-permute-start | bytes 1179656 | tf_op jit(solution)/shard_map/ppermute | solution.py:895
  731.7 17.4 %collective-permute-start.31 = (bf16[768,384]{1,0:T(8,128)(2,1)}, bf16[768,384]{1,0:T(8,128)(2,1)}, u32[]{:S(2)}, u32[]{:S(2)}) collective-permute-start(bf16[768,384]{1,0:T(8,128)(2,1)} %fusion.9), channel_id=1, source_target_pairs={{0,2},{1,3},{2,4},{3,5},{4,6},{5,7},{6,0},{7,1},{8,10},{9,11},{10,... | collective-permute-start | bytes 1769480 | tf_op jit(solution)/shard_map/ppermute | solution.py:949
  751.9 32.5 %collective-permute-start.39 = (bf16[4,432,384]{2,1,0:T(8,128)(2,1)}, bf16[4,432,384]{2,1,0:T(8,128)(2,1)}, u32[]{:S(2)}, u32[]{:S(2)}) collective-permute-start(bf16[4,432,384]{2,1,0:T(8,128)(2,1)} %fusion.2), channel_id=1, source_target_pairs={{0,1},{1,0},{2,3},{3,2},{4,5},{5,4},{6,7},{7,6},{8,9},{9,8},{10,11... | collective-permute-start | bytes 3981320 | tf_op jit(solution)/shard_map/ppermute | solution.py:931
  761.0 23.4 %collective-permute-start.37 = (bf16[768,384]{1,0:T(8,128)(2,1)}, bf16[768,384]{1,0:T(8,128)(2,1)}, u32[]{:S(2)}, u32[]{:S(2)}) collective-permute-start(bf16[768,384]{1,0:T(8,128)(2,1)} %fusion.7), channel_id=1, source_target_pairs={{0,2},{1,3},{2,4},{3,5},{4,6},{5,7},{6,0},{7,1},{8,10},{9,11},{10,... | collective-permute-start | bytes 1769480 | tf_op jit(solution)/shard_map/ppermute | solution.py:949
  764.2 20.2 %collective-permute-start.34 = (bf16[256,768]{1,0:T(8,128)(2,1)}, bf16[256,768]{1,0:T(8,128)(2,1)}, u32[]{:S(2)}, u32[]{:S(2)}) collective-permute-start(bf16[256,768]{1,0:T(8,128)(2,1)} %get-tuple-element.688), channel_id=1, source_target_pairs={{0,24},{8,16},{1,25},{9,17},{2,26},{10,18},{3,27},{11,19},{4,28},{... | collective-permute-start | bytes 1179656 | tf_op jit(solution)/shard_map/ppermute | solution.py:895
  787.3 18.4 %collective-permute-start.40 = (bf16[432,384]{1,0:T(8,128)(2,1)S(1)}, bf16[432,384]{1,0:T(8,128)(2,1)S(1)}, u32[]{:S(2)}, u32[]{:S(2)}) collective-permute-start(bf16[432,384]{1,0:T(8,128)(2,1)S(1)} %get-tuple-element.678), channel_id=1, source_target_pairs={{0,6},{1,7},{8,14},{9,15},{16,22},{17,23},{24,30},{25,31}} | collective-permute-start | bytes 995336 | tf_op jit(solution)/shard_map/ppermute | solution.py:959
  788.7 24.4 %collective-permute-start.41 = (bf16[432,384]{1,0:T(8,128)(2,1)S(1)}, bf16[432,384]{1,0:T(8,128)(2,1)S(1)}, u32[]{:S(2)}, u32[]{:S(2)}) collective-permute-start(bf16[432,384]{1,0:T(8,128)(2,1)S(1)} %get-tuple-element.683), channel_id=1, source_target_pairs={{6,0},{7,1},{14,8},{15,9},{22,16},{23,17},{30,24},{31,25}} | collective-permute-start | bytes 995336 | tf_op jit(solution)/shard_map/ppermute | solution.py:959
  789.3 26.0 %collective-permute-start.42 = (bf16[432,384]{1,0:T(8,128)(2,1)S(1)}, bf16[432,384]{1,0:T(8,128)(2,1)S(1)}, u32[]{:S(2)}, u32[]{:S(2)}) collective-permute-start(bf16[432,384]{1,0:T(8,128)(2,1)S(1)} %get-tuple-element.682), channel_id=1, source_target_pairs={{0,4},{1,5},{2,6},{3,7},{8,12},{9,13},{10,14},{11,15},{16,20},{17,... | collective-permute-start | bytes 995336 | tf_op jit(solution)/shard_map/ppermute | solution.py:959
  802.4 19.5 %collective-permute-start.44 = (bf16[432,384]{1,0:T(8,128)(2,1)S(1)}, bf16[432,384]{1,0:T(8,128)(2,1)S(1)}, u32[]{:S(2)}, u32[]{:S(2)}) collective-permute-start(bf16[432,384]{1,0:T(8,128)(2,1)S(1)} %get-tuple-element.680), channel_id=1, source_target_pairs={{0,2},{1,3},{2,4},{3,5},{4,6},{5,7},{8,10},{9,11},{10,12},{11,13},... | collective-permute-start | bytes 995336 | tf_op jit(solution)/shard_map/ppermute | solution.py:959
  805.7 22.0 %collective-permute-start.45 = (bf16[432,384]{1,0:T(8,128)(2,1)S(1)}, bf16[432,384]{1,0:T(8,128)(2,1)S(1)}, u32[]{:S(2)}, u32[]{:S(2)}) collective-permute-start(bf16[432,384]{1,0:T(8,128)(2,1)S(1)} %get-tuple-element.679), channel_id=1, source_target_pairs={{2,0},{3,1},{4,2},{5,3},{6,4},{7,5},{10,8},{11,9},{12,10},{13,11},... | collective-permute-start | bytes 995336 | tf_op jit(solution)/shard_map/ppermute | solution.py:959
  813.0 22.9 %collective-permute-start.47 = (bf16[768,384]{1,0:T(8,128)(2,1)}, bf16[768,384]{1,0:T(8,128)(2,1)}, u32[]{:S(2)}, u32[]{:S(2)}) collective-permute-start(bf16[768,384]{1,0:T(8,128)(2,1)} %fusion.5), channel_id=1, source_target_pairs={{8,0},{24,16},{9,1},{25,17},{10,2},{26,18},{11,3},{27,19},{12,4},{... | collective-permute-start | bytes 1769480 | tf_op jit(solution)/shard_map/ppermute | solution.py:895
  (66 other events, 1799.7 us)

commit v2 on v1

--- a/solution.py
+++ b/solution.py
@@ -106,9 +106,25 @@
     return jnp.where(rows < HEAD, flat[:PAIR, :QB], flat[:PAIR, QB:]).T
 
 
+SAFE_SCORE = 70.0
+
+
+def score_bound(peak):
+    lanes = lax.broadcasted_iota(jnp.int32, peak.shape, 1)
+    return jnp.max(jnp.where(lanes < HEAD, peak, 0.0)) * jnp.max(jnp.where(lanes < HEAD, 0.0, peak))
+
+
+def head_lanes(width):
+    rows = lax.broadcasted_iota(jnp.int32, (2 * width, PAIR), 0)
+    lanes = lax.broadcasted_iota(jnp.int32, (2 * width, PAIR), 1)
+    head = lax.shift_right_logical(rows, 6)
+    wanted = jnp.where(rows < width, head, head - width // HEAD + HEAD)
+    return jnp.where(lanes == wanted, 1.0, 0.0).astype(BF)
+
+
 def attend_forward(
     begin_ref, count_ref, qkv_ref, key_code_ref, query_code_ref, out_ref, logsum_ref,
-    value_scr, query_scr, total_scr,
+    value_scr, query_scr, total_scr, is_safe,
 ):
     length = qkv_ref.shape[1]
     pairs = qkv_ref.shape[2] // PAIR
@@ -118,7 +134,7 @@
         value_scr[p, :PAIR, :] = qkv_ref[2, :, cols[p]].T
         value_scr[p, PAIR:, :] = jnp.ones((value_scr.shape[1] - PAIR, length), BF)
 
-    def one_query_block(i, _):
+    def one_query_block(shifted, i, _):
         query_at = pl.multiple_of(i * QB, QB)
         begin, count = begin_ref[i], count_ref[i]
         query_code = query_code_ref[pl.ds(i, 1), :]
@@ -130,6 +146,11 @@
             rows = pl.ds(key_at, size)
             bias = block_bias(key_code_ref[rows, :], query_code, key_at, query_at)
             scores = [dot_nt(qkv_ref[1, rows, cols[p]], query_scr[p]) + bias for p in every]
+            if not shifted:
+                probs = [jnp.exp(scores[p]).astype(BF) for p in every]
+                for p in every:
+                    total_scr[p] += dot(value_scr[p, :, rows], probs[p])
+                return tops
             fresh = [
                 jnp.maximum(tops[p], jnp.max(scores[p], axis=0, keepdims=True)) for p in every
             ]
@@ -140,7 +161,8 @@
                 )
             return tuple(fresh)
 
-        tops = tuple(jnp.full((1, 2 * QB), 2 * NEG_FILL, F32) for _ in every)
+        lowest = 2 * NEG_FILL if shifted else 0.0
+        tops = tuple(jnp.full((1, 2 * QB), lowest, F32) for _ in every)
         tops = over_keys(begin, count, one_key_block, tops)
         for p in every:
             weight = total_scr[p, PAIR : PAIR + 1, :]
@@ -150,7 +172,11 @@
             ).astype(BF)
         return 0
 
-    lax.fori_loop(0, length // QB, one_query_block, 0)
+    for wanted, shifted in ((is_safe, False), (jnp.logical_not(is_safe), True)):
+
+        @pl.when(wanted)
+        def _():
+            lax.fori_loop(0, length // QB, partial(one_query_block, shifted), 0)
 
 
 def attend_backward(
@@ -191,18 +217,21 @@
         def one_key_block(key_at, size, state):
             rows = pl.ds(key_at, size)
             bias = block_bias(key_code_ref[rows, :], query_code, key_at, query_at)
-            grads = [
-                (dot_nt(qkv[2, rows, cols[p]], given_scr[p]) - inner[p]).astype(BF) for p in every
-            ]
-            parts = [dot_nt(qkv[1, rows, cols[p]], query_scr[p]) + bias for p in every]
-            probs = [jnp.exp(parts[p] - logsum[p]).astype(BF) for p in every]
-            scores = [probs[p] * grads[p] for p in every]
-            for p in every:
-                grad_value_scr[rows, cols[p]] += dot(probs[p], given_scr[p])
-            for p in every:
-                grad_key_scr[rows, cols[p]] += dot(scores[p], query_scr[p])
-            for p in every:
-                down_scr[p] += dot(key_scr[p, :, rows], scores[p])
+            parts, grads, probs, scores = {}, {}, {}, {}
+            for p in range(pairs + 1):
+                if p < pairs:
+                    grads[p] = dot_nt(qkv[2, rows, cols[p]], given_scr[p]) - inner[p]
+                    parts[p] = dot_nt(qkv[1, rows, cols[p]], query_scr[p]) + bias
+                if 0 <= p - 1 < pairs:
+                    q = p - 1
+                    probs[q] = jnp.exp(parts.pop(q) - logsum[q])
+                    scores[q] = (probs[q] * grads.pop(q)).astype(BF)
+                    probs[q] = probs[q].astype(BF)
+                if 0 <= p - 1 < pairs:
+                    q = p - 1
+                    grad_value_scr[rows, cols[q]] += dot(probs.pop(q), given_scr[q])
+                    grad_key_scr[rows, cols[q]] += dot(scores[q], query_scr[q])
+                    down_scr[q] += dot(key_scr[q, :, rows], scores.pop(q))
             return state
 
         over_keys(begin, count, one_key_block, 0)
@@ -608,6 +637,122 @@
     )(sel, proj, *late_even, *late_odd, *even, *odd)
 
 
+def refine_block(
+    rows, x, context, w_out, w_up, w_down, small_ref,
+    hidden_rows, out_rows, scale1_ref, scale2_ref, active_rows, slope_rows,
+):
+    width, ff_width = w_up.shape
+    at = small_slices(width, ff_width)
+
+    def vector(name):
+        return small_ref[0, :, at[name]]
+
+    summed = x[rows, :].astype(F32) + dot(context[rows, :], w_out[...]) + vector("b_out")
+    hat, inverse = normalized(summed)
+    hidden = hat * vector("gain1") + vector("shift1")
+    scale1_ref[rows, :] = jnp.broadcast_to(inverse, (ROWS, 128))
+    hidden_low = hidden.astype(BF)
+    hidden_rows[rows, :] = hidden_low
+    total = hidden + vector("b_down")
+    parts = [slice(f, f + FB) for f in range(0, ff_width, FB)]
+    raised = dot(hidden_low, w_up[:, parts[0]])
+    for m, part in enumerate(parts):
+        following = dot(hidden_low, w_up[:, parts[m + 1]]) if m + 1 < len(parts) else None
+        active, slope = gelu_parts(raised + small_ref[0, :, part])
+        active = active.astype(BF)
+        active_rows[rows, part] = active
+        slope_rows[rows, part] = slope.astype(BF)
+        total += dot(active, w_down[part, :])
+        raised = following
+    hat, inverse = normalized(total)
+    scale2_ref[rows, :] = jnp.broadcast_to(inverse, (ROWS, 128))
+    out_rows[rows, :] = (hat * vector("gain2") + vector("shift2")).astype(BF)
+
+
+def refine_rest_kernel(
+    layer, sel_ref, x_hbm, context_hbm,
+    out_own_ref, out_other_ref, up_own_ref, up_other_ref, down_own_ref, down_other_ref, small_ref,
+    hidden_begun, scale1_begun, scale2_begun, active_begun, slope_begun,
+    out_hbm, hidden_hbm, scale1_ref, scale2_ref, active_hbm, slope_hbm,
+    w_out, w_up, w_down, x, context, hidden_rows, out_rows, active_rows, slope_rows,
+    weight_sems, in_sems, row_sems,
+):
+    pairs = [(out_own_ref, out_other_ref), (up_own_ref, up_other_ref), (down_own_ref, down_other_ref)]
+    count = x.shape[0]
+    first = x_hbm.shape[0] - count
+    weights = Held(sel_ref, layer, pairs, [w_out, w_up, w_down], weight_sems, True)
+    loads = [
+        pltpu.make_async_copy(whole.at[pl.ds(first, count)], held, in_sems.at[n])
+        for n, (whole, held) in enumerate(((x_hbm, x), (context_hbm, context)))
+    ]
+    for load in loads:
+        load.start()
+    weights.start()
+    for load in loads:
+        load.wait()
+    for n in range(3):
+        weights.wait(n)
+    saved = [
+        (hidden_rows, hidden_hbm, first), (out_rows, out_hbm, 0),
+        (active_rows, active_hbm, first), (slope_rows, slope_hbm, first),
+    ]
+
+    def row_copies(n):
+        return [
+            pltpu.make_async_copy(
+                rows.at[pl.ds(pl.multiple_of(n * ROWS, ROWS), ROWS)],
+                whole.at[pl.ds(pl.multiple_of(n * ROWS + at, ROWS), ROWS)],
+                row_sems.at[k, n],
+            )
+            for k, (rows, whole, at) in enumerate(saved)
+        ]
+
+    def refine_rows(n, _):
+        refine_block(
+            pl.ds(pl.multiple_of(n * ROWS, ROWS), ROWS), x, context, w_out, w_up, w_down,
+            small_ref, hidden_rows, out_rows, scale1_ref, scale2_ref, active_rows, slope_rows,
+        )
+        for copy in row_copies(n):
+            copy.start()
+        return 0
+
+    lax.fori_loop(0, count // ROWS, refine_rows, 0)
+    for n in range(count // ROWS):
+        for copy in row_copies(n):
+            copy.wait()
+
+
+def refine_rest(sel, x, context, weights, layer, begun, count):
+    _, w_out, w_up, w_down, small = weights
+    length, width = x.shape
+    ff_width = w_up[0].shape[1]
+    row = pltpu.VMEM((count, width), BF)
+    wide = pltpu.VMEM((count, ff_width), BF)
+    lanes = pl.BlockSpec((count, 128), lambda n, _: (length // count - 1, 0))
+    return pl.pallas_call(
+        partial(refine_rest_kernel, layer),
+        name="refine_rest",
+        grid_spec=pltpu.PrefetchScalarGridSpec(
+            num_scalar_prefetch=1,
+            grid=(1,),
+            in_specs=[ANY] * 8 + [small_spec(layer, small.shape[2])] + [ANY] * 5,
+            out_specs=[ANY, ANY, lanes, lanes, ANY, ANY],
+            scratch_shapes=[
+                *held_shapes(w_out, w_up, w_down),
+                row, row, row, row, wide, wide,
+                pltpu.SemaphoreType.DMA((3,)),
+                pltpu.SemaphoreType.DMA((2,)),
+                pltpu.SemaphoreType.DMA((4, count // ROWS)),
+            ],
+        ),
+        out_shape=[jax.ShapeDtypeStruct((count, width), BF)]
+        + [jax.ShapeDtypeStruct(part.shape, part.dtype) for part in begun],
+        input_output_aliases={10 + n: 1 + n for n in range(5)},
+        compiler_params=PARAMS,
+        cost_estimate=cost(14),
+    )(sel, x, context, *w_out, *w_up, *w_down, small, *begun)
+
+
 def forward_kernel(
     layer, begin_ref, count_ref, sel_ref, x_hbm, key_code_ref, query_code_ref,
     mix_own_ref, mix_other_ref, out_own_ref, out_other_ref,
@@ -615,7 +760,7 @@
     qkv_hbm, context_hbm, logsum_ref, out_hbm, hidden_hbm, scale1_ref, scale2_ref,
     active_hbm, slope_hbm,
     w_mix, w_out, w_up, w_down, x, qkv, context, hidden_rows, out_rows, active_rows, slope_rows,
-    value_scr, query_scr, total_scr, weight_sems, in_sems, qkv_sems, row_sems, context_sem,
+    value_scr, query_scr, total_scr, peak, weight_sems, in_sems, qkv_sems, row_sems, context_sem,
 ):
     pairs = [
         (mix_own_ref, mix_other_ref), (out_own_ref, out_other_ref),
@@ -655,22 +800,30 @@
     for n in range(blocks):
         x_copy(n).start()
     weights.start()
+    peak[...] = jnp.zeros_like(peak)
+    lanes_of = head_lanes(width)
     weights.wait(0)
 
     def mix_rows(n, _):
         x_copy(n).wait()
         rows = rows_of(n)
         part = dot(x[rows, :], w_mix[...])
-        qkv[0, rows, :] = ((part[:, :width] + vector("b_q")) * HEAD**-0.5).astype(BF)
-        qkv[1, rows, :] = part[:, width : 2 * width].astype(BF)
+        queries = ((part[:, :width] + vector("b_q")) * HEAD**-0.5).astype(BF)
+        keys = part[:, width : 2 * width].astype(BF)
+        qkv[0, rows, :] = queries
+        qkv[1, rows, :] = keys
         qkv[2, rows, :] = (part[:, 2 * width :] + vector("b_v")).astype(BF)
+        lengths = dot(jnp.concatenate([queries * queries, keys * keys], axis=1), lanes_of)
+        folded = lengths.reshape(ROWS // 8, 8, lengths.shape[1])
+        peak[...] = jnp.maximum(peak[...], jnp.max(folded, axis=0))
         qkv_copy(n).start()
         return 0
 
     lax.fori_loop(0, blocks, mix_rows, 0)
+    is_safe = score_bound(peak[...]) * 1.02 < SAFE_SCORE * SAFE_SCORE
     attend_forward(
         begin_ref, count_ref, qkv, key_code_ref, query_code_ref, context, logsum_ref,
-        value_scr, query_scr, total_scr,
+        value_scr, query_scr, total_scr, is_safe,
     )
     context_copy = pltpu.make_async_copy(context, context_hbm, context_sem)
     context_copy.start()
@@ -678,40 +831,25 @@
         weights.wait(n)
 
     def refine_rows(n, _):
-        rows = rows_of(n)
-        summed = x[rows, :].astype(F32) + dot(context[rows, :], w_out[...]) + vector("b_out")
-        hat, inverse = normalized(summed)
-        hidden = hat * vector("gain1") + vector("shift1")
-        scale1_ref[rows, :] = jnp.broadcast_to(inverse, (ROWS, 128))
-        hidden_low = hidden.astype(BF)
-        hidden_rows[rows, :] = hidden_low
-        total = hidden + vector("b_down")
-        parts = [slice(f, f + FB) for f in range(0, ff_width, FB)]
-        raised = dot(hidden_low, w_up[:, parts[0]])
-        for m, part in enumerate(parts):
-            following = dot(hidden_low, w_up[:, parts[m + 1]]) if m + 1 < len(parts) else None
-            active, slope = gelu_parts(raised + small_ref[0, :, part])
-            active = active.astype(BF)
-            active_rows[rows, part] = active
-            slope_rows[rows, part] = slope.astype(BF)
-            total += dot(active, w_down[part, :])
-            raised = following
-        hat, inverse = normalized(total)
-        scale2_ref[rows, :] = jnp.broadcast_to(inverse, (ROWS, 128))
-        out_rows[rows, :] = (hat * vector("gain2") + vector("shift2")).astype(BF)
+        refine_block(
+            rows_of(n), x, context, w_out, w_up, w_down, small_ref,
+            hidden_rows, out_rows, scale1_ref, scale2_ref, active_rows, slope_rows,
+        )
         for copy in row_copies(n):
             copy.start()
         return 0
 
-    lax.fori_loop(0, blocks, refine_rows, 0)
+    last = out_hbm.shape[0] // ROWS
+    lax.fori_loop(0, last, refine_rows, 0)
     context_copy.wait()
     for n in range(blocks):
         qkv_copy(n).wait()
+    for n in range(last):
         for copy in row_copies(n):
             copy.wait()
 
 
-def layer_forward(sel, x, weights, layer, plan):
+def layer_forward(sel, x, weights, layer, plan, fed=None):
     w_qkv, w_out, w_up, w_down, small = weights
     begin, count, key_code, query_code = plan
     length, width = x.shape
@@ -751,6 +889,7 @@
                 pltpu.VMEM((pairs, PAIR + 16, length), BF),
                 pltpu.VMEM((pairs, 2 * QB, PAIR), BF),
                 pltpu.VMEM((pairs, PAIR + 16, 2 * QB), F32),
+                pltpu.VMEM((8, PAIR), F32),
                 pltpu.SemaphoreType.DMA((4,)),
                 pltpu.SemaphoreType.DMA((blocks,)),
                 pltpu.SemaphoreType.DMA((blocks,)),
@@ -760,12 +899,25 @@
         ),
         out_shape=[
             jax.ShapeDtypeStruct((3, length, width), BF), row,
-            jax.ShapeDtypeStruct(logsum_shape, F32), row, row, lanes, lanes, wide, wide,
+            jax.ShapeDtypeStruct(logsum_shape, F32),
+            jax.ShapeDtypeStruct((fed or length, width), BF),
+            row, lanes, lanes, wide, wide,
         ],
         compiler_params=PARAMS,
         cost_estimate=cost(48),
     )(begin, count, sel, x, key_code, query_code, *w_qkv, *w_out, *w_up, *w_down, small)
     return (out, (x, qkv, context, logsum, hidden, out, scale1, scale2, slope, active))
+
+
+def layer_forward_halves(sel, x, weights, layer, plan):
+    half = x.shape[0] // 2
+    first, kept = layer_forward(sel, x, weights, layer, plan, half)
+    _, qkv, context, logsum, hidden, _, scale1, scale2, slope, active = kept
+    second, hidden, scale1, scale2, active, slope = refine_rest(
+        sel, x, context, weights, layer, (hidden, scale1, scale2, active, slope), half
+    )
+    out = jnp.concatenate([first, second], axis=0)
+    return ((first, second), (x, qkv, context, logsum, hidden, out, scale1, scale2, slope, active))
 
 
 def feed_backward(sel, grads, kept, weights, layer):
@@ -1010,8 +1162,17 @@
         axis=0,
     )
 
+    plan = attention_plan(pick_row(seg_starts, core), pick_row(pad_mask, core))
+
+    def both_forward(rows):
+        middle, kept_even = layer_forward(sel_mine, rows, weights, 0, plan)
+        last, kept_odd = layer_forward(sel_mine, middle, weights, 1, plan)
+        return (last, kept_even, kept_odd)
+
+    middle, kept_even = layer_forward(sel_mine, x, weights, 0, plan)
     head_own = jnp.concatenate([w_proj.T, pick_row(cotangent, core).T], axis=1)
     head_other = jnp.concatenate([w_proj.T, pick_row(cotangent, 1 - core).T], axis=1)
+    middle, head_own, head_other = lax.optimization_barrier((middle, head_own, head_other))
     head_late = send(head_other, [(2, 3), (3, 2)])
     head_straight = send(head_own, [(0, 2), (1, 3)])
     head_crossed = send(head_other, [(0, 3), (1, 2)])
@@ -1025,16 +1186,11 @@
         axis=0,
     )
     proj_rows, given_rows = head_cols[:, :width], head_cols[:, width:]
-    plan = attention_plan(pick_row(seg_starts, core), pick_row(pad_mask, core))
-
-    def both_forward(rows):
-        middle, kept_even = layer_forward(sel_mine, rows, weights, 0, plan)
-        last, kept_odd = layer_forward(sel_mine, middle, weights, 1, plan)
-        return (last, kept_even, kept_odd)
-
-    early, kept_even, kept_odd = both_forward(x)
-    hopped = send(early, [(0, 2), (1, 3)])
-    hopped, proj_rows, given_rows = lax.optimization_barrier((hopped, proj_rows, given_rows))
+    (first, second), kept_odd = layer_forward_halves(sel_mine, middle, weights, 1, plan)
+    first, proj_rows, given_rows = lax.optimization_barrier((first, proj_rows, given_rows))
+    arrived = send(first, [(0, 2), (1, 3)])
+    arrived, second = lax.optimization_barrier((arrived, second))
+    hopped = jnp.concatenate([arrived, send(second, [(0, 2), (1, 3)])], axis=0)
 
     def late_turn(rows, *_):
         last, kept_even, kept_odd = both_forward(rows)

time: 859 us -> 838 us (0.976); the launches traced: 842 us -> 830 us
  Pallas kernels: 502 us -> 534 us
  starting transfers between devices: 118 us -> 89.3 us
  waiting for transfers between devices: 122 us -> 98.6 us
    pallas_call x4, Pallas kernels: 122 us -> 142 us  [mixed_backward(): pl.pallas_call(partial(mixed_backward_kernel, layer), name='mixed_backwar...]
    ppermute x29 -> x30, starting transfers between devices: 59.9 us -> 40.6 us  [send(): return lax.ppermute(value, 'section', routes)]
    pallas_call x0 -> x1, Pallas kernels: none -> 18.2 us  [refine_rest(): pl.pallas_call(partial(refine_rest_kernel, layer), name='refine_rest', gr...]
    ppermute x29 -> x30, waiting for transfers between devices: 69.8 us -> 53.1 us  [send(): return lax.ppermute(value, 'section', routes)]
    ppermute x5, waiting for transfers between devices: 29 us -> 20.1 us  [cross(): self.crossed += (lax.ppermute(plus(*others), 'dp', pairs),)]
  transfers between devices with their start and end apart: 49 -> 50, of which waited for: 16 -> 16; matrix products, arithmetic and copies ran while one was open for 8% -> 8% of each run, Pallas kernels for 21% -> 29%
where the time goes in v2:
time: 838 us; the launch traced here: 830 us
  Pallas kernels  534 us (64%)
  waiting for transfers between devices  98.6 us (12%)
  starting transfers between devices  89.3 us (11%)
  other arithmetic  68.4 us (8%)
  local copies, waits for them, and re-layouts  36.5 us (4%)
    pallas_call x4, Pallas kernels, layer_forward(): pl.pallas_call(partial(forward_kernel, layer), name='layer_forward', grid...  177 us
    pallas_call x4, Pallas kernels, mixed_backward(): pl.pallas_call(partial(mixed_backward_kernel, layer), name='mixed_backwar...  142 us
    pallas_call x5, Pallas kernels, refine_back(): pl.pallas_call(partial(refine_back_second_kernel if begun else refine_bac...  103 us
    ppermute x30, waiting for transfers between devices, send(): return lax.ppermute(value, 'section', routes)  53.1 us
    pallas_call x4, Pallas kernels, feed_grads(): pl.pallas_call(feed_grads_kernel, name='feed_grads', grid_spec=pltpu.Pref...  53 us
    ppermute x30, starting transfers between devices, send(): return lax.ppermute(value, 'section', routes)  40.6 us
    convert_element_type x19, other arithmetic, plus(): return sum((value.astype(F32) for value in values)).astype(BF)  40.5 us
    pallas_call x4, Pallas kernels, attend_grads(): pl.pallas_call(attend_grads_kernel, name='attend_grads', grid_spec=pltpu....  34.6 us
  transfers between devices with their start and end apart: 50, of which 16 were waited for; matrix products, arithmetic and copies ran while one was open for 8% of the time, Pallas kernels for 29%

profile of v2, /device:TPU:13, one launch (start us, length us, event | category | flops | bytes accessed | tf_op | source)
XLA Modules:
  0.0 829.9 jit_solution(12903169367941589815)
XLA Ops:
  17.4 8.3 %collective-permute-done.2 = bf16[256,768]{1,0:T(8,128)(2,1)S(1)} collective-permute-done((bf16[256,768]{1,0:T(8,128)(2,1)S(1)}, bf16[256,768]{1,0:T(8,128)(2,1)S(1)}, u32[]{:S(2)}, u32[]{:S(2)}) %collective-permute-start.2) | collective-permute-done | bytes 393248 | tf_op jit(solution)/shard_map/ppermute | solution.py:1047
  33.5 46.6 %layer_forward.6 = (bf16[3,1024,768]{2,1,0:T(8,128)(2,1)}, bf16[1024,768]{1,0:T(8,128)(2,1)}, f32[48,256]{1,0:T(8,128)}, bf16[1024,768]{1,0:T(8,128)(2,1)S(1)}, ...) custom-call(s32[8]{0:T(128)S(1)} %get-tuple-element.610.begin_ref, ...), custom_call_target="tpu_custom_call" | custom-call | flops 48000000000 | bytes 1024 | tf_op jit(solution)/shard_map/layer_forward/pallas_call | solution.py:867
  84.6 35.4 %layer_forward.7 = (bf16[3,1024,768]{2,1,0:T(8,128)(2,1)}, bf16[1024,768]{1,0:T(8,128)(2,1)}, f32[48,256]{1,0:T(8,128)}, bf16[512,768]{1,0:T(8,128)(2,1)}, bf16[...) custom-call(s32[8]{0:T(128)S(1)} %get-tuple-element.610.begin_ref, ...), custom_call_target="tpu_custom_call" | custom-call | flops 48000000000 | bytes 1024 | tf_op jit(solution)/shard_map/layer_forward/pallas_call | solution.py:867
  122.5 18.2 %refine_rest.1 = (bf16[512,768]{1,0:T(8,128)(2,1)}, bf16[1024,768]{1,0:T(8,128)(2,1)}, f32[1024,128]{1,0:T(8,128)S(1)}, f32[1024,128]{1,0:T(8,128)}, bf16[1024,3...) custom-call(s32[3]{0:T(128)S(1)} %pad_add_fusion.sel_ref.refs_0_, ...), custom_call_target="tpu_custom_call", output_to_operand_aliasing={{1}: (10, {}), {2}: (11, {}), {3}: (12, {}), {4}: (13, {}),... | custom-call | flops 14000000000 | bytes 1024 | tf_op jit(solution)/shard_map/refine_rest/pallas_call | solution.py:732
  145.2 16.6 %collective-permute-done.12 = bf16[512,768]{1,0:T(8,128)(2,1)} collective-permute-done((bf16[512,768]{1,0:T(8,128)(2,1)}, bf16[512,768]{1,0:T(8,128)(2,1)}, u32[]{:S(2)}, u32[]{:S(2)}) %collective-permute-start.12) | collective-permute-done | bytes 786464 | tf_op jit(solution)/shard_map/ppermute | solution.py:1047
  163.3 221.6 %conditional.1 = (bf16[1024,768]{1,0:T(8,128)(2,1)}, bf16[3,1024,768]{2,1,0:T(8,128)(2,1)}, bf16[1024,768]{1,0:T(8,128)(2,1)}, f32[48,256]{1,0:T(8,128)}, bf16[1...) conditional(s32[]{:T(128)} %convert_element_type.504, ...), branch_computations={%region_3.4_spmd, %region_4.5_spmd} | conditional | flops 226000011264 | bytes 47062592 | solution.py:1221
  163.5 47.8 %layer_forward.4 = (bf16[3,1024,768]{2,1,0:T(8,128)(2,1)}, bf16[1024,768]{1,0:T(8,128)(2,1)}, f32[48,256]{1,0:T(8,128)S(1)}, bf16[1024,768]{1,0:T(8,128)(2,1)S(1...) custom-call(s32[8]{0:T(128)S(1)} %get-tuple-element.96.begin_ref, ...), custom_call_target="tpu_custom_call" | custom-call | flops 48000000000 | bytes 1024 | tf_op jit(solution)/shard_map/cond/branch_1_fun/layer_forward/pallas_call | solution.py:867
  211.3 46.7 %layer_forward.5 = (bf16[3,1024,768]{2,1,0:T(8,128)(2,1)}, bf16[1024,768]{1,0:T(8,128)(2,1)}, f32[48,256]{1,0:T(8,128)S(1)}, bf16[1024,768]{1,0:T(8,128)(2,1)S(1...) custom-call(s32[8]{0:T(128)S(1)} %get-tuple-element.96.begin_ref, ...), custom_call_target="tpu_custom_call" | custom-call | flops 48000000000 | bytes 1024 | tf_op jit(solution)/shard_map/cond/branch_1_fun/layer_forward/pallas_call | solution.py:867
  262.0 24.2 %refine_back.5 = (bf16[1024,768]{1,0:T(8,128)(2,1)}, bf16[1024,3072]{1,0:T(8,128)(2,1)}, bf16[1024,768]{1,0:T(8,128)(2,1)}, bf16[1024,768]{1,0:T(8,128)(2,1)}, f32[6,768]{1,0:T(8,128)}, /*index=5*/f32[1,3072]{1,0:T(1,128)}) custom-call(s32[3]{0:T(128)S(1)} %get-tuple-element.98.sel_ref, bf16[1024,768]{1,0:T(8,128)(2,1)} %get-tuple-element.131.grad_ref, ...), custom_call_target="tpu_custom_call" | custom-call | flops 24000000000 | bytes 1024 | tf_op jit(solution)/shard_map/cond/branch_1_fun/refine_back/pallas_call | solution.py:392
  286.2 35.3 %mixed_backward.4 = (bf16[3,1024,768]{2,1,0:T(8,128)(2,1)}, bf16[1024,768]{1,0:T(8,128)(2,1)}, f32[2,768]{1,0:T(2,128)}) custom-call(s32[8]{0:T(128)S(1)} %get-tuple-element.96.begin_ref, s32[8]{0:T(128)S(1)} %get-tuple-element.97.count_ref, s32[3]{0:T(128)S(1)} %get-tuple-element.98.sel_ref, bf16[3,1024,768]{2,1,0:T(8,128)(2,1)} %get-tuple-element.707.qkv_hbm, ...), custom_call_target="tpu_custom_call" | custom-call | flops 38000001024 | bytes 1024 | tf_op jit(solution)/shard_map/cond/branch_1_fun/mixed_backward/pallas_call | solution.py:999
  321.6 24.3 %refine_back.6 = (bf16[1024,768]{1,0:T(8,128)(2,1)}, bf16[1024,3072]{1,0:T(8,128)(2,1)}, bf16[1024,768]{1,0:T(8,128)(2,1)}, bf16[1024,768]{1,0:T(8,128)(2,1)}, f32[6,768]{1,0:T(8,128)}, /*index=5*/f32[1,3072]{1,0:T(1,128)}) custom-call(s32[3]{0:T(128)S(1)} %get-tuple-element.98.sel_ref, bf16[1024,768]{1,0:T(8,128)(2,1)} %get-tuple-element.134.grad_ref, ...), custom_call_target="tpu_custom_call" | custom-call | flops 24000000000 | bytes 1024 | tf_op jit(solution)/shard_map/cond/branch_1_fun/refine_back/pallas_call | solution.py:392
  345.9 35.2 %mixed_backward.5 = (bf16[3,1024,768]{2,1,0:T(8,128)(2,1)}, bf16[1024,768]{1,0:T(8,128)(2,1)}, f32[2,768]{1,0:T(2,128)}) custom-call(s32[8]{0:T(128)S(1)} %get-tuple-element.96.begin_ref, s32[8]{0:T(128)S(1)} %get-tuple-element.97.count_ref, s32[3]{0:T(128)S(1)} %get-tuple-element.98.sel_ref, bf16[3,1024,768]{2,1,0:T(8,128)(2,1)} %get-tuple-element.697.qkv_hbm, ...), custom_call_target="tpu_custom_call" | custom-call | flops 38000001024 | bytes 1024 | tf_op jit(solution)/shard_map/cond/branch_1_fun/mixed_backward/pallas_call | solution.py:999
  391.9 8.2 collective-permute-done.14.grad_ref
  401.0 15.5 %refine_back.7 = (bf16[1024,768]{1,0:T(8,128)(2,1)}, bf16[1024,3072]{1,0:T(8,128)(2,1)}, bf16[1024,768]{1,0:T(8,128)(2,1)}, bf16[1024,768]{1,0:T(8,128)(2,1)}, f32[6,768]{1,0:T(8,128)}, /*index=5*/f32[1,3072]{1,0:T(1,128)}) custom-call(s32[3]{0:T(128)S(1)} %pad_add_fusion.sel_ref.refs_0_, bf16[512,768]{1,0:T(8,128)(2,1)} %copy-done.48, ...), custom_call_target="tpu_custom_call" | custom-call | flops 24000000000 | bytes 1024 | tf_op jit(solution)/shard_map/refine_back/pallas_call | solution.py:392
  416.5 15.4 %refine_back.8 = (bf16[1024,768]{1,0:T(8,128)(2,1)}, bf16[1024,3072]{1,0:T(8,128)(2,1)}, bf16[1024,768]{1,0:T(8,128)(2,1)}, bf16[1024,768]{1,0:T(8,128)(2,1)}, f32[6,768]{1,0:T(8,128)}, /*index=5*/f32[1,3072]{1,0:T(1,128)}) custom-call(s32[3]{0:T(128)S(1)} %pad_add_fusion.sel_ref.refs_0_, ...), custom_call_target="tpu_custom_call", output_to_operand_aliasing={{0}: (14, {}), {1}: (15, {}), {2}: (16, {}), {3}: (17, {})} | custom-call | flops 24000000000 | bytes 1024 | tf_op jit(solution)/shard_map/refine_back/pallas_call | solution.py:392
  431.9 13.5 %feed_grads.5 = bf16[8,768,384]{2,1,0:T(8,128)(2,1)} custom-call(s32[3]{0:T(128)} %pad_add_fusion.2.sel_ref, bf16[1024,768]{1,0:T(8,128)(2,1)} %get-tuple-element.407.hidden_ref.refs_2_, bf16[1024,3072]{1,0:T(8,128)(2,1)} %get-tuple-element.421.raised_late_ref, bf16[1024,3072]{1,0:T(8,128)(2,1)} %get-tuple-element.422.raised_ref, ...), custom_call_target="tpu_custom_call" | custom-call | flops 12000000000 | bytes 1024 | tf_op jit(solution)/shard_map/feed_grads/pallas_call | solution.py:504
  453.0 13.0 %feed_grads.4 = bf16[8,768,384]{2,1,0:T(8,128)(2,1)} custom-call(s32[3]{0:T(128)S(1)} %copy-done.60, bf16[1024,768]{1,0:T(8,128)(2,1)S(1)} %copy-done.50, bf16[1024,3072]{1,0:T(8,128)(2,1)} %get-tuple-element.421.raised_late_ref, bf16[1024,3072]{1,0:T(8,128)(2,1)} %get-tuple-element.422.raised_ref, bf16[1024,3072]{1,0:T(8,128)(2,1)} %get-tuple-element.423.active_ref, ...), custom_call_target="tpu_custom_call" | custom-call | flops 12000000000 | bytes 1024 | tf_op jit(solution)/shard_map/feed_grads/pallas_call | solution.py:504
  472.5 16.4 %collective-permute-start.19 = (bf16[4,576,384]{2,1,0:T(8,128)(2,1)}, bf16[4,576,384]{2,1,0:T(8,128)(2,1)S(1)}, u32[]{:S(2)}, u32[]{:S(2)}) collective-permute-start(bf16[4,576,384]{2,1,0:T(8,128)(2,1)} %fusion.1), channel_id=1, source_target_pairs={{0,1},{1,0},{2,3},{3,2},{4,5},{5,4},{6,7},{7,6},{8,9},{9,8},{10,11... | collective-permute-start | bytes 5308424 | tf_op jit(solution)/shard_map/ppermute | solution.py:1083
  488.9 36.1 %mixed_backward.6 = (bf16[3,1024,768]{2,1,0:T(8,128)(2,1)}, bf16[1024,768]{1,0:T(8,128)(2,1)}, f32[2,768]{1,0:T(2,128)}) custom-call(s32[8]{0:T(128)S(1)} %copy-done.41, s32[8]{0:T(128)S(1)} %copy-done.43, s32[3]{0:T(128)S(1)} %copy-done.61, bf16[3,1024,768]{2,1,0:T(8,128)(2,1)} %get-tuple-element.418.qkv_hbm, f32[1024,128]{1,0:T(8,128)S(1)} %copy-done.23, ...), custom_call_target="tpu_custom_call" | custom-call | flops 38000001024 | bytes 1024 | tf_op jit(solution)/shard_map/mixed_backward/pallas_call | solution.py:999
  533.7 8.9 %attend_grads.4 = bf16[8,384,384]{2,1,0:T(8,128)(2,1)} custom-call(s32[3]{0:T(128)} %pad_add_fusion.2.sel_ref, bf16[1024,768]{1,0:T(8,128)(2,1)} %get-tuple-element.451.context_hbm.context_ref, bf16[1024,768]{1,0:T(8,128)(2,1)} %copy-done.13, bf16[1024,768]{1,0:T(8,128)(2,1)} %get-tuple-element.453.attn_late_ref, ...), custom_call_target="tpu_custom_call" | custom-call | flops 8000000000 | bytes 1024 | tf_op jit(solution)/shard_map/attend_grads/pallas_call | solution.py:570
  551.8 8.8 %attend_grads.5 = bf16[8,384,384]{2,1,0:T(8,128)(2,1)} custom-call(s32[3]{0:T(128)S(1)} %copy-done.62, bf16[1024,768]{1,0:T(8,128)(2,1)} %get-tuple-element.451.context_hbm.context_ref, bf16[1024,768]{1,0:T(8,128)(2,1)} %copy-done.13, bf16[1024,768]{1,0:T(8,128)(2,1)} %get-tuple-element.453.attn_late_ref, ...), custom_call_target="tpu_custom_call" | custom-call | flops 8000000000 | bytes 1024 | tf_op jit(solution)/shard_map/attend_grads/pallas_call | solution.py:570
  575.1 24.1 %refine_back.9 = (bf16[1024,768]{1,0:T(8,128)(2,1)}, bf16[1024,3072]{1,0:T(8,128)(2,1)}, bf16[1024,768]{1,0:T(8,128)(2,1)}, bf16[1024,768]{1,0:T(8,128)(2,1)}, f32[6,768]{1,0:T(8,128)}, /*index=5*/f32[1,3072]{1,0:T(1,128)}) custom-call(s32[3]{0:T(128)S(1)} %copy-done.62, bf16[1024,768]{1,0:T(8,128)(2,1)} %get-tuple-element.458.grad_ref, ...), custom_call_target="tpu_custom_call" | custom-call | flops 24000000000 | bytes 1024 | tf_op jit(solution)/shard_map/refine_back/pallas_call | solution.py:392
  603.3 13.3 %feed_grads.6 = bf16[8,768,384]{2,1,0:T(8,128)(2,1)} custom-call(s32[3]{0:T(128)} %pad_add_fusion.2.sel_ref, bf16[1024,768]{1,0:T(8,128)(2,1)S(1)} %copy-done.49, bf16[1024,3072]{1,0:T(8,128)(2,1)} %get-tuple-element.493.raised_late_ref, bf16[1024,3072]{1,0:T(8,128)(2,1)} %get-tuple-element.494.raised_ref, bf16[1024,3072]{1,0:T(8,128)(2,1)} %get-tuple-element.495.active_ref, ...), custom_call_target="tpu_custom_call" | custom-call | flops 12000000000 | bytes 1024 | tf_op jit(solution)/shard_map/feed_grads/pallas_call | solution.py:504
  622.8 13.2 %feed_grads.7 = bf16[8,768,384]{2,1,0:T(8,128)(2,1)} custom-call(s32[3]{0:T(128)S(1)} %copy-done.62, bf16[1024,768]{1,0:T(8,128)(2,1)S(1)} %copy-done.49, bf16[1024,3072]{1,0:T(8,128)(2,1)} %get-tuple-element.493.raised_late_ref, bf16[1024,3072]{1,0:T(8,128)(2,1)} %get-tuple-element.494.raised_ref, bf16[1024,3072]{1,0:T(8,128)(2,1)} %get-tuple-element.495.active_ref, ...), custom_call_target="tpu_custom_call" | custom-call | flops 12000000000 | bytes 1024 | tf_op jit(solution)/shard_map/feed_grads/pallas_call | solution.py:504
  642.2 35.4 %mixed_backward.7 = (bf16[3,1024,768]{2,1,0:T(8,128)(2,1)}, bf16[1024,768]{1,0:T(8,128)(2,1)}, f32[2,768]{1,0:T(2,128)}) custom-call(s32[8]{0:T(128)S(1)} %copy-done.41, s32[8]{0:T(128)S(1)} %copy-done.44, s32[3]{0:T(128)S(1)} %copy-done.62, bf16[3,1024,768]{2,1,0:T(8,128)(2,1)} %get-tuple-element.466.qkv_hbm, f32[1024,128]{1,0:T(8,128)S(1)} %copy-done.24, ...), custom_call_target="tpu_custom_call" | custom-call | flops 38000001024 | bytes 1024 | tf_op jit(solution)/shard_map/mixed_backward/pallas_call | solution.py:999
  681.6 12.7 %collective-permute-done.28 = bf16[4,768,384]{2,1,0:T(8,128)(2,1)} collective-permute-done((bf16[4,768,384]{2,1,0:T(8,128)(2,1)S(1)}, bf16[4,768,384]{2,1,0:T(8,128)(2,1)}, u32[]{:S(2)}, u32[]{:S(2)}) %collective-permute-start.28) | collective-permute-done | bytes 2359328 | tf_op jit(solution)/shard_map/ppermute | solution.py:1083
  698.4 8.4 %attend_grads.6 = bf16[8,384,384]{2,1,0:T(8,128)(2,1)} custom-call(s32[3]{0:T(128)} %pad_add_fusion.2.sel_ref, bf16[1024,768]{1,0:T(8,128)(2,1)} %get-tuple-element.534.context_hbm.context_ref, bf16[1024,768]{1,0:T(8,128)(2,1)S(1)} %copy-done.10, bf16[1024,768]{1,0:T(8,128)(2,1)} %get-tuple-element.536.attn_late_ref, ...), custom_call_target="tpu_custom_call" | custom-call | flops 8000000000 | bytes 1024 | tf_op jit(solution)/shard_map/attend_grads/pallas_call | solution.py:570
  720.9 8.6 %attend_grads.7 = bf16[8,384,384]{2,1,0:T(8,128)(2,1)} custom-call(s32[3]{0:T(128)S(1)} %copy-done.62, bf16[1024,768]{1,0:T(8,128)(2,1)} %get-tuple-element.534.context_hbm.context_ref, bf16[1024,768]{1,0:T(8,128)(2,1)S(1)} %copy-done.10, bf16[1024,768]{1,0:T(8,128)(2,1)} %get-tuple-element.536.attn_late_ref, ...), custom_call_target="tpu_custom_call" | custom-call | flops 8000000000 | bytes 1024 | tf_op jit(solution)/shard_map/attend_grads/pallas_call | solution.py:570
  731.5 6.6 collective-permute-done.32
  761.5 10.7 %collective-permute-done.35 = bf16[256,768]{1,0:T(8,128)(2,1)} collective-permute-done((bf16[256,768]{1,0:T(8,128)(2,1)}, bf16[256,768]{1,0:T(8,128)(2,1)}, u32[]{:S(2)}, u32[]{:S(2)}) %collective-permute-start.35) | collective-permute-done | bytes 393248 | tf_op jit(solution)/shard_map/ppermute | solution.py:1047
  777.3 11.5 %collective-permute-start.43 = (bf16[432,384]{1,0:T(8,128)(2,1)S(1)}, bf16[432,384]{1,0:T(8,128)(2,1)S(1)}, u32[]{:S(2)}, u32[]{:S(2)}) collective-permute-start(bf16[432,384]{1,0:T(8,128)(2,1)S(1)} %get-tuple-element.618), channel_id=1, source_target_pairs={{0,4},{1,5},{2,6},{3,7},{8,12},{9,13},{10,14},{11,15},{16,20},{17,... | collective-permute-start | bytes 995336 | tf_op jit(solution)/shard_map/ppermute | solution.py:1111
  803.1 6.5 collective-permute-done.45
  (338 shorter events, 201.4 us)
Async XLA Ops:
  9.7 21.6 %collective-permute-start.5 = (bf16[768,3072]{1,0:T(8,128)(2,1)}, bf16[768,3072]{1,0:T(8,128)(2,1)}, u32[]{:S(2)}, u32[]{:S(2)}) collective-permute-start(bf16[768,3072]{1,0:T(8,128)(2,1)} %bitcast.318), channel_id=1, source_target_pairs={{0,8},{8,0},{16,24},{24,16},{1,9},{9,1},{17,25},{25,17},{2,10},{10... | collective-permute-start | bytes 14155784 | tf_op jit(solution)/shard_map/ppermute | solution.py:1047
  9.7 21.7 %collective-permute-start.6 = (bf16[3072,768]{1,0:T(8,128)(2,1)}, bf16[3072,768]{1,0:T(8,128)(2,1)}, u32[]{:S(2)}, u32[]{:S(2)}) collective-permute-start(bf16[3072,768]{1,0:T(8,128)(2,1)} %bitcast.326), channel_id=1, source_target_pairs={{0,8},{8,0},{16,24},{24,16},{1,9},{9,1},{17,25},{25,17},{2,10},{10... | collective-permute-start | bytes 14155784 | tf_op jit(solution)/shard_map/ppermute | solution.py:1047
  13.1 18.2 %collective-permute-start.3 = (bf16[768,2304]{1,0:T(8,128)(2,1)}, bf16[768,2304]{1,0:T(8,128)(2,1)S(1)}, u32[]{:S(2)}, u32[]{:S(2)}) collective-permute-start(bf16[768,2304]{1,0:T(8,128)(2,1)} %bitcast.334), channel_id=1, source_target_pairs={{0,8},{8,0},{16,24},{24,16},{1,9},{9,1},{17,25},{25,17},{2,10},{10... | collective-permute-start | bytes 10616840 | tf_op jit(solution)/shard_map/ppermute | solution.py:1047
  13.3 18.0 %collective-permute-start.4 = (bf16[768,768]{1,0:T(8,128)(2,1)}, bf16[768,768]{1,0:T(8,128)(2,1)S(1)}, u32[]{:S(2)}, u32[]{:S(2)}) collective-permute-start(bf16[768,768]{1,0:T(8,128)(2,1)} %bitcast.340), channel_id=1, source_target_pairs={{0,8},{8,0},{16,24},{24,16},{1,9},{9,1},{17,25},{25,17},{2,10},{10... | collective-permute-start | bytes 3538952 | tf_op jit(solution)/shard_map/ppermute | solution.py:1047
  80.1 40.0 %collective-permute-start.8 = (bf16[32,1792]{1,0:T(8,128)(2,1)S(1)}, bf16[32,1792]{1,0:T(8,128)(2,1)S(1)}, u32[]{:S(2)}, u32[]{:S(2)}) collective-permute-start(bf16[32,1792]{1,0:T(8,128)(2,1)S(1)} %get-tuple-element.396), channel_id=1, source_target_pairs={{0,24},{8,16},{1,25},{9,17},{2,26},{10,18},{3,27},{11,19},{4,28},{... | collective-permute-start | bytes 344072 | tf_op jit(solution)/shard_map/ppermute | solution.py:1047
  81.4 38.6 %collective-permute-start.10 = (bf16[32,1792]{1,0:T(8,128)(2,1)S(1)}, bf16[32,1792]{1,0:T(8,128)(2,1)S(1)}, u32[]{:S(2)}, u32[]{:S(2)}) collective-permute-start(bf16[32,1792]{1,0:T(8,128)(2,1)S(1)} %get-tuple-element.396), channel_id=1, source_target_pairs={{16,24},{24,16},{17,25},{25,17},{18,26},{26,18},{19,27},{27,19},{2... | collective-permute-start | bytes 344072 | tf_op jit(solution)/shard_map/ppermute | solution.py:1047
  83.3 36.8 %collective-permute-start.9 = (bf16[32,1792]{1,0:T(8,128)(2,1)S(1)}, bf16[32,1792]{1,0:T(8,128)(2,1)S(1)}, u32[]{:S(2)}, u32[]{:S(2)}) collective-permute-start(bf16[32,1792]{1,0:T(8,128)(2,1)S(1)} %get-tuple-element.397), channel_id=1, source_target_pairs={{0,16},{8,24},{1,17},{9,25},{2,18},{10,26},{3,19},{11,27},{4,20},{... | collective-permute-start | bytes 344072 | tf_op jit(solution)/shard_map/ppermute | solution.py:1047
  121.2 19.6 %collective-permute-start.11 = (bf16[512,768]{1,0:T(8,128)(2,1)S(1)}, bf16[512,768]{1,0:T(8,128)(2,1)S(1)}, u32[]{:S(2)}, u32[]{:S(2)}) collective-permute-start(bf16[512,768]{1,0:T(8,128)(2,1)S(1)} %copy-done.17), channel_id=1, source_target_pairs={{0,16},{8,24},{1,17},{9,25},{2,18},{10,26},{3,19},{11,27},{4,20},{... | collective-permute-start | bytes 2359304 | tf_op jit(solution)/shard_map/ppermute | solution.py:1047
  141.5 20.2 %collective-permute-start.12 = (bf16[512,768]{1,0:T(8,128)(2,1)}, bf16[512,768]{1,0:T(8,128)(2,1)}, u32[]{:S(2)}, u32[]{:S(2)}) collective-permute-start(bf16[512,768]{1,0:T(8,128)(2,1)} %get-tuple-element.400), channel_id=1, source_target_pairs={{0,16},{8,24},{1,17},{9,25},{2,18},{10,26},{3,19},{11,27},{4,20},{... | collective-permute-start | bytes 2359304 | tf_op jit(solution)/shard_map/ppermute | solution.py:1047
  389.8 26.7 %collective-permute-start.13 = (bf16[512,768]{1,0:T(8,128)(2,1)}, bf16[512,768]{1,0:T(8,128)(2,1)}, u32[]{:S(2)}, u32[]{:S(2)}) collective-permute-start(bf16[512,768]{1,0:T(8,128)(2,1)} %get-tuple-element.627), channel_id=1, source_target_pairs={{16,0},{24,8},{17,1},{25,9},{18,2},{26,10},{19,3},{27,11},{20,4},{... | collective-permute-start | bytes 2359304 | tf_op jit(solution)/shard_map/ppermute | solution.py:1047
  445.4 20.5 %collective-permute-start.15 = (bf16[8,768,384]{2,1,0:T(8,128)(2,1)}, bf16[8,768,384]{2,1,0:T(8,128)(2,1)}, u32[]{:S(2)}, u32[]{:S(2)}) collective-permute-start(bf16[8,768,384]{2,1,0:T(8,128)(2,1)} %feed_grads.5), channel_id=1, source_target_pairs={{0,8},{8,0},{16,24},{24,16},{1,9},{9,1},{17,25},{25,17},{2,10},{10... | collective-permute-start | bytes 14155784 | tf_op jit(solution)/shard_map/ppermute | solution.py:1047
  447.0 78.0 %collective-permute-start.16 = (bf16[32,1024]{1,0:T(8,128)(2,1)}, bf16[32,1024]{1,0:T(8,128)(2,1)S(1)}, u32[]{:S(2)}, u32[]{:S(2)}) collective-permute-start(bf16[32,1024]{1,0:T(8,128)(2,1)} %get-tuple-element.640), channel_id=1, source_target_pairs={{16,0},{24,8},{17,1},{25,9},{18,2},{26,10},{19,3},{27,11},{20,4},{... | collective-permute-start | bytes 196616 | tf_op jit(solution)/shard_map/ppermute | solution.py:1047
  450.8 74.2 %collective-permute-start.17 = (bf16[32,1024]{1,0:T(8,128)(2,1)}, bf16[32,1024]{1,0:T(8,128)(2,1)S(1)}, u32[]{:S(2)}, u32[]{:S(2)}) collective-permute-start(bf16[32,1024]{1,0:T(8,128)(2,1)} %get-tuple-element.639), channel_id=1, source_target_pairs={{16,8},{24,0},{17,9},{25,1},{18,10},{26,2},{19,11},{27,3},{20,12},... | collective-permute-start | bytes 196616 | tf_op jit(solution)/shard_map/ppermute | solution.py:1047
  452.5 72.6 %collective-permute-start.18 = (bf16[32,1024]{1,0:T(8,128)(2,1)}, bf16[32,1024]{1,0:T(8,128)(2,1)}, u32[]{:S(2)}, u32[]{:S(2)}) collective-permute-start(bf16[32,1024]{1,0:T(8,128)(2,1)} %get-tuple-element.638), channel_id=1, source_target_pairs={{0,8},{8,0},{16,24},{24,16},{1,9},{9,1},{17,25},{25,17},{2,10},{10... | collective-permute-start | bytes 196616 | tf_op jit(solution)/shard_map/ppermute | solution.py:1047
  472.5 55.5 %collective-permute-start.19 = (bf16[4,576,384]{2,1,0:T(8,128)(2,1)}, bf16[4,576,384]{2,1,0:T(8,128)(2,1)S(1)}, u32[]{:S(2)}, u32[]{:S(2)}) collective-permute-start(bf16[4,576,384]{2,1,0:T(8,128)(2,1)} %fusion.1), channel_id=1, source_target_pairs={{0,1},{1,0},{2,3},{3,2},{4,5},{5,4},{6,7},{7,6},{8,9},{9,8},{10,11... | collective-permute-start | bytes 5308424 | tf_op jit(solution)/shard_map/ppermute | solution.py:1083
  547.0 20.1 %collective-permute-start.22 = (bf16[8,384,384]{2,1,0:T(8,128)(2,1)}, bf16[8,384,384]{2,1,0:T(8,128)(2,1)}, u32[]{:S(2)}, u32[]{:S(2)}) collective-permute-start(bf16[8,384,384]{2,1,0:T(8,128)(2,1)} %attend_grads.4), channel_id=1, source_target_pairs={{0,8},{8,0},{16,24},{24,16},{1,9},{9,1},{17,25},{25,17},{2,10},{10... | collective-permute-start | bytes 7077896 | tf_op jit(solution)/shard_map/ppermute | solution.py:1047
  570.0 29.2 %collective-permute-start.24 = (bf16[4,384,384]{2,1,0:T(8,128)(2,1)}, bf16[4,384,384]{2,1,0:T(8,128)(2,1)}, u32[]{:S(2)}, u32[]{:S(2)}) collective-permute-start(bf16[4,384,384]{2,1,0:T(8,128)(2,1)} %fusion.3), channel_id=1, source_target_pairs={{0,1},{1,0},{2,3},{3,2},{4,5},{5,4},{6,7},{7,6},{8,9},{9,8},{10,11... | collective-permute-start | bytes 3538952 | tf_op jit(solution)/shard_map/ppermute | solution.py:1083
  574.9 24.3 %collective-permute-start.23 = (bf16[768,384]{1,0:T(8,128)(2,1)}, bf16[768,384]{1,0:T(8,128)(2,1)}, u32[]{:S(2)}, u32[]{:S(2)}) collective-permute-start(bf16[768,384]{1,0:T(8,128)(2,1)} %fusion.16), channel_id=1, source_target_pairs={{0,2},{1,3},{2,4},{3,5},{4,6},{5,7},{6,0},{7,1},{8,10},{9,11},{10,... | collective-permute-start | bytes 1769480 | tf_op jit(solution)/shard_map/ppermute | solution.py:1101
  616.6 19.4 %collective-permute-start.26 = (bf16[8,768,384]{2,1,0:T(8,128)(2,1)}, bf16[8,768,384]{2,1,0:T(8,128)(2,1)}, u32[]{:S(2)}, u32[]{:S(2)}) collective-permute-start(bf16[8,768,384]{2,1,0:T(8,128)(2,1)} %feed_grads.6), channel_id=1, source_target_pairs={{0,8},{8,0},{16,24},{24,16},{1,9},{9,1},{17,25},{25,17},{2,10},{10... | collective-permute-start | bytes 14155784 | tf_op jit(solution)/shard_map/ppermute | solution.py:1047
  638.1 43.5 %collective-permute-start.29 = (bf16[384,384]{1,0:T(8,128)(2,1)}, bf16[384,384]{1,0:T(8,128)(2,1)}, u32[]{:S(2)}, u32[]{:S(2)}) collective-permute-start(bf16[384,384]{1,0:T(8,128)(2,1)} %fusion.37), channel_id=1, source_target_pairs={{0,2},{1,3},{2,4},{3,5},{4,6},{5,7},{6,0},{7,1},{8,10},{9,11},{10,... | collective-permute-start | bytes 884744 | tf_op jit(solution)/shard_map/ppermute | solution.py:1101
  641.8 52.5 %collective-permute-start.28 = (bf16[4,768,384]{2,1,0:T(8,128)(2,1)S(1)}, bf16[4,768,384]{2,1,0:T(8,128)(2,1)}, u32[]{:S(2)}, u32[]{:S(2)}) collective-permute-start(bf16[4,768,384]{2,1,0:T(8,128)(2,1)S(1)} %fusion), channel_id=1, source_target_pairs={{0,1},{1,0},{2,3},{3,2},{4,5},{5,4},{6,7},{7,6},{8,9},{9,8},{10,11... | collective-permute-start | bytes 7077896 | tf_op jit(solution)/shard_map/ppermute | solution.py:1083
  710.3 27.8 %collective-permute-start.39 = (bf16[8,432,384]{2,1,0:T(8,128)(2,1)}, bf16[8,432,384]{2,1,0:T(8,128)(2,1)}, u32[]{:S(2)}, u32[]{:S(2)}) collective-permute-start(bf16[8,432,384]{2,1,0:T(8,128)(2,1)} %pad_maximum_fusion), channel_id=1, source_target_pairs={{0,8},{8,0},{16,24},{24,16},{1,9},{9,1},{17,25},{25,17},{2,10},{10... | collective-permute-start | bytes 7962632 | tf_op jit(solution)/shard_map/ppermute | solution.py:1047
  713.7 17.8 %collective-permute-start.31 = (bf16[256,768]{1,0:T(8,128)(2,1)}, bf16[256,768]{1,0:T(8,128)(2,1)}, u32[]{:S(2)}, u32[]{:S(2)}) collective-permute-start(bf16[256,768]{1,0:T(8,128)(2,1)} %dynamic-slice_bitcast_fusion.6), channel_id=1, source_target_pairs={{0,8},{8,0},{16,24},{24,16},{1,9},{9,1},{17,25},{25,17},{2,10},{10... | collective-permute-start | bytes 1179656 | tf_op jit(solution)/shard_map/ppermute | solution.py:1047
  740.7 31.5 %collective-permute-start.40 = (bf16[4,432,384]{2,1,0:T(8,128)(2,1)}, bf16[4,432,384]{2,1,0:T(8,128)(2,1)}, u32[]{:S(2)}, u32[]{:S(2)}) collective-permute-start(bf16[4,432,384]{2,1,0:T(8,128)(2,1)} %fusion.2), channel_id=1, source_target_pairs={{0,1},{1,0},{2,3},{3,2},{4,5},{5,4},{6,7},{7,6},{8,9},{9,8},{10,11... | collective-permute-start | bytes 3981320 | tf_op jit(solution)/shard_map/ppermute | solution.py:1083
  748.7 23.5 %collective-permute-start.38 = (bf16[768,384]{1,0:T(8,128)(2,1)}, bf16[768,384]{1,0:T(8,128)(2,1)}, u32[]{:S(2)}, u32[]{:S(2)}) collective-permute-start(bf16[768,384]{1,0:T(8,128)(2,1)} %fusion.7), channel_id=1, source_target_pairs={{0,2},{1,3},{2,4},{3,5},{4,6},{5,7},{6,0},{7,1},{8,10},{9,11},{10,... | collective-permute-start | bytes 1769480 | tf_op jit(solution)/shard_map/ppermute | solution.py:1101
  751.9 20.3 %collective-permute-start.35 = (bf16[256,768]{1,0:T(8,128)(2,1)}, bf16[256,768]{1,0:T(8,128)(2,1)}, u32[]{:S(2)}, u32[]{:S(2)}) collective-permute-start(bf16[256,768]{1,0:T(8,128)(2,1)} %get-tuple-element.624), channel_id=1, source_target_pairs={{0,24},{8,16},{1,25},{9,17},{2,26},{10,18},{3,27},{11,19},{4,28},{... | collective-permute-start | bytes 1179656 | tf_op jit(solution)/shard_map/ppermute | solution.py:1047
  775.3 18.1 %collective-permute-start.41 = (bf16[432,384]{1,0:T(8,128)(2,1)S(1)}, bf16[432,384]{1,0:T(8,128)(2,1)S(1)}, u32[]{:S(2)}, u32[]{:S(2)}) collective-permute-start(bf16[432,384]{1,0:T(8,128)(2,1)S(1)} %get-tuple-element.614), channel_id=1, source_target_pairs={{0,6},{1,7},{8,14},{9,15},{16,22},{17,23},{24,30},{25,31}} | collective-permute-start | bytes 995336 | tf_op jit(solution)/shard_map/ppermute | solution.py:1111
  776.6 24.1 %collective-permute-start.42 = (bf16[432,384]{1,0:T(8,128)(2,1)S(1)}, bf16[432,384]{1,0:T(8,128)(2,1)S(1)}, u32[]{:S(2)}, u32[]{:S(2)}) collective-permute-start(bf16[432,384]{1,0:T(8,128)(2,1)S(1)} %get-tuple-element.619), channel_id=1, source_target_pairs={{6,0},{7,1},{14,8},{15,9},{22,16},{23,17},{30,24},{31,25}} | collective-permute-start | bytes 995336 | tf_op jit(solution)/shard_map/ppermute | solution.py:1111
  777.3 25.7 %collective-permute-start.43 = (bf16[432,384]{1,0:T(8,128)(2,1)S(1)}, bf16[432,384]{1,0:T(8,128)(2,1)S(1)}, u32[]{:S(2)}, u32[]{:S(2)}) collective-permute-start(bf16[432,384]{1,0:T(8,128)(2,1)S(1)} %get-tuple-element.618), channel_id=1, source_target_pairs={{0,4},{1,5},{2,6},{3,7},{8,12},{9,13},{10,14},{11,15},{16,20},{17,... | collective-permute-start | bytes 995336 | tf_op jit(solution)/shard_map/ppermute | solution.py:1111
  790.1 19.5 %collective-permute-start.45 = (bf16[432,384]{1,0:T(8,128)(2,1)S(1)}, bf16[432,384]{1,0:T(8,128)(2,1)S(1)}, u32[]{:S(2)}, u32[]{:S(2)}) collective-permute-start(bf16[432,384]{1,0:T(8,128)(2,1)S(1)} %get-tuple-element.616), channel_id=1, source_target_pairs={{0,2},{1,3},{2,4},{3,5},{4,6},{5,7},{8,10},{9,11},{10,12},{11,13},... | collective-permute-start | bytes 995336 | tf_op jit(solution)/shard_map/ppermute | solution.py:1111
  793.4 22.0 %collective-permute-start.46 = (bf16[432,384]{1,0:T(8,128)(2,1)S(1)}, bf16[432,384]{1,0:T(8,128)(2,1)S(1)}, u32[]{:S(2)}, u32[]{:S(2)}) collective-permute-start(bf16[432,384]{1,0:T(8,128)(2,1)S(1)} %get-tuple-element.615), channel_id=1, source_target_pairs={{2,0},{3,1},{4,2},{5,3},{6,4},{7,5},{10,8},{11,9},{12,10},{13,11},... | collective-permute-start | bytes 995336 | tf_op jit(solution)/shard_map/ppermute | solution.py:1111
  800.7 22.9 %collective-permute-start.48 = (bf16[768,384]{1,0:T(8,128)(2,1)}, bf16[768,384]{1,0:T(8,128)(2,1)}, u32[]{:S(2)}, u32[]{:S(2)}) collective-permute-start(bf16[768,384]{1,0:T(8,128)(2,1)} %fusion.5), channel_id=1, source_target_pairs={{8,0},{24,16},{9,1},{25,17},{10,2},{26,18},{11,3},{27,19},{12,4},{... | collective-permute-start | bytes 1769480 | tf_op jit(solution)/shard_map/ppermute | solution.py:1047
  (81 other events, 2186.6 us)

commit v3 on v2

--- a/solution.py
+++ b/solution.py
@@ -181,7 +181,7 @@
 
 def attend_backward(
     begin_ref, count_ref, qkv, key_code_ref, query_code_ref, context, logsum_ref, grad, sums_ref,
-    key_scr, query_scr, given_scr, down_scr, grad_key_scr, grad_value_scr,
+    key_scr, query_scr, given_scr, down_scr, grad_key_scr, grad_value_scr, ready,
 ):
     length = qkv.shape[1]
     pairs = qkv.shape[2] // PAIR
@@ -190,6 +190,7 @@
     cols = [slice(p * PAIR, (p + 1) * PAIR) for p in every]
     for p in every:
         key_scr[p] = qkv[1, :, cols[p]].T
+    ready()
 
     def one_query_block(i, _):
         query_at = pl.multiple_of(i * QB, QB)
@@ -325,8 +326,8 @@
     grad_low_ref, grad_raised_ref, grad_attn_ref, grad_context_ref, sums_ref, up_sums_ref,
     w_out, w_up, w_down, sems,
 ):
-    pairs = [(out_own_ref, out_other_ref), (up_own_ref, up_other_ref), (down_own_ref, down_other_ref)]
-    weights = Held(sel_ref, layer, pairs, [w_out, w_up, w_down], sems)
+    pairs = [(down_own_ref, down_other_ref), (up_own_ref, up_other_ref), (out_own_ref, out_other_ref)]
+    weights = Held(sel_ref, layer, pairs, [w_down, w_up, w_out], sems)
     weights.start()
     rows, width = grad_ref.shape
     ff_width = slope_ref.shape[1]
@@ -351,7 +352,7 @@
     add(2, grad * hat)
     add(4, grad)
     add(5, low.astype(F32))
-    weights.wait(2)
+    weights.wait(0)
     weights.wait(1)
     total = joined
     parts = [slice(f, f + FB) for f in range(0, ff_width, FB)]
@@ -368,7 +369,7 @@
     summed = normalized_pull(total * vector("gain1"), hat, scale1_ref[:, :1])
     attn = summed.astype(BF)
     grad_attn_ref[...] = attn
-    weights.wait(0)
+    weights.wait(2)
     grad_context_ref[...] = dot_nt(attn, w_out[...]).astype(BF)
     add(1, total * hat)
     add(3, total)
@@ -953,12 +954,17 @@
     grad_key_scr[...] = jnp.zeros_like(grad_key_scr)
     grad_value_scr[...] = jnp.zeros_like(grad_value_scr)
     sums_ref[...] = jnp.zeros_like(sums_ref)
-    for load in loads:
-        load.wait()
+    loads[0].wait()
+
+    def ready():
+        loads[1].wait()
+        loads[2].wait()
+
     attend_backward(
         begin_ref, count_ref, qkv, key_code_ref, query_code_ref, context, logsum_ref, grad,
-        sums_ref, key_scr, query_scr, given_scr, down_scr, grad_key_scr, grad_value_scr,
-    )
+        sums_ref, key_scr, query_scr, given_scr, down_scr, grad_key_scr, grad_value_scr, ready,
+    )
+    loads[3].wait()
     store = pltpu.make_async_copy(qkv, mixed_hbm, mixed_sems.at[0])
     store.start()
     weights.wait(0)
@@ -1077,8 +1083,13 @@
         self.crossed_rows = last
         others = []
         for term in self.terms:
-            cut = term.reshape(4, 2, *term.shape[1:])[:, :, first:last]
-            others.append(pick_row(cut, 1 - self.x, 1))
+            cols = term.shape[2]
+            cut = lax.dynamic_slice(
+                term.reshape(4, 2, *term.shape[1:]),
+                (0, 1 - self.x, first, 0),
+                (4, 1, last - first, cols),
+            )
+            others.append(cut[:, 0])
         pairs = [(n, n ^ 1) for n in range(8)]
         self.crossed += (lax.ppermute(plus(*others), "dp", pairs),)
 
@@ -1298,7 +1309,6 @@
     args, theirs, extras = tie_sums((args, theirs, extras), feed_even)
     arrived = swap_cores(theirs)
     feed_even.ring()
-    attend_odd.ring()
     quarters = grad.reshape(4, quarter, width)
     near_grad = swap_cores(pick_row(quarters, 1 - core))
     mine = jnp.concatenate([attend_grads(sel_mine, *args), extras.astype(BF)], axis=1)
@@ -1306,15 +1316,15 @@
     attend_even = RowSum(mine, arrived, attend_blocks)
     attend_even.cross()
     feed_even.ring()
-    attend_odd = attend_odd.result()
-    sent_odd = [send(part, routes_odd) for part in (feed_odd, attend_odd)]
+    attend_odd.ring()
     straight_grad = send(pick_row(quarters, 2 + core), [(0, 2), (1, 3)])
     crossed_grad = send(pick_row(quarters, 3 - core), [(0, 3), (1, 2)])
-    straight_grad, crossed_grad, sent_odd = tie_sums(
-        (straight_grad, crossed_grad, sent_odd), feed_even, attend_even
+    straight_grad, crossed_grad = tie_sums(
+        (straight_grad, crossed_grad), feed_even, attend_even, attend_odd
     )
     attend_even.direct()
-    feed_even = feed_even.result()
+    feed_even, attend_odd = feed_even.result(), attend_odd.result()
+    sent_odd = [send(part, routes_odd) for part in (feed_odd, attend_odd)]
     if shards == SHARDS:
         tail = attend_even.result()
         attend_even, extras = tail[: 4 * share], tail[4 * share :].astype(F32)

time: 838 us -> 826 us (0.986)
  starting transfers between devices: 89.3 us -> 125 us
  Pallas kernels: 534 us -> 507 us
  local copies, waits for them, and re-layouts: 36.5 us -> 27.1 us
    ppermute x30, starting transfers between devices: 40.6 us -> 62.1 us  [send(): return lax.ppermute(value, 'section', routes)]
    ppermute x9, starting transfers between devices: 9.88 us -> 30.2 us  [ring(): lax.ppermute(passing, 'dp', [(n, (n + 2) % 8) for n in range(8)])]
    pallas_call x4, Pallas kernels: 142 us -> 124 us  [mixed_backward(): pl.pallas_call(partial(mixed_backward_kernel, layer), name='mixed_backwar...]
    ppermute x30, waiting for transfers between devices: 53.1 us -> 36.4 us  [send(): return lax.ppermute(value, 'section', routes)]
    ppermute x5, waiting for transfers between devices: 20.1 us -> 30.1 us  [cross(): self.crossed += (lax.ppermute(plus(*others), 'dp', pairs),)]
  transfers between devices with their start and end apart: 50 -> 50, of which waited for: 16 -> 16; matrix products, arithmetic and copies ran while one was open for 8% -> 8% of each run, Pallas kernels for 29% -> 28%
where the time goes in v3:
time: 826 us; the launch traced here: 823 us
  Pallas kernels  507 us (61%)
  starting transfers between devices  125 us (15%)
  waiting for transfers between devices  95.2 us (12%)
  other arithmetic  65.7 us (8%)
  local copies, waits for them, and re-layouts  27.1 us (3%)
    pallas_call x4, Pallas kernels, layer_forward(): pl.pallas_call(partial(forward_kernel, layer), name='layer_forward', grid...  168 us
    pallas_call x4, Pallas kernels, mixed_backward(): pl.pallas_call(partial(mixed_backward_kernel, layer), name='mixed_backwar...  124 us
    pallas_call x5, Pallas kernels, refine_back(): pl.pallas_call(partial(refine_back_second_kernel if begun else refine_bac...  102 us
    ppermute x30, starting transfers between devices, send(): return lax.ppermute(value, 'section', routes)  62.1 us
    pallas_call x4, Pallas kernels, feed_grads(): pl.pallas_call(feed_grads_kernel, name='feed_grads', grid_spec=pltpu.Pref...  52.9 us
    convert_element_type x19, other arithmetic, plus(): return sum((value.astype(F32) for value in values)).astype(BF)  38.1 us
    ppermute x30, waiting for transfers between devices, send(): return lax.ppermute(value, 'section', routes)  36.4 us
    pallas_call x4, Pallas kernels, attend_grads(): pl.pallas_call(attend_grads_kernel, name='attend_grads', grid_spec=pltpu....  35.6 us
  transfers between devices with their start and end apart: 50, of which 16 were waited for; matrix products, arithmetic and copies ran while one was open for 8% of the time, Pallas kernels for 28%

profile of v3, /device:TPU:13, one launch (start us, length us, event | category | flops | bytes accessed | tf_op | source)
XLA Modules:
  0.0 823.5 jit_solution(4314548707268483913)
XLA Ops:
  17.4 8.3 %collective-permute-done.2 = bf16[256,768]{1,0:T(8,128)(2,1)S(1)} collective-permute-done((bf16[256,768]{1,0:T(8,128)(2,1)S(1)}, bf16[256,768]{1,0:T(8,128)(2,1)S(1)}, u32[]{:S(2)}, u32[]{:S(2)}) %collective-permute-start.2) | collective-permute-done | bytes 393248 | tf_op jit(solution)/shard_map/ppermute | solution.py:1053
  33.5 44.6 %layer_forward.6 = (bf16[3,1024,768]{2,1,0:T(8,128)(2,1)}, bf16[1024,768]{1,0:T(8,128)(2,1)}, f32[48,256]{1,0:T(8,128)}, bf16[1024,768]{1,0:T(8,128)(2,1)S(1)}, ...) custom-call(s32[8]{0:T(128)S(1)} %get-tuple-element.614.begin_ref, ...), custom_call_target="tpu_custom_call" | custom-call | flops 48000000000 | bytes 1024 | tf_op jit(solution)/shard_map/layer_forward/pallas_call | solution.py:868
  85.0 33.4 %layer_forward.7 = (bf16[3,1024,768]{2,1,0:T(8,128)(2,1)}, bf16[1024,768]{1,0:T(8,128)(2,1)}, f32[48,256]{1,0:T(8,128)}, bf16[512,768]{1,0:T(8,128)(2,1)}, bf16[...) custom-call(s32[8]{0:T(128)S(1)} %get-tuple-element.614.begin_ref, ...), custom_call_target="tpu_custom_call" | custom-call | flops 48000000000 | bytes 1024 | tf_op jit(solution)/shard_map/layer_forward/pallas_call | solution.py:868
  120.9 18.2 %refine_rest.1 = (bf16[512,768]{1,0:T(8,128)(2,1)}, bf16[1024,768]{1,0:T(8,128)(2,1)}, f32[1024,128]{1,0:T(8,128)S(1)}, f32[1024,128]{1,0:T(8,128)}, bf16[1024,3...) custom-call(s32[3]{0:T(128)S(1)} %pad_add_fusion.sel_ref.refs_0_, ...), custom_call_target="tpu_custom_call", output_to_operand_aliasing={{1}: (10, {}), {2}: (11, {}), {3}: (12, {}), {4}: (13, {}),... | custom-call | flops 14000000000 | bytes 1024 | tf_op jit(solution)/shard_map/refine_rest/pallas_call | solution.py:733
  143.6 15.3 %collective-permute-done.12 = bf16[512,768]{1,0:T(8,128)(2,1)} collective-permute-done((bf16[512,768]{1,0:T(8,128)(2,1)}, bf16[512,768]{1,0:T(8,128)(2,1)}, u32[]{:S(2)}, u32[]{:S(2)}) %collective-permute-start.12) | collective-permute-done | bytes 786464 | tf_op jit(solution)/shard_map/ppermute | solution.py:1053
  160.4 208.0 %conditional.1 = (bf16[1024,768]{1,0:T(8,128)(2,1)}, bf16[3,1024,768]{2,1,0:T(8,128)(2,1)}, bf16[1024,768]{1,0:T(8,128)(2,1)}, f32[48,256]{1,0:T(8,128)}, bf16[1...) conditional(s32[]{:T(128)} %convert_element_type.504, ...), branch_computations={%region_3.4_spmd, %region_4.5_spmd} | conditional | flops 226000011264 | bytes 47062592 | solution.py:1232
  160.6 45.8 %layer_forward.4 = (bf16[3,1024,768]{2,1,0:T(8,128)(2,1)}, bf16[1024,768]{1,0:T(8,128)(2,1)}, f32[48,256]{1,0:T(8,128)S(1)}, bf16[1024,768]{1,0:T(8,128)(2,1)S(1...) custom-call(s32[8]{0:T(128)S(1)} %get-tuple-element.96.begin_ref, ...), custom_call_target="tpu_custom_call" | custom-call | flops 48000000000 | bytes 1024 | tf_op jit(solution)/shard_map/cond/branch_1_fun/layer_forward/pallas_call | solution.py:868
  206.5 44.7 %layer_forward.5 = (bf16[3,1024,768]{2,1,0:T(8,128)(2,1)}, bf16[1024,768]{1,0:T(8,128)(2,1)}, f32[48,256]{1,0:T(8,128)S(1)}, bf16[1024,768]{1,0:T(8,128)(2,1)S(1...) custom-call(s32[8]{0:T(128)S(1)} %get-tuple-element.96.begin_ref, ...), custom_call_target="tpu_custom_call" | custom-call | flops 48000000000 | bytes 1024 | tf_op jit(solution)/shard_map/cond/branch_1_fun/layer_forward/pallas_call | solution.py:868
  255.1 23.9 %refine_back.5 = (bf16[1024,768]{1,0:T(8,128)(2,1)}, bf16[1024,3072]{1,0:T(8,128)(2,1)}, bf16[1024,768]{1,0:T(8,128)(2,1)}, bf16[1024,768]{1,0:T(8,128)(2,1)}, f32[6,768]{1,0:T(8,128)}, /*index=5*/f32[1,3072]{1,0:T(1,128)}) custom-call(s32[3]{0:T(128)S(1)} %get-tuple-element.98.sel_ref, bf16[1024,768]{1,0:T(8,128)(2,1)} %get-tuple-element.131.grad_ref, ...), custom_call_target="tpu_custom_call" | custom-call | flops 24000000000 | bytes 1024 | tf_op jit(solution)/shard_map/cond/branch_1_fun/refine_back/pallas_call | solution.py:393
  279.0 30.9 %mixed_backward.4 = (bf16[3,1024,768]{2,1,0:T(8,128)(2,1)}, bf16[1024,768]{1,0:T(8,128)(2,1)}, f32[2,768]{1,0:T(2,128)}) custom-call(s32[8]{0:T(128)S(1)} %get-tuple-element.96.begin_ref, s32[8]{0:T(128)S(1)} %get-tuple-element.97.count_ref, s32[3]{0:T(128)S(1)} %get-tuple-element.98.sel_ref, bf16[3,1024,768]{2,1,0:T(8,128)(2,1)} %get-tuple-element.711.qkv_hbm, ...), custom_call_target="tpu_custom_call" | custom-call | flops 38000001024 | bytes 1024 | tf_op jit(solution)/shard_map/cond/branch_1_fun/mixed_backward/pallas_call | solution.py:1005
  310.0 23.8 %refine_back.6 = (bf16[1024,768]{1,0:T(8,128)(2,1)}, bf16[1024,3072]{1,0:T(8,128)(2,1)}, bf16[1024,768]{1,0:T(8,128)(2,1)}, bf16[1024,768]{1,0:T(8,128)(2,1)}, f32[6,768]{1,0:T(8,128)}, /*index=5*/f32[1,3072]{1,0:T(1,128)}) custom-call(s32[3]{0:T(128)S(1)} %get-tuple-element.98.sel_ref, bf16[1024,768]{1,0:T(8,128)(2,1)} %get-tuple-element.134.grad_ref, ...), custom_call_target="tpu_custom_call" | custom-call | flops 24000000000 | bytes 1024 | tf_op jit(solution)/shard_map/cond/branch_1_fun/refine_back/pallas_call | solution.py:393
  333.8 30.8 %mixed_backward.5 = (bf16[3,1024,768]{2,1,0:T(8,128)(2,1)}, bf16[1024,768]{1,0:T(8,128)(2,1)}, f32[2,768]{1,0:T(2,128)}) custom-call(s32[8]{0:T(128)S(1)} %get-tuple-element.96.begin_ref, s32[8]{0:T(128)S(1)} %get-tuple-element.97.count_ref, s32[3]{0:T(128)S(1)} %get-tuple-element.98.sel_ref, bf16[3,1024,768]{2,1,0:T(8,128)(2,1)} %get-tuple-element.701.qkv_hbm, ...), custom_call_target="tpu_custom_call" | custom-call | flops 38000001024 | bytes 1024 | tf_op jit(solution)/shard_map/cond/branch_1_fun/mixed_backward/pallas_call | solution.py:1005
  382.5 15.2 %refine_back.7 = (bf16[1024,768]{1,0:T(8,128)(2,1)}, bf16[1024,3072]{1,0:T(8,128)(2,1)}, bf16[1024,768]{1,0:T(8,128)(2,1)}, bf16[1024,768]{1,0:T(8,128)(2,1)}, f32[6,768]{1,0:T(8,128)}, /*index=5*/f32[1,3072]{1,0:T(1,128)}) custom-call(s32[3]{0:T(128)S(1)} %pad_add_fusion.sel_ref.refs_0_, bf16[512,768]{1,0:T(8,128)(2,1)} %copy-done.44, ...), custom_call_target="tpu_custom_call" | custom-call | flops 24000000000 | bytes 1024 | tf_op jit(solution)/shard_map/refine_back/pallas_call | solution.py:393
  397.7 15.1 %refine_back.8 = (bf16[1024,768]{1,0:T(8,128)(2,1)}, bf16[1024,3072]{1,0:T(8,128)(2,1)}, bf16[1024,768]{1,0:T(8,128)(2,1)}, bf16[1024,768]{1,0:T(8,128)(2,1)}, f32[6,768]{1,0:T(8,128)}, /*index=5*/f32[1,3072]{1,0:T(1,128)}) custom-call(s32[3]{0:T(128)S(1)} %pad_add_fusion.sel_ref.refs_0_, ...), custom_call_target="tpu_custom_call", output_to_operand_aliasing={{0}: (14, {}), {1}: (15, {}), {2}: (16, {}), {3}: (17, {})} | custom-call | flops 24000000000 | bytes 1024 | tf_op jit(solution)/shard_map/refine_back/pallas_call | solution.py:393
  412.8 13.5 %feed_grads.5 = bf16[8,768,384]{2,1,0:T(8,128)(2,1)} custom-call(s32[3]{0:T(128)} %pad_add_fusion.2.sel_ref, bf16[1024,768]{1,0:T(8,128)(2,1)} %get-tuple-element.409.hidden_ref.refs_2_, bf16[1024,3072]{1,0:T(8,128)(2,1)} %get-tuple-element.423.raised_late_ref, bf16[1024,3072]{1,0:T(8,128)(2,1)} %get-tuple-element.424.raised_ref, ...), custom_call_target="tpu_custom_call" | custom-call | flops 12000000000 | bytes 1024 | tf_op jit(solution)/shard_map/feed_grads/pallas_call | solution.py:505
  426.3 17.3 %collective-permute-start.15 = (bf16[8,768,384]{2,1,0:T(8,128)(2,1)}, bf16[8,768,384]{2,1,0:T(8,128)(2,1)}, u32[]{:S(2)}, u32[]{:S(2)}) collective-permute-start(bf16[8,768,384]{2,1,0:T(8,128)(2,1)} %feed_grads.5), channel_id=1, source_target_pairs={{0,8},{8,0},{16,24},{24,16},{1,9},{9,1},{17,25},{25,17},{2,10},{10... | collective-permute-start | bytes 14155784 | tf_op jit(solution)/shard_map/ppermute | solution.py:1053
  451.2 12.9 %feed_grads.4 = bf16[8,768,384]{2,1,0:T(8,128)(2,1)} custom-call(s32[3]{0:T(128)S(1)} %copy-done.56, bf16[1024,768]{1,0:T(8,128)(2,1)S(1)} %copy-done.46, bf16[1024,3072]{1,0:T(8,128)(2,1)} %get-tuple-element.423.raised_late_ref, bf16[1024,3072]{1,0:T(8,128)(2,1)} %get-tuple-element.424.raised_ref, bf16[1024,3072]{1,0:T(8,128)(2,1)} %get-tuple-element.425.active_ref, ...), custom_call_target="tpu_custom_call" | custom-call | flops 12000000000 | bytes 1024 | tf_op jit(solution)/shard_map/feed_grads/pallas_call | solution.py:505
  468.0 12.4 %collective-permute-start.19 = (bf16[4,576,384]{2,1,0:T(8,128)(2,1)}, bf16[4,576,384]{2,1,0:T(8,128)(2,1)S(1)}, u32[]{:S(2)}, u32[]{:S(2)}) collective-permute-start(bf16[4,576,384]{2,1,0:T(8,128)(2,1)} %fusion.1), channel_id=1, source_target_pairs={{0,1},{1,0},{2,3},{3,2},{4,5},{5,4},{6,7},{7,6},{8,9},{9,8},{10,11... | collective-permute-start | bytes 5308424 | tf_op jit(solution)/shard_map/ppermute | solution.py:1094
  480.5 31.7 %mixed_backward.6 = (bf16[3,1024,768]{2,1,0:T(8,128)(2,1)}, bf16[1024,768]{1,0:T(8,128)(2,1)}, f32[2,768]{1,0:T(2,128)}) custom-call(s32[8]{0:T(128)S(1)} %copy-done.37, s32[8]{0:T(128)S(1)} %copy-done.39, s32[3]{0:T(128)S(1)} %copy-done.57, bf16[3,1024,768]{2,1,0:T(8,128)(2,1)} %get-tuple-element.420.qkv_hbm, f32[1024,128]{1,0:T(8,128)S(1)} %copy-done.21, ...), custom_call_target="tpu_custom_call" | custom-call | flops 38000001024 | bytes 1024 | tf_op jit(solution)/shard_map/mixed_backward/pallas_call | solution.py:1005
  512.2 7.3 collective-permute-done.19
  523.5 9.3 %attend_grads.4 = bf16[8,384,384]{2,1,0:T(8,128)(2,1)} custom-call(s32[3]{0:T(128)} %pad_add_fusion.2.sel_ref, bf16[1024,768]{1,0:T(8,128)(2,1)} %get-tuple-element.453.context_hbm.context_ref, bf16[1024,768]{1,0:T(8,128)(2,1)} %copy-done.12, bf16[1024,768]{1,0:T(8,128)(2,1)} %get-tuple-element.455.attn_late_ref, ...), custom_call_target="tpu_custom_call" | custom-call | flops 8000000000 | bytes 1024 | tf_op jit(solution)/shard_map/attend_grads/pallas_call | solution.py:571
  541.8 20.3 %collective-permute-start.21 = (bf16[768,384]{1,0:T(8,128)(2,1)}, bf16[768,384]{1,0:T(8,128)(2,1)}, u32[]{:S(2)}, u32[]{:S(2)}) collective-permute-start(bf16[768,384]{1,0:T(8,128)(2,1)} %fusion.17), channel_id=1, source_target_pairs={{0,2},{1,3},{2,4},{3,5},{4,6},{5,7},{6,0},{7,1},{8,10},{9,11},{10,... | collective-permute-start | bytes 1769480 | tf_op jit(solution)/shard_map/ppermute | solution.py:1112
  562.1 8.7 %attend_grads.5 = bf16[8,384,384]{2,1,0:T(8,128)(2,1)} custom-call(s32[3]{0:T(128)S(1)} %copy-done.58, bf16[1024,768]{1,0:T(8,128)(2,1)} %get-tuple-element.453.context_hbm.context_ref, bf16[1024,768]{1,0:T(8,128)(2,1)} %copy-done.12, bf16[1024,768]{1,0:T(8,128)(2,1)} %get-tuple-element.455.attn_late_ref, ...), custom_call_target="tpu_custom_call" | custom-call | flops 8000000000 | bytes 1024 | tf_op jit(solution)/shard_map/attend_grads/pallas_call | solution.py:571
  584.8 23.8 %refine_back.9 = (bf16[1024,768]{1,0:T(8,128)(2,1)}, bf16[1024,3072]{1,0:T(8,128)(2,1)}, bf16[1024,768]{1,0:T(8,128)(2,1)}, bf16[1024,768]{1,0:T(8,128)(2,1)}, f32[6,768]{1,0:T(8,128)}, /*index=5*/f32[1,3072]{1,0:T(1,128)}) custom-call(s32[3]{0:T(128)S(1)} %copy-done.58, bf16[1024,768]{1,0:T(8,128)(2,1)} %get-tuple-element.460.grad_ref, ...), custom_call_target="tpu_custom_call" | custom-call | flops 24000000000 | bytes 1024 | tf_op jit(solution)/shard_map/refine_back/pallas_call | solution.py:393
  611.9 13.4 %feed_grads.6 = bf16[8,768,384]{2,1,0:T(8,128)(2,1)} custom-call(s32[3]{0:T(128)} %pad_add_fusion.2.sel_ref, bf16[1024,768]{1,0:T(8,128)(2,1)S(1)} %copy-done.45, bf16[1024,3072]{1,0:T(8,128)(2,1)} %get-tuple-element.495.raised_late_ref, bf16[1024,3072]{1,0:T(8,128)(2,1)} %get-tuple-element.496.raised_ref, bf16[1024,3072]{1,0:T(8,128)(2,1)} %get-tuple-element.497.active_ref, ...), custom_call_target="tpu_custom_call" | custom-call | flops 12000000000 | bytes 1024 | tf_op jit(solution)/shard_map/feed_grads/pallas_call | solution.py:505
  630.2 13.0 %feed_grads.7 = bf16[8,768,384]{2,1,0:T(8,128)(2,1)} custom-call(s32[3]{0:T(128)S(1)} %copy-done.58, bf16[1024,768]{1,0:T(8,128)(2,1)S(1)} %copy-done.45, bf16[1024,3072]{1,0:T(8,128)(2,1)} %get-tuple-element.495.raised_late_ref, bf16[1024,3072]{1,0:T(8,128)(2,1)} %get-tuple-element.496.raised_ref, bf16[1024,3072]{1,0:T(8,128)(2,1)} %get-tuple-element.497.active_ref, ...), custom_call_target="tpu_custom_call" | custom-call | flops 12000000000 | bytes 1024 | tf_op jit(solution)/shard_map/feed_grads/pallas_call | solution.py:505
  649.6 30.9 %mixed_backward.7 = (bf16[3,1024,768]{2,1,0:T(8,128)(2,1)}, bf16[1024,768]{1,0:T(8,128)(2,1)}, f32[2,768]{1,0:T(2,128)}) custom-call(s32[8]{0:T(128)S(1)} %copy-done.37, s32[8]{0:T(128)S(1)} %copy-done.40, s32[3]{0:T(128)S(1)} %copy-done.58, bf16[3,1024,768]{2,1,0:T(8,128)(2,1)} %get-tuple-element.468.qkv_hbm, f32[1024,128]{1,0:T(8,128)S(1)} %copy-done.22, ...), custom_call_target="tpu_custom_call" | custom-call | flops 38000001024 | bytes 1024 | tf_op jit(solution)/shard_map/mixed_backward/pallas_call | solution.py:1005
  684.6 17.0 %collective-permute-done.28 = bf16[4,768,384]{2,1,0:T(8,128)(2,1)} collective-permute-done((bf16[4,768,384]{2,1,0:T(8,128)(2,1)S(1)}, bf16[4,768,384]{2,1,0:T(8,128)(2,1)}, u32[]{:S(2)}, u32[]{:S(2)}) %collective-permute-start.28) | collective-permute-done | bytes 2359328 | tf_op jit(solution)/shard_map/ppermute | solution.py:1094
  705.4 8.4 %attend_grads.6 = bf16[8,384,384]{2,1,0:T(8,128)(2,1)} custom-call(s32[3]{0:T(128)} %pad_add_fusion.2.sel_ref, bf16[1024,768]{1,0:T(8,128)(2,1)} %get-tuple-element.536.context_hbm.context_ref, bf16[1024,768]{1,0:T(8,128)(2,1)S(1)} %copy-done.9, bf16[1024,768]{1,0:T(8,128)(2,1)} %get-tuple-element.538.attn_late_ref, ...), custom_call_target="tpu_custom_call" | custom-call | flops 8000000000 | bytes 1024 | tf_op jit(solution)/shard_map/attend_grads/pallas_call | solution.py:571
  725.8 9.0 %attend_grads.7 = bf16[8,384,384]{2,1,0:T(8,128)(2,1)} custom-call(s32[3]{0:T(128)S(1)} %copy-done.58, bf16[1024,768]{1,0:T(8,128)(2,1)} %get-tuple-element.536.context_hbm.context_ref, bf16[1024,768]{1,0:T(8,128)(2,1)} %get-tuple-element.537.x_ref, bf16[1024,768]{1,0:T(8,128)(2,1)} %get-tuple-element.538.attn_late_ref, ...), custom_call_target="tpu_custom_call" | custom-call | flops 8000000000 | bytes 1024 | tf_op jit(solution)/shard_map/attend_grads/pallas_call | solution.py:571
  753.7 12.7 %collective-permute-done.38 = bf16[384,384]{1,0:T(8,128)(2,1)S(1)} collective-permute-done((bf16[384,384]{1,0:T(8,128)(2,1)S(1)}, bf16[384,384]{1,0:T(8,128)(2,1)S(1)}, u32[]{:S(2)}, u32[]{:S(2)}) %collective-permute-start.38) | collective-permute-done | bytes 294944 | tf_op jit(solution)/shard_map/ppermute | solution.py:1112
  771.5 9.8 %collective-permute-start.42 = (bf16[432,384]{1,0:T(8,128)(2,1)S(1)}, bf16[432,384]{1,0:T(8,128)(2,1)S(1)}, u32[]{:S(2)}, u32[]{:S(2)}) collective-permute-start(bf16[432,384]{1,0:T(8,128)(2,1)S(1)} %get-tuple-element.622), channel_id=1, source_target_pairs={{0,4},{1,5},{2,6},{3,7},{8,12},{9,13},{10,14},{11,15},{16,20},{17,... | collective-permute-start | bytes 995336 | tf_op jit(solution)/shard_map/ppermute | solution.py:1122
  (326 shorter events, 198.7 us)
Async XLA Ops:
  9.7 21.6 %collective-permute-start.5 = (bf16[768,3072]{1,0:T(8,128)(2,1)}, bf16[768,3072]{1,0:T(8,128)(2,1)}, u32[]{:S(2)}, u32[]{:S(2)}) collective-permute-start(bf16[768,3072]{1,0:T(8,128)(2,1)} %bitcast.321), channel_id=1, source_target_pairs={{0,8},{8,0},{16,24},{24,16},{1,9},{9,1},{17,25},{25,17},{2,10},{10... | collective-permute-start | bytes 14155784 | tf_op jit(solution)/shard_map/ppermute | solution.py:1053
  9.7 21.7 %collective-permute-start.6 = (bf16[3072,768]{1,0:T(8,128)(2,1)}, bf16[3072,768]{1,0:T(8,128)(2,1)}, u32[]{:S(2)}, u32[]{:S(2)}) collective-permute-start(bf16[3072,768]{1,0:T(8,128)(2,1)} %bitcast.329), channel_id=1, source_target_pairs={{0,8},{8,0},{16,24},{24,16},{1,9},{9,1},{17,25},{25,17},{2,10},{10... | collective-permute-start | bytes 14155784 | tf_op jit(solution)/shard_map/ppermute | solution.py:1053
  78.1 40.4 %collective-permute-start.8 = (bf16[32,1792]{1,0:T(8,128)(2,1)S(1)}, bf16[32,1792]{1,0:T(8,128)(2,1)S(1)}, u32[]{:S(2)}, u32[]{:S(2)}) collective-permute-start(bf16[32,1792]{1,0:T(8,128)(2,1)S(1)} %get-tuple-element.398), channel_id=1, source_target_pairs={{0,24},{8,16},{1,25},{9,17},{2,26},{10,18},{3,27},{11,19},{4,28},{... | collective-permute-start | bytes 344072 | tf_op jit(solution)/shard_map/ppermute | solution.py:1053
  79.4 39.1 %collective-permute-start.10 = (bf16[32,1792]{1,0:T(8,128)(2,1)S(1)}, bf16[32,1792]{1,0:T(8,128)(2,1)S(1)}, u32[]{:S(2)}, u32[]{:S(2)}) collective-permute-start(bf16[32,1792]{1,0:T(8,128)(2,1)S(1)} %get-tuple-element.398), channel_id=1, source_target_pairs={{16,24},{24,16},{17,25},{25,17},{18,26},{26,18},{19,27},{27,19},{2... | collective-permute-start | bytes 344072 | tf_op jit(solution)/shard_map/ppermute | solution.py:1053
  83.7 34.8 %collective-permute-start.9 = (bf16[32,1792]{1,0:T(8,128)(2,1)S(1)}, bf16[32,1792]{1,0:T(8,128)(2,1)S(1)}, u32[]{:S(2)}, u32[]{:S(2)}) collective-permute-start(bf16[32,1792]{1,0:T(8,128)(2,1)S(1)} %get-tuple-element.399), channel_id=1, source_target_pairs={{0,16},{8,24},{1,17},{9,25},{2,18},{10,26},{3,19},{11,27},{4,20},{... | collective-permute-start | bytes 344072 | tf_op jit(solution)/shard_map/ppermute | solution.py:1053
  119.6 19.5 %collective-permute-start.11 = (bf16[512,768]{1,0:T(8,128)(2,1)S(1)}, bf16[512,768]{1,0:T(8,128)(2,1)S(1)}, u32[]{:S(2)}, u32[]{:S(2)}) collective-permute-start(bf16[512,768]{1,0:T(8,128)(2,1)S(1)} %copy-done.16), channel_id=1, source_target_pairs={{0,16},{8,24},{1,17},{9,25},{2,18},{10,26},{3,19},{11,27},{4,20},{... | collective-permute-start | bytes 2359304 | tf_op jit(solution)/shard_map/ppermute | solution.py:1053
  139.9 19.0 %collective-permute-start.12 = (bf16[512,768]{1,0:T(8,128)(2,1)}, bf16[512,768]{1,0:T(8,128)(2,1)}, u32[]{:S(2)}, u32[]{:S(2)}) collective-permute-start(bf16[512,768]{1,0:T(8,128)(2,1)} %get-tuple-element.402), channel_id=1, source_target_pairs={{0,16},{8,24},{1,17},{9,25},{2,18},{10,26},{3,19},{11,27},{4,20},{... | collective-permute-start | bytes 2359304 | tf_op jit(solution)/shard_map/ppermute | solution.py:1053
  373.3 24.3 %collective-permute-start.13 = (bf16[512,768]{1,0:T(8,128)(2,1)}, bf16[512,768]{1,0:T(8,128)(2,1)}, u32[]{:S(2)}, u32[]{:S(2)}) collective-permute-start(bf16[512,768]{1,0:T(8,128)(2,1)} %get-tuple-element.631), channel_id=1, source_target_pairs={{16,0},{24,8},{17,1},{25,9},{18,2},{26,10},{19,3},{27,11},{20,4},{... | collective-permute-start | bytes 2359304 | tf_op jit(solution)/shard_map/ppermute | solution.py:1053
  426.3 37.8 %collective-permute-start.15 = (bf16[8,768,384]{2,1,0:T(8,128)(2,1)}, bf16[8,768,384]{2,1,0:T(8,128)(2,1)}, u32[]{:S(2)}, u32[]{:S(2)}) collective-permute-start(bf16[8,768,384]{2,1,0:T(8,128)(2,1)} %feed_grads.5), channel_id=1, source_target_pairs={{0,8},{8,0},{16,24},{24,16},{1,9},{9,1},{17,25},{25,17},{2,10},{10... | collective-permute-start | bytes 14155784 | tf_op jit(solution)/shard_map/ppermute | solution.py:1053
  445.2 67.0 %collective-permute-start.16 = (bf16[32,1024]{1,0:T(8,128)(2,1)}, bf16[32,1024]{1,0:T(8,128)(2,1)S(1)}, u32[]{:S(2)}, u32[]{:S(2)}) collective-permute-start(bf16[32,1024]{1,0:T(8,128)(2,1)} %get-tuple-element.644), channel_id=1, source_target_pairs={{16,0},{24,8},{17,1},{25,9},{18,2},{26,10},{19,3},{27,11},{20,4},{... | collective-permute-start | bytes 196616 | tf_op jit(solution)/shard_map/ppermute | solution.py:1053
  449.4 62.7 %collective-permute-start.17 = (bf16[32,1024]{1,0:T(8,128)(2,1)}, bf16[32,1024]{1,0:T(8,128)(2,1)S(1)}, u32[]{:S(2)}, u32[]{:S(2)}) collective-permute-start(bf16[32,1024]{1,0:T(8,128)(2,1)} %get-tuple-element.643), channel_id=1, source_target_pairs={{16,8},{24,0},{17,9},{25,1},{18,10},{26,2},{19,11},{27,3},{20,12},... | collective-permute-start | bytes 196616 | tf_op jit(solution)/shard_map/ppermute | solution.py:1053
  450.7 61.5 %collective-permute-start.18 = (bf16[32,1024]{1,0:T(8,128)(2,1)}, bf16[32,1024]{1,0:T(8,128)(2,1)}, u32[]{:S(2)}, u32[]{:S(2)}) collective-permute-start(bf16[32,1024]{1,0:T(8,128)(2,1)} %get-tuple-element.642), channel_id=1, source_target_pairs={{0,8},{8,0},{16,24},{24,16},{1,9},{9,1},{17,25},{25,17},{2,10},{10... | collective-permute-start | bytes 196616 | tf_op jit(solution)/shard_map/ppermute | solution.py:1053
  468.0 51.5 %collective-permute-start.19 = (bf16[4,576,384]{2,1,0:T(8,128)(2,1)}, bf16[4,576,384]{2,1,0:T(8,128)(2,1)S(1)}, u32[]{:S(2)}, u32[]{:S(2)}) collective-permute-start(bf16[4,576,384]{2,1,0:T(8,128)(2,1)} %fusion.1), channel_id=1, source_target_pairs={{0,1},{1,0},{2,3},{3,2},{4,5},{5,4},{6,7},{7,6},{8,9},{9,8},{10,11... | collective-permute-start | bytes 5308424 | tf_op jit(solution)/shard_map/ppermute | solution.py:1094
  536.9 37.7 %collective-permute-start.22 = (bf16[8,384,384]{2,1,0:T(8,128)(2,1)}, bf16[8,384,384]{2,1,0:T(8,128)(2,1)}, u32[]{:S(2)}, u32[]{:S(2)}) collective-permute-start(bf16[8,384,384]{2,1,0:T(8,128)(2,1)} %attend_grads.4), channel_id=1, source_target_pairs={{0,8},{8,0},{16,24},{24,16},{1,9},{9,1},{17,25},{25,17},{2,10},{10... | collective-permute-start | bytes 7077896 | tf_op jit(solution)/shard_map/ppermute | solution.py:1053
  541.8 32.8 %collective-permute-start.21 = (bf16[768,384]{1,0:T(8,128)(2,1)}, bf16[768,384]{1,0:T(8,128)(2,1)}, u32[]{:S(2)}, u32[]{:S(2)}) collective-permute-start(bf16[768,384]{1,0:T(8,128)(2,1)} %fusion.17), channel_id=1, source_target_pairs={{0,2},{1,3},{2,4},{3,5},{4,6},{5,7},{6,0},{7,1},{8,10},{9,11},{10,... | collective-permute-start | bytes 1769480 | tf_op jit(solution)/shard_map/ppermute | solution.py:1112
  577.5 31.1 %collective-permute-start.24 = (bf16[4,384,384]{2,1,0:T(8,128)(2,1)}, bf16[4,384,384]{2,1,0:T(8,128)(2,1)}, u32[]{:S(2)}, u32[]{:S(2)}) collective-permute-start(bf16[4,384,384]{2,1,0:T(8,128)(2,1)} %fusion.3), channel_id=1, source_target_pairs={{0,1},{1,0},{2,3},{3,2},{4,5},{5,4},{6,7},{7,6},{8,9},{9,8},{10,11... | collective-permute-start | bytes 3538952 | tf_op jit(solution)/shard_map/ppermute | solution.py:1094
  582.6 26.0 %collective-permute-start.23 = (bf16[768,384]{1,0:T(8,128)(2,1)}, bf16[768,384]{1,0:T(8,128)(2,1)}, u32[]{:S(2)}, u32[]{:S(2)}) collective-permute-start(bf16[768,384]{1,0:T(8,128)(2,1)} %fusion.16), channel_id=1, source_target_pairs={{0,2},{1,3},{2,4},{3,5},{4,6},{5,7},{6,0},{7,1},{8,10},{9,11},{10,... | collective-permute-start | bytes 1769480 | tf_op jit(solution)/shard_map/ppermute | solution.py:1112
  645.2 39.3 %collective-permute-start.29 = (bf16[384,384]{1,0:T(8,128)(2,1)}, bf16[384,384]{1,0:T(8,128)(2,1)}, u32[]{:S(2)}, u32[]{:S(2)}) collective-permute-start(bf16[384,384]{1,0:T(8,128)(2,1)} %fusion.37), channel_id=1, source_target_pairs={{0,2},{1,3},{2,4},{3,5},{4,6},{5,7},{6,0},{7,1},{8,10},{9,11},{10,... | collective-permute-start | bytes 884744 | tf_op jit(solution)/shard_map/ppermute | solution.py:1112
  649.4 52.2 %collective-permute-start.28 = (bf16[4,768,384]{2,1,0:T(8,128)(2,1)S(1)}, bf16[4,768,384]{2,1,0:T(8,128)(2,1)}, u32[]{:S(2)}, u32[]{:S(2)}) collective-permute-start(bf16[4,768,384]{2,1,0:T(8,128)(2,1)S(1)} %fusion), channel_id=1, source_target_pairs={{0,1},{1,0},{2,3},{3,2},{4,5},{5,4},{6,7},{7,6},{8,9},{9,8},{10,11... | collective-permute-start | bytes 7077896 | tf_op jit(solution)/shard_map/ppermute | solution.py:1094
  717.3 22.0 %collective-permute-start.36 = (bf16[8,432,384]{2,1,0:T(8,128)(2,1)}, bf16[8,432,384]{2,1,0:T(8,128)(2,1)S(1)}, u32[]{:S(2)}, u32[]{:S(2)}) collective-permute-start(bf16[8,432,384]{2,1,0:T(8,128)(2,1)} %pad_maximum_fusion), channel_id=1, source_target_pairs={{0,8},{8,0},{16,24},{24,16},{1,9},{9,1},{17,25},{25,17},{2,10},{10... | collective-permute-start | bytes 7962632 | tf_op jit(solution)/shard_map/ppermute | solution.py:1053
  739.7 29.6 %collective-permute-start.37 = (bf16[4,432,384]{2,1,0:T(8,128)(2,1)S(1)}, bf16[4,432,384]{2,1,0:T(8,128)(2,1)S(1)}, u32[]{:S(2)}, u32[]{:S(2)}) collective-permute-start(bf16[4,432,384]{2,1,0:T(8,128)(2,1)S(1)} %fusion.2), channel_id=1, source_target_pairs={{0,1},{1,0},{2,3},{3,2},{4,5},{5,4},{6,7},{7,6},{8,9},{9,8},{10,11... | collective-permute-start | bytes 3981320 | tf_op jit(solution)/shard_map/ppermute | solution.py:1094
  744.8 22.7 %collective-permute-start.35 = (bf16[768,384]{1,0:T(8,128)(2,1)S(1)}, bf16[768,384]{1,0:T(8,128)(2,1)S(1)}, u32[]{:S(2)}, u32[]{:S(2)}) collective-permute-start(bf16[768,384]{1,0:T(8,128)(2,1)S(1)} %fusion.7), channel_id=1, source_target_pairs={{0,2},{1,3},{2,4},{3,5},{4,6},{5,7},{6,0},{7,1},{8,10},{9,11},{10,... | collective-permute-start | bytes 1769480 | tf_op jit(solution)/shard_map/ppermute | solution.py:1112
  746.1 20.3 %collective-permute-start.33 = (bf16[256,768]{1,0:T(8,128)(2,1)S(1)}, bf16[256,768]{1,0:T(8,128)(2,1)S(1)}, u32[]{:S(2)}, u32[]{:S(2)}) collective-permute-start(bf16[256,768]{1,0:T(8,128)(2,1)S(1)} %get-tuple-element.629), channel_id=1, source_target_pairs={{0,16},{8,24},{1,17},{9,25},{2,18},{10,26},{3,19},{11,27},{4,20},{... | collective-permute-start | bytes 1179656 | tf_op jit(solution)/shard_map/ppermute | solution.py:1053
  747.4 20.2 %collective-permute-start.34 = (bf16[256,768]{1,0:T(8,128)(2,1)S(1)}, bf16[256,768]{1,0:T(8,128)(2,1)S(1)}, u32[]{:S(2)}, u32[]{:S(2)}) collective-permute-start(bf16[256,768]{1,0:T(8,128)(2,1)S(1)} %get-tuple-element.628), channel_id=1, source_target_pairs={{0,24},{8,16},{1,25},{9,17},{2,26},{10,18},{3,27},{11,19},{4,28},{... | collective-permute-start | bytes 1179656 | tf_op jit(solution)/shard_map/ppermute | solution.py:1053
  770.8 22.3 %collective-permute-start.41 = (bf16[432,384]{1,0:T(8,128)(2,1)S(1)}, bf16[432,384]{1,0:T(8,128)(2,1)S(1)}, u32[]{:S(2)}, u32[]{:S(2)}) collective-permute-start(bf16[432,384]{1,0:T(8,128)(2,1)S(1)} %get-tuple-element.623), channel_id=1, source_target_pairs={{6,0},{7,1},{14,8},{15,9},{22,16},{23,17},{30,24},{31,25}} | collective-permute-start | bytes 995336 | tf_op jit(solution)/shard_map/ppermute | solution.py:1122
  771.5 25.3 %collective-permute-start.42 = (bf16[432,384]{1,0:T(8,128)(2,1)S(1)}, bf16[432,384]{1,0:T(8,128)(2,1)S(1)}, u32[]{:S(2)}, u32[]{:S(2)}) collective-permute-start(bf16[432,384]{1,0:T(8,128)(2,1)S(1)} %get-tuple-element.622), channel_id=1, source_target_pairs={{0,4},{1,5},{2,6},{3,7},{8,12},{9,13},{10,14},{11,15},{16,20},{17,... | collective-permute-start | bytes 995336 | tf_op jit(solution)/shard_map/ppermute | solution.py:1122
  781.3 19.0 %collective-permute-start.43 = (bf16[432,384]{1,0:T(8,128)(2,1)S(1)}, bf16[432,384]{1,0:T(8,128)(2,1)S(1)}, u32[]{:S(2)}, u32[]{:S(2)}) collective-permute-start(bf16[432,384]{1,0:T(8,128)(2,1)S(1)} %get-tuple-element.621), channel_id=1, source_target_pairs={{4,0},{5,1},{6,2},{7,3},{12,8},{13,9},{14,10},{15,11},{20,16},{21,... | collective-permute-start | bytes 995336 | tf_op jit(solution)/shard_map/ppermute | solution.py:1122
  782.6 21.3 %collective-permute-start.44 = (bf16[432,384]{1,0:T(8,128)(2,1)S(1)}, bf16[432,384]{1,0:T(8,128)(2,1)S(1)}, u32[]{:S(2)}, u32[]{:S(2)}) collective-permute-start(bf16[432,384]{1,0:T(8,128)(2,1)S(1)} %get-tuple-element.620), channel_id=1, source_target_pairs={{0,2},{1,3},{2,4},{3,5},{4,6},{5,7},{8,10},{9,11},{10,12},{11,13},... | collective-permute-start | bytes 995336 | tf_op jit(solution)/shard_map/ppermute | solution.py:1122
  785.9 23.0 %collective-permute-start.45 = (bf16[432,384]{1,0:T(8,128)(2,1)S(1)}, bf16[432,384]{1,0:T(8,128)(2,1)S(1)}, u32[]{:S(2)}, u32[]{:S(2)}) collective-permute-start(bf16[432,384]{1,0:T(8,128)(2,1)S(1)} %get-tuple-element.619), channel_id=1, source_target_pairs={{2,0},{3,1},{4,2},{5,3},{6,4},{7,5},{10,8},{11,9},{12,10},{13,11},... | collective-permute-start | bytes 995336 | tf_op jit(solution)/shard_map/ppermute | solution.py:1122
  793.1 23.1 %collective-permute-start.47 = (bf16[768,384]{1,0:T(8,128)(2,1)}, bf16[768,384]{1,0:T(8,128)(2,1)}, u32[]{:S(2)}, u32[]{:S(2)}) collective-permute-start(bf16[768,384]{1,0:T(8,128)(2,1)} %fusion.12), channel_id=1, source_target_pairs={{0,8},{16,24},{1,9},{17,25},{2,10},{18,26},{3,11},{19,27},{4,12},{... | collective-permute-start | bytes 1769480 | tf_op jit(solution)/shard_map/ppermute | solution.py:1053
  796.8 19.4 %collective-permute-start.48 = (bf16[768,384]{1,0:T(8,128)(2,1)}, bf16[768,384]{1,0:T(8,128)(2,1)}, u32[]{:S(2)}, u32[]{:S(2)}) collective-permute-start(bf16[768,384]{1,0:T(8,128)(2,1)} %fusion.5), channel_id=1, source_target_pairs={{8,0},{24,16},{9,1},{25,17},{10,2},{26,18},{11,3},{27,19},{12,4},{... | collective-permute-start | bytes 1769480 | tf_op jit(solution)/shard_map/ppermute | solution.py:1053
  800.3 19.7 %collective-permute-start.39 = (bf16[384,384]{1,0:T(8,128)(2,1)S(1)}, bf16[384,384]{1,0:T(8,128)(2,1)}, u32[]{:S(2)}, u32[]{:S(2)}) collective-permute-start(bf16[384,384]{1,0:T(8,128)(2,1)S(1)} %fusion.33), channel_id=1, source_target_pairs={{0,8},{16,24},{1,9},{17,25},{2,10},{18,26},{3,11},{19,27},{4,12},{... | collective-permute-start | bytes 884744 | tf_op jit(solution)/shard_map/ppermute | solution.py:1053
  (77 other events, 2181.6 us)

commit v4 on v3

--- a/solution.py
+++ b/solution.py
@@ -527,10 +527,26 @@
 
 
 def attend_grads_kernel(
-    sel_ref, context_ref, x_ref, attn_late_ref, attn_ref, mixed_late_ref, mixed_ref, out_ref
+    sel_ref, context_ref, x_ref, attn_late_ref, attn_ref, mixed_late_ref, mixed_ref, *rest
 ):
     step = pl.program_id(0)
     late = sel_ref[1] == 1
+    out_ref = rest[-1]
+    shards = out_ref.shape[0]
+    share = x_ref.shape[1] // shards
+
+    def store(n, rows, cols):
+        part = dot_tn(rows, cols).astype(BF).reshape(shards, share, cols.shape[1])
+        if len(rest) == 1:
+            out_ref[...] = part
+        else:
+            out_ref[:, n * share : (n + 1) * share, :] = part
+
+    if len(rest) > 1:
+
+        @pl.when(step == 0)
+        def _():
+            out_ref[:, 4 * share :, :] = rest[0][...].astype(BF)
 
     for wanted, attn_now, mixed_now in (
         (late, attn_late_ref, mixed_late_ref),
@@ -539,16 +555,16 @@
 
         @pl.when(wanted & (step == 0))
         def _():
-            part = dot_tn(context_ref[...], attn_now[...]).astype(BF)
-            out_ref[...] = part.reshape(out_ref.shape)
-
-        @pl.when(wanted & (step > 0))
-        def _():
-            part = dot_tn(x_ref[...], mixed_now[0]).astype(BF)
-            out_ref[...] = part.reshape(out_ref.shape)
-
-
-def attend_grads(sel, context, x, attn_late, attn, mixed_late, mixed):
+            store(0, context_ref[...], attn_now[...])
+
+        for n in (1, 2, 3):
+
+            @pl.when(wanted & (step == n))
+            def _():
+                store(n, x_ref[...], mixed_now[0])
+
+
+def attend_grads(sel, context, x, attn_late, attn, mixed_late, mixed, extras=None):
     length, width = x.shape
 
     def late_spec(wanted):
@@ -568,19 +584,25 @@
 
     whole = pl.BlockSpec((length, width), lambda n, _: (0, 0))
     share = width // SHARDS
+    more = () if extras is None else (extras,)
+    rows = 4 * share + sum(part.shape[1] for part in more)
+    out_spec = pl.BlockSpec((SHARDS, share, HALF), lambda n, _: (0, n, 0))
+    if more:
+        out_spec = pl.BlockSpec((SHARDS, rows, HALF), lambda n, _: (0, 0, 0))
     return pl.pallas_call(
         attend_grads_kernel,
         name="attend_grads",
         grid_spec=pltpu.PrefetchScalarGridSpec(
             num_scalar_prefetch=1,
             grid=(4,),
-            in_specs=[whole, whole, late_spec(1), late_spec(0), mixed_spec(1), mixed_spec(0)],
-            out_specs=pl.BlockSpec((SHARDS, share, HALF), lambda n, _: (0, n, 0)),
+            in_specs=[whole, whole, late_spec(1), late_spec(0), mixed_spec(1), mixed_spec(0)]
+            + [pl.BlockSpec(part.shape, lambda n, _: (0, 0, 0)) for part in more],
+            out_specs=out_spec,
         ),
-        out_shape=jax.ShapeDtypeStruct((SHARDS, 4 * share, HALF), BF),
+        out_shape=jax.ShapeDtypeStruct((SHARDS, rows, HALF), BF),
         compiler_params=PARAMS,
         cost_estimate=cost(8),
-    )(sel, context, x, attn_late, attn, mixed_late, mixed)
+    )(sel, context, x, attn_late, attn, mixed_late, mixed, *more)
 
 
 EXTRA_ROWS = 48
@@ -1303,15 +1325,14 @@
     feed_even.ring()
     routes_odd, routes_even = ((0, 1), (2, 3)), ((1, 0), (3, 2))
     feed_odd = feed_odd.result()
-    theirs = attend_grads(sel_theirs, *args)
     extras = pack_extras(sel_mine, grad_proj, late_sums_even, late_sums_odd, sums_even, sums_odd)
-    theirs = jnp.concatenate([theirs, extras.astype(BF)], axis=1)
+    theirs = attend_grads(sel_theirs, *args, extras)
     args, theirs, extras = tie_sums((args, theirs, extras), feed_even)
     arrived = swap_cores(theirs)
     feed_even.ring()
     quarters = grad.reshape(4, quarter, width)
     near_grad = swap_cores(pick_row(quarters, 1 - core))
-    mine = jnp.concatenate([attend_grads(sel_mine, *args), extras.astype(BF)], axis=1)
+    mine = attend_grads(sel_mine, *args, extras)
     mine, quarters, near_grad = tie_sums((mine, quarters, near_grad), feed_even, attend_odd)
     attend_even = RowSum(mine, arrived, attend_blocks)
     attend_even.cross()

time: 826 us -> 831 us (level)
  starting transfers between devices: 125 us -> 101 us
  waiting for transfers between devices: 95.2 us -> 114 us
  Pallas kernels: 507 us -> 519 us
    ppermute x30, starting transfers between devices: 62.1 us -> 42.8 us  [send(): return lax.ppermute(value, 'section', routes)]
    ppermute x30, waiting for transfers between devices: 36.4 us -> 47.8 us  [send(): return lax.ppermute(value, 'section', routes)]
    ppermute x5, starting transfers between devices: 15.2 us -> 4.77 us  [cross(): self.crossed += (lax.ppermute(plus(*others), 'dp', pairs),)]
  transfers between devices with their start and end apart: 50 -> 50, of which waited for: 16 -> 18; matrix products, arithmetic and copies ran while one was open for 8% -> 7% of each run, Pallas kernels for 28% -> 28%
where the time goes in v4:
time: 831 us; the launch traced here: 823 us
  Pallas kernels  519 us (62%)
  waiting for transfers between devices  114 us (14%)
  starting transfers between devices  101 us (12%)
  other arithmetic  59.6 us (7%)
  local copies, waits for them, and re-layouts  26 us (3%)
    pallas_call x4, Pallas kernels, layer_forward(): pl.pallas_call(partial(forward_kernel, layer), name='layer_forward', grid...  175 us
    pallas_call x4, Pallas kernels, mixed_backward(): pl.pallas_call(partial(mixed_backward_kernel, layer), name='mixed_backwar...  129 us
    pallas_call x5, Pallas kernels, refine_back(): pl.pallas_call(partial(refine_back_second_kernel if begun else refine_bac...  102 us
    pallas_call x4, Pallas kernels, feed_grads(): pl.pallas_call(feed_grads_kernel, name='feed_grads', grid_spec=pltpu.Pref...  52.8 us
    ppermute x30, waiting for transfers between devices, send(): return lax.ppermute(value, 'section', routes)  47.8 us
    ppermute x30, starting transfers between devices, send(): return lax.ppermute(value, 'section', routes)  42.8 us
    convert_element_type x19, other arithmetic, plus(): return sum((value.astype(F32) for value in values)).astype(BF)  39.3 us
    pallas_call x4, Pallas kernels, attend_grads(): pl.pallas_call(attend_grads_kernel, name='attend_grads', grid_spec=pltpu....  36.9 us
  transfers between devices with their start and end apart: 50, of which 18 were waited for; matrix products, arithmetic and copies ran while one was open for 7% of the time, Pallas kernels for 28%

profile of v4, /device:TPU:13, one launch (start us, length us, event | category | flops | bytes accessed | tf_op | source)
XLA Modules:
  0.0 822.9 jit_solution(5486597220514814880)
XLA Ops:
  17.4 8.3 %collective-permute-done.2 = bf16[256,768]{1,0:T(8,128)(2,1)S(1)} collective-permute-done((bf16[256,768]{1,0:T(8,128)(2,1)S(1)}, bf16[256,768]{1,0:T(8,128)(2,1)S(1)}, u32[]{:S(2)}, u32[]{:S(2)}) %collective-permute-start.2) | collective-permute-done | bytes 393248 | tf_op jit(solution)/shard_map/ppermute | solution.py:1075
  33.5 49.1 %layer_forward.6 = (bf16[3,1024,768]{2,1,0:T(8,128)(2,1)}, bf16[1024,768]{1,0:T(8,128)(2,1)}, f32[48,256]{1,0:T(8,128)}, bf16[1024,768]{1,0:T(8,128)(2,1)S(1)}, ...) custom-call(s32[8]{0:T(128)S(1)} %get-tuple-element.614.begin_ref, ...), custom_call_target="tpu_custom_call" | custom-call | flops 48000000000 | bytes 1024 | tf_op jit(solution)/shard_map/layer_forward/pallas_call | solution.py:890
  87.1 34.0 %layer_forward.7 = (bf16[3,1024,768]{2,1,0:T(8,128)(2,1)}, bf16[1024,768]{1,0:T(8,128)(2,1)}, f32[48,256]{1,0:T(8,128)}, bf16[512,768]{1,0:T(8,128)(2,1)}, bf16[...) custom-call(s32[8]{0:T(128)S(1)} %get-tuple-element.614.begin_ref, ...), custom_call_target="tpu_custom_call" | custom-call | flops 48000000000 | bytes 1024 | tf_op jit(solution)/shard_map/layer_forward/pallas_call | solution.py:890
  123.6 18.2 %refine_rest.1 = (bf16[512,768]{1,0:T(8,128)(2,1)}, bf16[1024,768]{1,0:T(8,128)(2,1)}, f32[1024,128]{1,0:T(8,128)S(1)}, f32[1024,128]{1,0:T(8,128)}, bf16[1024,3...) custom-call(s32[3]{0:T(128)S(1)} %pad_add_fusion.sel_ref.refs_0_, ...), custom_call_target="tpu_custom_call", output_to_operand_aliasing={{1}: (10, {}), {2}: (11, {}), {3}: (12, {}), {4}: (13, {}),... | custom-call | flops 14000000000 | bytes 1024 | tf_op jit(solution)/shard_map/refine_rest/pallas_call | solution.py:755
  147.1 16.9 %collective-permute-done.12 = bf16[512,768]{1,0:T(8,128)(2,1)} collective-permute-done((bf16[512,768]{1,0:T(8,128)(2,1)}, bf16[512,768]{1,0:T(8,128)(2,1)}, u32[]{:S(2)}, u32[]{:S(2)}) %collective-permute-start.12) | collective-permute-done | bytes 786464 | tf_op jit(solution)/shard_map/ppermute | solution.py:1075
  165.5 211.5 %conditional.1 = (bf16[1024,768]{1,0:T(8,128)(2,1)}, bf16[3,1024,768]{2,1,0:T(8,128)(2,1)}, bf16[1024,768]{1,0:T(8,128)(2,1)}, f32[48,256]{1,0:T(8,128)}, bf16[1...) conditional(s32[]{:T(128)} %convert_element_type.498, ...), branch_computations={%region_3.4_spmd, %region_4.5_spmd} | conditional | flops 226000011264 | bytes 47062592 | solution.py:1254
  165.7 46.4 %layer_forward.4 = (bf16[3,1024,768]{2,1,0:T(8,128)(2,1)}, bf16[1024,768]{1,0:T(8,128)(2,1)}, f32[48,256]{1,0:T(8,128)S(1)}, bf16[1024,768]{1,0:T(8,128)(2,1)S(1...) custom-call(s32[8]{0:T(128)S(1)} %get-tuple-element.96.begin_ref, ...), custom_call_target="tpu_custom_call" | custom-call | flops 48000000000 | bytes 1024 | tf_op jit(solution)/shard_map/cond/branch_1_fun/layer_forward/pallas_call | solution.py:890
  212.1 45.3 %layer_forward.5 = (bf16[3,1024,768]{2,1,0:T(8,128)(2,1)}, bf16[1024,768]{1,0:T(8,128)(2,1)}, f32[48,256]{1,0:T(8,128)S(1)}, bf16[1024,768]{1,0:T(8,128)(2,1)S(1...) custom-call(s32[8]{0:T(128)S(1)} %get-tuple-element.96.begin_ref, ...), custom_call_target="tpu_custom_call" | custom-call | flops 48000000000 | bytes 1024 | tf_op jit(solution)/shard_map/cond/branch_1_fun/layer_forward/pallas_call | solution.py:890
  261.4 23.9 %refine_back.5 = (bf16[1024,768]{1,0:T(8,128)(2,1)}, bf16[1024,3072]{1,0:T(8,128)(2,1)}, bf16[1024,768]{1,0:T(8,128)(2,1)}, bf16[1024,768]{1,0:T(8,128)(2,1)}, f32[6,768]{1,0:T(8,128)}, /*index=5*/f32[1,3072]{1,0:T(1,128)}) custom-call(s32[3]{0:T(128)S(1)} %get-tuple-element.98.sel_ref, bf16[1024,768]{1,0:T(8,128)(2,1)} %get-tuple-element.131.grad_ref, ...), custom_call_target="tpu_custom_call" | custom-call | flops 24000000000 | bytes 1024 | tf_op jit(solution)/shard_map/cond/branch_1_fun/refine_back/pallas_call | solution.py:393
  285.3 32.1 %mixed_backward.4 = (bf16[3,1024,768]{2,1,0:T(8,128)(2,1)}, bf16[1024,768]{1,0:T(8,128)(2,1)}, f32[2,768]{1,0:T(2,128)}) custom-call(s32[8]{0:T(128)S(1)} %get-tuple-element.96.begin_ref, s32[8]{0:T(128)S(1)} %get-tuple-element.97.count_ref, s32[3]{0:T(128)S(1)} %get-tuple-element.98.sel_ref, bf16[3,1024,768]{2,1,0:T(8,128)(2,1)} %get-tuple-element.711.qkv_hbm, ...), custom_call_target="tpu_custom_call" | custom-call | flops 38000001024 | bytes 1024 | tf_op jit(solution)/shard_map/cond/branch_1_fun/mixed_backward/pallas_call | solution.py:1027
  317.4 23.8 %refine_back.6 = (bf16[1024,768]{1,0:T(8,128)(2,1)}, bf16[1024,3072]{1,0:T(8,128)(2,1)}, bf16[1024,768]{1,0:T(8,128)(2,1)}, bf16[1024,768]{1,0:T(8,128)(2,1)}, f32[6,768]{1,0:T(8,128)}, /*index=5*/f32[1,3072]{1,0:T(1,128)}) custom-call(s32[3]{0:T(128)S(1)} %get-tuple-element.98.sel_ref, bf16[1024,768]{1,0:T(8,128)(2,1)} %get-tuple-element.134.grad_ref, ...), custom_call_target="tpu_custom_call" | custom-call | flops 24000000000 | bytes 1024 | tf_op jit(solution)/shard_map/cond/branch_1_fun/refine_back/pallas_call | solution.py:393
  341.2 32.0 %mixed_backward.5 = (bf16[3,1024,768]{2,1,0:T(8,128)(2,1)}, bf16[1024,768]{1,0:T(8,128)(2,1)}, f32[2,768]{1,0:T(2,128)}) custom-call(s32[8]{0:T(128)S(1)} %get-tuple-element.96.begin_ref, s32[8]{0:T(128)S(1)} %get-tuple-element.97.count_ref, s32[3]{0:T(128)S(1)} %get-tuple-element.98.sel_ref, bf16[3,1024,768]{2,1,0:T(8,128)(2,1)} %get-tuple-element.701.qkv_hbm, ...), custom_call_target="tpu_custom_call" | custom-call | flops 38000001024 | bytes 1024 | tf_op jit(solution)/shard_map/cond/branch_1_fun/mixed_backward/pallas_call | solution.py:1027
  384.1 14.6 %collective-permute-done.14.grad_ref = bf16[512,768]{1,0:T(8,128)(2,1)S(1)} collective-permute-done((bf16[512,768]{1,0:T(8,128)(2,1)S(1)}, bf16[512,768]{1,0:T(8,128)(2,1)S(1)}, u32[]{:S(2)}, u32[]{:S(2)}) %collective-permute-start.14) | collective-permute-done | bytes 786464 | tf_op jit(solution)/shard_map/ppermute | solution.py:1075
  399.5 15.2 %refine_back.7 = (bf16[1024,768]{1,0:T(8,128)(2,1)}, bf16[1024,3072]{1,0:T(8,128)(2,1)}, bf16[1024,768]{1,0:T(8,128)(2,1)}, bf16[1024,768]{1,0:T(8,128)(2,1)}, f32[6,768]{1,0:T(8,128)}, /*index=5*/f32[1,3072]{1,0:T(1,128)}) custom-call(s32[3]{0:T(128)S(1)} %pad_add_fusion.sel_ref.refs_0_, bf16[512,768]{1,0:T(8,128)(2,1)} %copy-done.43, ...), custom_call_target="tpu_custom_call" | custom-call | flops 24000000000 | bytes 1024 | tf_op jit(solution)/shard_map/refine_back/pallas_call | solution.py:393
  414.8 15.1 %refine_back.8 = (bf16[1024,768]{1,0:T(8,128)(2,1)}, bf16[1024,3072]{1,0:T(8,128)(2,1)}, bf16[1024,768]{1,0:T(8,128)(2,1)}, bf16[1024,768]{1,0:T(8,128)(2,1)}, f32[6,768]{1,0:T(8,128)}, /*index=5*/f32[1,3072]{1,0:T(1,128)}) custom-call(s32[3]{0:T(128)S(1)} %pad_add_fusion.sel_ref.refs_0_, ...), custom_call_target="tpu_custom_call", output_to_operand_aliasing={{0}: (14, {}), {1}: (15, {}), {2}: (16, {}), {3}: (17, {})} | custom-call | flops 24000000000 | bytes 1024 | tf_op jit(solution)/shard_map/refine_back/pallas_call | solution.py:393
  429.9 13.5 %feed_grads.5 = bf16[8,768,384]{2,1,0:T(8,128)(2,1)} custom-call(s32[3]{0:T(128)} %pad_add_fusion.2.sel_ref, bf16[1024,768]{1,0:T(8,128)(2,1)} %get-tuple-element.409.hidden_ref.refs_2_, bf16[1024,3072]{1,0:T(8,128)(2,1)} %get-tuple-element.423.raised_late_ref, bf16[1024,3072]{1,0:T(8,128)(2,1)} %get-tuple-element.424.raised_ref, ...), custom_call_target="tpu_custom_call" | custom-call | flops 12000000000 | bytes 1024 | tf_op jit(solution)/shard_map/feed_grads/pallas_call | solution.py:505
  451.3 13.1 %feed_grads.4 = bf16[8,768,384]{2,1,0:T(8,128)(2,1)} custom-call(s32[3]{0:T(128)S(1)} %copy-done.55, bf16[1024,768]{1,0:T(8,128)(2,1)S(1)} %copy-done.45, bf16[1024,3072]{1,0:T(8,128)(2,1)} %get-tuple-element.423.raised_late_ref, bf16[1024,3072]{1,0:T(8,128)(2,1)} %get-tuple-element.424.raised_ref, bf16[1024,3072]{1,0:T(8,128)(2,1)} %get-tuple-element.425.active_ref, ...), custom_call_target="tpu_custom_call" | custom-call | flops 12000000000 | bytes 1024 | tf_op jit(solution)/shard_map/feed_grads/pallas_call | solution.py:505
  469.2 32.8 %mixed_backward.6 = (bf16[3,1024,768]{2,1,0:T(8,128)(2,1)}, bf16[1024,768]{1,0:T(8,128)(2,1)}, f32[2,768]{1,0:T(2,128)}) custom-call(s32[8]{0:T(128)S(1)} %copy-done.36, s32[8]{0:T(128)S(1)} %copy-done.38, s32[3]{0:T(128)S(1)} %copy-done.56, bf16[3,1024,768]{2,1,0:T(8,128)(2,1)} %get-tuple-element.420.qkv_hbm, f32[1024,128]{1,0:T(8,128)S(1)} %copy-done.20, ...), custom_call_target="tpu_custom_call" | custom-call | flops 38000001024 | bytes 1024 | tf_op jit(solution)/shard_map/mixed_backward/pallas_call | solution.py:1027
  512.6 9.3 %attend_grads.4 = bf16[8,384,384]{2,1,0:T(8,128)(2,1)} custom-call(s32[3]{0:T(128)} %pad_add_fusion.2.sel_ref, bf16[1024,768]{1,0:T(8,128)(2,1)} %get-tuple-element.453.context_hbm.context_ref, bf16[1024,768]{1,0:T(8,128)(2,1)} %copy-done.12, bf16[1024,768]{1,0:T(8,128)(2,1)} %get-tuple-element.455.attn_late_ref, ...), custom_call_target="tpu_custom_call" | custom-call | flops 8000000000 | bytes 1024 | tf_op jit(solution)/shard_map/attend_grads/pallas_call | solution.py:592
  531.0 12.4 %collective-permute-start.21 = (bf16[768,384]{1,0:T(8,128)(2,1)}, bf16[768,384]{1,0:T(8,128)(2,1)}, u32[]{:S(2)}, u32[]{:S(2)}) collective-permute-start(bf16[768,384]{1,0:T(8,128)(2,1)} %fusion.17), channel_id=1, source_target_pairs={{0,2},{1,3},{2,4},{3,5},{4,6},{5,7},{6,0},{7,1},{8,10},{9,11},{10,... | collective-permute-start | bytes 1769480 | tf_op jit(solution)/shard_map/ppermute | solution.py:1134
  543.4 8.8 %attend_grads.5 = bf16[8,384,384]{2,1,0:T(8,128)(2,1)} custom-call(s32[3]{0:T(128)S(1)} %copy-done.57, bf16[1024,768]{1,0:T(8,128)(2,1)} %get-tuple-element.453.context_hbm.context_ref, bf16[1024,768]{1,0:T(8,128)(2,1)} %copy-done.12, bf16[1024,768]{1,0:T(8,128)(2,1)} %get-tuple-element.455.attn_late_ref, ...), custom_call_target="tpu_custom_call" | custom-call | flops 8000000000 | bytes 1024 | tf_op jit(solution)/shard_map/attend_grads/pallas_call | solution.py:592
  552.2 7.6 collective-permute-done.21
  566.6 12.8 %collective-permute-start.23 = (bf16[768,384]{1,0:T(8,128)(2,1)}, bf16[768,384]{1,0:T(8,128)(2,1)}, u32[]{:S(2)}, u32[]{:S(2)}) collective-permute-start(bf16[768,384]{1,0:T(8,128)(2,1)} %fusion.16), channel_id=1, source_target_pairs={{0,2},{1,3},{2,4},{3,5},{4,6},{5,7},{6,0},{7,1},{8,10},{9,11},{10,... | collective-permute-start | bytes 1769480 | tf_op jit(solution)/shard_map/ppermute | solution.py:1134
  579.3 23.8 %refine_back.9 = (bf16[1024,768]{1,0:T(8,128)(2,1)}, bf16[1024,3072]{1,0:T(8,128)(2,1)}, bf16[1024,768]{1,0:T(8,128)(2,1)}, bf16[1024,768]{1,0:T(8,128)(2,1)}, f32[6,768]{1,0:T(8,128)}, /*index=5*/f32[1,3072]{1,0:T(1,128)}) custom-call(s32[3]{0:T(128)S(1)} %copy-done.57, bf16[1024,768]{1,0:T(8,128)(2,1)} %get-tuple-element.460.grad_ref, ...), custom_call_target="tpu_custom_call" | custom-call | flops 24000000000 | bytes 1024 | tf_op jit(solution)/shard_map/refine_back/pallas_call | solution.py:393
  608.3 13.2 %feed_grads.6 = bf16[8,768,384]{2,1,0:T(8,128)(2,1)} custom-call(s32[3]{0:T(128)} %pad_add_fusion.2.sel_ref, bf16[1024,768]{1,0:T(8,128)(2,1)S(1)} %copy-done.44, bf16[1024,3072]{1,0:T(8,128)(2,1)} %get-tuple-element.495.raised_late_ref, bf16[1024,3072]{1,0:T(8,128)(2,1)} %get-tuple-element.496.raised_ref, bf16[1024,3072]{1,0:T(8,128)(2,1)} %get-tuple-element.497.active_ref, ...), custom_call_target="tpu_custom_call" | custom-call | flops 12000000000 | bytes 1024 | tf_op jit(solution)/shard_map/feed_grads/pallas_call | solution.py:505
  627.6 12.9 %feed_grads.7 = bf16[8,768,384]{2,1,0:T(8,128)(2,1)} custom-call(s32[3]{0:T(128)S(1)} %copy-done.57, bf16[1024,768]{1,0:T(8,128)(2,1)S(1)} %copy-done.44, bf16[1024,3072]{1,0:T(8,128)(2,1)} %get-tuple-element.495.raised_late_ref, bf16[1024,3072]{1,0:T(8,128)(2,1)} %get-tuple-element.496.raised_ref, bf16[1024,3072]{1,0:T(8,128)(2,1)} %get-tuple-element.497.active_ref, ...), custom_call_target="tpu_custom_call" | custom-call | flops 12000000000 | bytes 1024 | tf_op jit(solution)/shard_map/feed_grads/pallas_call | solution.py:505
  648.0 32.1 %mixed_backward.7 = (bf16[3,1024,768]{2,1,0:T(8,128)(2,1)}, bf16[1024,768]{1,0:T(8,128)(2,1)}, f32[2,768]{1,0:T(2,128)}) custom-call(s32[8]{0:T(128)S(1)} %copy-done.36, s32[8]{0:T(128)S(1)} %copy-done.39, s32[3]{0:T(128)S(1)} %copy-done.57, bf16[3,1024,768]{2,1,0:T(8,128)(2,1)} %get-tuple-element.468.qkv_hbm, f32[1024,128]{1,0:T(8,128)S(1)} %copy-done.21, ...), custom_call_target="tpu_custom_call" | custom-call | flops 38000001024 | bytes 1024 | tf_op jit(solution)/shard_map/mixed_backward/pallas_call | solution.py:1027
  682.3 16.7 %collective-permute-done.28 = bf16[4,768,384]{2,1,0:T(8,128)(2,1)} collective-permute-done((bf16[4,768,384]{2,1,0:T(8,128)(2,1)S(1)}, bf16[4,768,384]{2,1,0:T(8,128)(2,1)}, u32[]{:S(2)}, u32[]{:S(2)}) %collective-permute-start.28) | collective-permute-done | bytes 2359328 | tf_op jit(solution)/shard_map/ppermute | solution.py:1116
  702.5 9.1 %attend_grads.6 = bf16[8,432,384]{2,1,0:T(8,128)(2,1)} custom-call(s32[3]{0:T(128)} %pad_add_fusion.2.sel_ref, bf16[1024,768]{1,0:T(8,128)(2,1)} %get-tuple-element.536.context_hbm.context_ref, bf16[1024,768]{1,0:T(8,128)(2,1)S(1)} %copy-done.9, bf16[1024,768]{1,0:T(8,128)(2,1)} %get-tuple-element.538.attn_late_ref, ...), custom_call_target="tpu_custom_call" | custom-call | flops 8000000000 | bytes 1024 | tf_op jit(solution)/shard_map/attend_grads/pallas_call | solution.py:592
  722.8 9.6 %attend_grads.7 = bf16[8,432,384]{2,1,0:T(8,128)(2,1)} custom-call(s32[3]{0:T(128)S(1)} %copy-done.57, bf16[1024,768]{1,0:T(8,128)(2,1)} %get-tuple-element.536.context_hbm.context_ref, bf16[1024,768]{1,0:T(8,128)(2,1)} %get-tuple-element.537.x_ref, bf16[1024,768]{1,0:T(8,128)(2,1)} %get-tuple-element.538.attn_late_ref, ...), custom_call_target="tpu_custom_call" | custom-call | flops 8000000000 | bytes 1024 | tf_op jit(solution)/shard_map/attend_grads/pallas_call | solution.py:592
  753.3 12.4 %collective-permute-done.38 = bf16[384,384]{1,0:T(8,128)(2,1)S(1)} collective-permute-done((bf16[384,384]{1,0:T(8,128)(2,1)S(1)}, bf16[384,384]{1,0:T(8,128)(2,1)S(1)}, u32[]{:S(2)}, u32[]{:S(2)}) %collective-permute-start.38) | collective-permute-done | bytes 294944 | tf_op jit(solution)/shard_map/ppermute | solution.py:1134
  770.3 10.4 %collective-permute-start.42 = (bf16[432,384]{1,0:T(8,128)(2,1)S(1)}, bf16[432,384]{1,0:T(8,128)(2,1)S(1)}, u32[]{:S(2)}, u32[]{:S(2)}) collective-permute-start(bf16[432,384]{1,0:T(8,128)(2,1)S(1)} %get-tuple-element.622), channel_id=1, source_target_pairs={{0,4},{1,5},{2,6},{3,7},{8,12},{9,13},{10,14},{11,15},{16,20},{17,... | collective-permute-start | bytes 995336 | tf_op jit(solution)/shard_map/ppermute | solution.py:1144
  (320 shorter events, 194.4 us)
Async XLA Ops:
  9.7 21.6 %collective-permute-start.5 = (bf16[768,3072]{1,0:T(8,128)(2,1)}, bf16[768,3072]{1,0:T(8,128)(2,1)}, u32[]{:S(2)}, u32[]{:S(2)}) collective-permute-start(bf16[768,3072]{1,0:T(8,128)(2,1)} %bitcast.321), channel_id=1, source_target_pairs={{0,8},{8,0},{16,24},{24,16},{1,9},{9,1},{17,25},{25,17},{2,10},{10... | collective-permute-start | bytes 14155784 | tf_op jit(solution)/shard_map/ppermute | solution.py:1075
  9.7 21.7 %collective-permute-start.6 = (bf16[3072,768]{1,0:T(8,128)(2,1)}, bf16[3072,768]{1,0:T(8,128)(2,1)}, u32[]{:S(2)}, u32[]{:S(2)}) collective-permute-start(bf16[3072,768]{1,0:T(8,128)(2,1)} %bitcast.329), channel_id=1, source_target_pairs={{0,8},{8,0},{16,24},{24,16},{1,9},{9,1},{17,25},{25,17},{2,10},{10... | collective-permute-start | bytes 14155784 | tf_op jit(solution)/shard_map/ppermute | solution.py:1075
  82.6 38.6 %collective-permute-start.8 = (bf16[32,1792]{1,0:T(8,128)(2,1)S(1)}, bf16[32,1792]{1,0:T(8,128)(2,1)S(1)}, u32[]{:S(2)}, u32[]{:S(2)}) collective-permute-start(bf16[32,1792]{1,0:T(8,128)(2,1)S(1)} %get-tuple-element.398), channel_id=1, source_target_pairs={{0,24},{8,16},{1,25},{9,17},{2,26},{10,18},{3,27},{11,19},{4,28},{... | collective-permute-start | bytes 344072 | tf_op jit(solution)/shard_map/ppermute | solution.py:1075
  83.9 37.3 %collective-permute-start.10 = (bf16[32,1792]{1,0:T(8,128)(2,1)S(1)}, bf16[32,1792]{1,0:T(8,128)(2,1)S(1)}, u32[]{:S(2)}, u32[]{:S(2)}) collective-permute-start(bf16[32,1792]{1,0:T(8,128)(2,1)S(1)} %get-tuple-element.398), channel_id=1, source_target_pairs={{16,24},{24,16},{17,25},{25,17},{18,26},{26,18},{19,27},{27,19},{2... | collective-permute-start | bytes 344072 | tf_op jit(solution)/shard_map/ppermute | solution.py:1075
  85.8 35.4 %collective-permute-start.9 = (bf16[32,1792]{1,0:T(8,128)(2,1)S(1)}, bf16[32,1792]{1,0:T(8,128)(2,1)S(1)}, u32[]{:S(2)}, u32[]{:S(2)}) collective-permute-start(bf16[32,1792]{1,0:T(8,128)(2,1)S(1)} %get-tuple-element.399), channel_id=1, source_target_pairs={{0,16},{8,24},{1,17},{9,25},{2,18},{10,26},{3,19},{11,27},{4,20},{... | collective-permute-start | bytes 344072 | tf_op jit(solution)/shard_map/ppermute | solution.py:1075
  122.3 21.1 %collective-permute-start.11 = (bf16[512,768]{1,0:T(8,128)(2,1)S(1)}, bf16[512,768]{1,0:T(8,128)(2,1)S(1)}, u32[]{:S(2)}, u32[]{:S(2)}) collective-permute-start(bf16[512,768]{1,0:T(8,128)(2,1)S(1)} %copy-done.15), channel_id=1, source_target_pairs={{0,16},{8,24},{1,17},{9,25},{2,18},{10,26},{3,19},{11,27},{4,20},{... | collective-permute-start | bytes 2359304 | tf_op jit(solution)/shard_map/ppermute | solution.py:1075
  143.5 20.5 %collective-permute-start.12 = (bf16[512,768]{1,0:T(8,128)(2,1)}, bf16[512,768]{1,0:T(8,128)(2,1)}, u32[]{:S(2)}, u32[]{:S(2)}) collective-permute-start(bf16[512,768]{1,0:T(8,128)(2,1)} %get-tuple-element.402), channel_id=1, source_target_pairs={{0,16},{8,24},{1,17},{9,25},{2,18},{10,26},{3,19},{11,27},{4,20},{... | collective-permute-start | bytes 2359304 | tf_op jit(solution)/shard_map/ppermute | solution.py:1075
  381.9 32.9 %collective-permute-start.13 = (bf16[512,768]{1,0:T(8,128)(2,1)}, bf16[512,768]{1,0:T(8,128)(2,1)}, u32[]{:S(2)}, u32[]{:S(2)}) collective-permute-start(bf16[512,768]{1,0:T(8,128)(2,1)} %get-tuple-element.631), channel_id=1, source_target_pairs={{16,0},{24,8},{17,1},{25,9},{18,2},{26,10},{19,3},{27,11},{20,4},{... | collective-permute-start | bytes 2359304 | tf_op jit(solution)/shard_map/ppermute | solution.py:1075
  443.4 21.0 %collective-permute-start.15 = (bf16[8,768,384]{2,1,0:T(8,128)(2,1)}, bf16[8,768,384]{2,1,0:T(8,128)(2,1)}, u32[]{:S(2)}, u32[]{:S(2)}) collective-permute-start(bf16[8,768,384]{2,1,0:T(8,128)(2,1)} %feed_grads.5), channel_id=1, source_target_pairs={{0,8},{8,0},{16,24},{24,16},{1,9},{9,1},{17,25},{25,17},{2,10},{10... | collective-permute-start | bytes 14155784 | tf_op jit(solution)/shard_map/ppermute | solution.py:1075
  445.0 57.1 %collective-permute-start.16 = (bf16[32,1024]{1,0:T(8,128)(2,1)}, bf16[32,1024]{1,0:T(8,128)(2,1)S(1)}, u32[]{:S(2)}, u32[]{:S(2)}) collective-permute-start(bf16[32,1024]{1,0:T(8,128)(2,1)} %get-tuple-element.644), channel_id=1, source_target_pairs={{16,0},{24,8},{17,1},{25,9},{18,2},{26,10},{19,3},{27,11},{20,4},{... | collective-permute-start | bytes 196616 | tf_op jit(solution)/shard_map/ppermute | solution.py:1075
  449.2 53.0 %collective-permute-start.17 = (bf16[32,1024]{1,0:T(8,128)(2,1)}, bf16[32,1024]{1,0:T(8,128)(2,1)S(1)}, u32[]{:S(2)}, u32[]{:S(2)}) collective-permute-start(bf16[32,1024]{1,0:T(8,128)(2,1)} %get-tuple-element.643), channel_id=1, source_target_pairs={{16,8},{24,0},{17,9},{25,1},{18,10},{26,2},{19,11},{27,3},{20,12},... | collective-permute-start | bytes 196616 | tf_op jit(solution)/shard_map/ppermute | solution.py:1075
  450.8 51.3 %collective-permute-start.18 = (bf16[32,1024]{1,0:T(8,128)(2,1)}, bf16[32,1024]{1,0:T(8,128)(2,1)}, u32[]{:S(2)}, u32[]{:S(2)}) collective-permute-start(bf16[32,1024]{1,0:T(8,128)(2,1)} %get-tuple-element.642), channel_id=1, source_target_pairs={{0,8},{8,0},{16,24},{24,16},{1,9},{9,1},{17,25},{25,17},{2,10},{10... | collective-permute-start | bytes 196616 | tf_op jit(solution)/shard_map/ppermute | solution.py:1075
  468.3 40.5 %collective-permute-start.19 = (bf16[4,576,384]{2,1,0:T(8,128)(2,1)}, bf16[4,576,384]{2,1,0:T(8,128)(2,1)S(1)}, u32[]{:S(2)}, u32[]{:S(2)}) collective-permute-start(bf16[4,576,384]{2,1,0:T(8,128)(2,1)} %fusion.1), channel_id=1, source_target_pairs={{0,1},{1,0},{2,3},{3,2},{4,5},{5,4},{6,7},{7,6},{8,9},{9,8},{10,11... | collective-permute-start | bytes 5308424 | tf_op jit(solution)/shard_map/ppermute | solution.py:1116
  526.1 33.8 %collective-permute-start.22 = (bf16[8,384,384]{2,1,0:T(8,128)(2,1)}, bf16[8,384,384]{2,1,0:T(8,128)(2,1)}, u32[]{:S(2)}, u32[]{:S(2)}) collective-permute-start(bf16[8,384,384]{2,1,0:T(8,128)(2,1)} %attend_grads.4), channel_id=1, source_target_pairs={{0,8},{8,0},{16,24},{24,16},{1,9},{9,1},{17,25},{25,17},{2,10},{10... | collective-permute-start | bytes 7077896 | tf_op jit(solution)/shard_map/ppermute | solution.py:1075
  531.0 28.9 %collective-permute-start.21 = (bf16[768,384]{1,0:T(8,128)(2,1)}, bf16[768,384]{1,0:T(8,128)(2,1)}, u32[]{:S(2)}, u32[]{:S(2)}) collective-permute-start(bf16[768,384]{1,0:T(8,128)(2,1)} %fusion.17), channel_id=1, source_target_pairs={{0,2},{1,3},{2,4},{3,5},{4,6},{5,7},{6,0},{7,1},{8,10},{9,11},{10,... | collective-permute-start | bytes 1769480 | tf_op jit(solution)/shard_map/ppermute | solution.py:1134
  562.8 40.4 %collective-permute-start.24 = (bf16[4,384,384]{2,1,0:T(8,128)(2,1)}, bf16[4,384,384]{2,1,0:T(8,128)(2,1)}, u32[]{:S(2)}, u32[]{:S(2)}) collective-permute-start(bf16[4,384,384]{2,1,0:T(8,128)(2,1)} %fusion.3), channel_id=1, source_target_pairs={{0,1},{1,0},{2,3},{3,2},{4,5},{5,4},{6,7},{7,6},{8,9},{9,8},{10,11... | collective-permute-start | bytes 3538952 | tf_op jit(solution)/shard_map/ppermute | solution.py:1116
  566.6 36.6 %collective-permute-start.23 = (bf16[768,384]{1,0:T(8,128)(2,1)}, bf16[768,384]{1,0:T(8,128)(2,1)}, u32[]{:S(2)}, u32[]{:S(2)}) collective-permute-start(bf16[768,384]{1,0:T(8,128)(2,1)} %fusion.16), channel_id=1, source_target_pairs={{0,2},{1,3},{2,4},{3,5},{4,6},{5,7},{6,0},{7,1},{8,10},{9,11},{10,... | collective-permute-start | bytes 1769480 | tf_op jit(solution)/shard_map/ppermute | solution.py:1134
  621.5 19.0 %collective-permute-start.26 = (bf16[8,768,384]{2,1,0:T(8,128)(2,1)}, bf16[8,768,384]{2,1,0:T(8,128)(2,1)}, u32[]{:S(2)}, u32[]{:S(2)}) collective-permute-start(bf16[8,768,384]{2,1,0:T(8,128)(2,1)} %feed_grads.6), channel_id=1, source_target_pairs={{0,8},{8,0},{16,24},{24,16},{1,9},{9,1},{17,25},{25,17},{2,10},{10... | collective-permute-start | bytes 14155784 | tf_op jit(solution)/shard_map/ppermute | solution.py:1075
  642.6 39.6 %collective-permute-start.29 = (bf16[384,384]{1,0:T(8,128)(2,1)}, bf16[384,384]{1,0:T(8,128)(2,1)}, u32[]{:S(2)}, u32[]{:S(2)}) collective-permute-start(bf16[384,384]{1,0:T(8,128)(2,1)} %fusion.37), channel_id=1, source_target_pairs={{0,2},{1,3},{2,4},{3,5},{4,6},{5,7},{6,0},{7,1},{8,10},{9,11},{10,... | collective-permute-start | bytes 884744 | tf_op jit(solution)/shard_map/ppermute | solution.py:1134
  646.7 52.3 %collective-permute-start.28 = (bf16[4,768,384]{2,1,0:T(8,128)(2,1)S(1)}, bf16[4,768,384]{2,1,0:T(8,128)(2,1)}, u32[]{:S(2)}, u32[]{:S(2)}) collective-permute-start(bf16[4,768,384]{2,1,0:T(8,128)(2,1)S(1)} %fusion), channel_id=1, source_target_pairs={{0,1},{1,0},{2,3},{3,2},{4,5},{5,4},{6,7},{7,6},{8,9},{9,8},{10,11... | collective-permute-start | bytes 7077896 | tf_op jit(solution)/shard_map/ppermute | solution.py:1116
  714.1 22.6 %collective-permute-start.36 = (bf16[8,432,384]{2,1,0:T(8,128)(2,1)}, bf16[8,432,384]{2,1,0:T(8,128)(2,1)S(1)}, u32[]{:S(2)}, u32[]{:S(2)}) collective-permute-start(bf16[8,432,384]{2,1,0:T(8,128)(2,1)} %attend_grads.6), channel_id=1, source_target_pairs={{0,8},{8,0},{16,24},{24,16},{1,9},{9,1},{17,25},{25,17},{2,10},{10... | collective-permute-start | bytes 7962632 | tf_op jit(solution)/shard_map/ppermute | solution.py:1075
  738.4 29.6 %collective-permute-start.37 = (bf16[4,432,384]{2,1,0:T(8,128)(2,1)S(1)}, bf16[4,432,384]{2,1,0:T(8,128)(2,1)S(1)}, u32[]{:S(2)}, u32[]{:S(2)}) collective-permute-start(bf16[4,432,384]{2,1,0:T(8,128)(2,1)S(1)} %fusion.2), channel_id=1, source_target_pairs={{0,1},{1,0},{2,3},{3,2},{4,5},{5,4},{6,7},{7,6},{8,9},{9,8},{10,11... | collective-permute-start | bytes 3981320 | tf_op jit(solution)/shard_map/ppermute | solution.py:1116
  744.3 22.3 %collective-permute-start.35 = (bf16[768,384]{1,0:T(8,128)(2,1)S(1)}, bf16[768,384]{1,0:T(8,128)(2,1)S(1)}, u32[]{:S(2)}, u32[]{:S(2)}) collective-permute-start(bf16[768,384]{1,0:T(8,128)(2,1)S(1)} %fusion.7), channel_id=1, source_target_pairs={{0,2},{1,3},{2,4},{3,5},{4,6},{5,7},{6,0},{7,1},{8,10},{9,11},{10,... | collective-permute-start | bytes 1769480 | tf_op jit(solution)/shard_map/ppermute | solution.py:1134
  745.1 20.5 %collective-permute-start.33 = (bf16[256,768]{1,0:T(8,128)(2,1)S(1)}, bf16[256,768]{1,0:T(8,128)(2,1)S(1)}, u32[]{:S(2)}, u32[]{:S(2)}) collective-permute-start(bf16[256,768]{1,0:T(8,128)(2,1)S(1)} %get-tuple-element.629), channel_id=1, source_target_pairs={{0,16},{8,24},{1,17},{9,25},{2,18},{10,26},{3,19},{11,27},{4,20},{... | collective-permute-start | bytes 1179656 | tf_op jit(solution)/shard_map/ppermute | solution.py:1075
  746.4 20.2 %collective-permute-start.34 = (bf16[256,768]{1,0:T(8,128)(2,1)S(1)}, bf16[256,768]{1,0:T(8,128)(2,1)S(1)}, u32[]{:S(2)}, u32[]{:S(2)}) collective-permute-start(bf16[256,768]{1,0:T(8,128)(2,1)S(1)} %get-tuple-element.628), channel_id=1, source_target_pairs={{0,24},{8,16},{1,25},{9,17},{2,26},{10,18},{3,27},{11,19},{4,28},{... | collective-permute-start | bytes 1179656 | tf_op jit(solution)/shard_map/ppermute | solution.py:1075
  769.6 23.0 %collective-permute-start.41 = (bf16[432,384]{1,0:T(8,128)(2,1)S(1)}, bf16[432,384]{1,0:T(8,128)(2,1)S(1)}, u32[]{:S(2)}, u32[]{:S(2)}) collective-permute-start(bf16[432,384]{1,0:T(8,128)(2,1)S(1)} %get-tuple-element.623), channel_id=1, source_target_pairs={{6,0},{7,1},{14,8},{15,9},{22,16},{23,17},{30,24},{31,25}} | collective-permute-start | bytes 995336 | tf_op jit(solution)/shard_map/ppermute | solution.py:1144
  770.3 25.9 %collective-permute-start.42 = (bf16[432,384]{1,0:T(8,128)(2,1)S(1)}, bf16[432,384]{1,0:T(8,128)(2,1)S(1)}, u32[]{:S(2)}, u32[]{:S(2)}) collective-permute-start(bf16[432,384]{1,0:T(8,128)(2,1)S(1)} %get-tuple-element.622), channel_id=1, source_target_pairs={{0,4},{1,5},{2,6},{3,7},{8,12},{9,13},{10,14},{11,15},{16,20},{17,... | collective-permute-start | bytes 995336 | tf_op jit(solution)/shard_map/ppermute | solution.py:1144
  782.0 21.3 %collective-permute-start.44 = (bf16[432,384]{1,0:T(8,128)(2,1)S(1)}, bf16[432,384]{1,0:T(8,128)(2,1)S(1)}, u32[]{:S(2)}, u32[]{:S(2)}) collective-permute-start(bf16[432,384]{1,0:T(8,128)(2,1)S(1)} %get-tuple-element.620), channel_id=1, source_target_pairs={{0,2},{1,3},{2,4},{3,5},{4,6},{5,7},{8,10},{9,11},{10,12},{11,13},... | collective-permute-start | bytes 995336 | tf_op jit(solution)/shard_map/ppermute | solution.py:1144
  785.3 23.0 %collective-permute-start.45 = (bf16[432,384]{1,0:T(8,128)(2,1)S(1)}, bf16[432,384]{1,0:T(8,128)(2,1)S(1)}, u32[]{:S(2)}, u32[]{:S(2)}) collective-permute-start(bf16[432,384]{1,0:T(8,128)(2,1)S(1)} %get-tuple-element.619), channel_id=1, source_target_pairs={{2,0},{3,1},{4,2},{5,3},{6,4},{7,5},{10,8},{11,9},{12,10},{13,11},... | collective-permute-start | bytes 995336 | tf_op jit(solution)/shard_map/ppermute | solution.py:1144
  792.6 23.0 %collective-permute-start.47 = (bf16[768,384]{1,0:T(8,128)(2,1)}, bf16[768,384]{1,0:T(8,128)(2,1)}, u32[]{:S(2)}, u32[]{:S(2)}) collective-permute-start(bf16[768,384]{1,0:T(8,128)(2,1)} %fusion.12), channel_id=1, source_target_pairs={{0,8},{16,24},{1,9},{17,25},{2,10},{18,26},{3,11},{19,27},{4,12},{... | collective-permute-start | bytes 1769480 | tf_op jit(solution)/shard_map/ppermute | solution.py:1075
  796.2 19.4 %collective-permute-start.48 = (bf16[768,384]{1,0:T(8,128)(2,1)}, bf16[768,384]{1,0:T(8,128)(2,1)}, u32[]{:S(2)}, u32[]{:S(2)}) collective-permute-start(bf16[768,384]{1,0:T(8,128)(2,1)} %fusion.5), channel_id=1, source_target_pairs={{8,0},{24,16},{9,1},{25,17},{10,2},{26,18},{11,3},{27,19},{12,4},{... | collective-permute-start | bytes 1769480 | tf_op jit(solution)/shard_map/ppermute | solution.py:1075
  799.5 19.9 %collective-permute-start.39 = (bf16[384,384]{1,0:T(8,128)(2,1)S(1)}, bf16[384,384]{1,0:T(8,128)(2,1)}, u32[]{:S(2)}, u32[]{:S(2)}) collective-permute-start(bf16[384,384]{1,0:T(8,128)(2,1)S(1)} %fusion.33), channel_id=1, source_target_pairs={{0,8},{16,24},{1,9},{17,25},{2,10},{18,26},{3,11},{19,27},{4,12},{... | collective-permute-start | bytes 884744 | tf_op jit(solution)/shard_map/ppermute | solution.py:1075
  (76 other events, 2195.1 us)
